TPU v7x, 128 devices: a whole 4x4x4 slice. The times are simulated.
128 devices in a mesh: tmpl: 4 (over z_hi, core), row: 32 (over y, z_lo, x).
Axes of the slice: x: 4, y: 4, z: 4 (z_hi: 2, z_lo: 2; z = z_hi * 2 + z_lo), core: 2. Of those that a mesh axis runs over, the one named last changes fastest.
Arguments:
- template_pair: bfloat16 [4, 256, 256, 64], P('tmpl', 'row'), may hold values from -6 to 6
- template_mask: int32 [4, 256], replicated, may hold values 0 or 1
- residue_index: int32 [256], replicated, may hold values from 0 to 509, as said below
- query_pair: bfloat16 [256, 256, 128], P('row'), may hold values from -6 to 6
- relpos_table: bfloat16 [128, 64], replicated, may hold values from -3 to 3
- norm_gain: float32 [64], replicated, may hold values from 0.5 to 1.5
- left_weight: bfloat16 [64, 64], replicated, may hold values from -0.75 to 0.75
- right_weight: bfloat16 [64, 64], replicated, may hold values from -0.75 to 0.75
- gate_weight: bfloat16 [64, 64], replicated, may hold values from -0.75 to 0.75
- out_weight: bfloat16 [64, 64], replicated, may hold values from -0.75 to 0.75
- tri_gain: float32 [64], replicated, may hold values from 0.5 to 1.5
- pair_gain: float32 [64], replicated, may hold values from 0.5 to 1.5
- kv_weight: bfloat16 [64, 128], replicated, may hold values from -0.75 to 0.75
- query_gain: float32 [128], replicated, may hold values from 0.5 to 1.5
- query_weight: bfloat16 [128, 64], replicated, may hold values from -0.5 to 0.5
- attn_out_weight: bfloat16 [64, 128], replicated, may hold values from -0.75 to 0.75
- cotangent: bfloat16 [256, 256, 128], P('row'), may hold values from -6 to 6
Outputs:
- template_grad: float32 [4, 256, 256, 64], P('tmpl', 'row')
- query_grad: float32 [256, 256, 128], P('row')
- projection_grad: float32 [2, 64, 64], replicated
Inputs may be any that keep to these rules, and one draw needn't show every extreme that they name: `residue_index`: strictly increasing, starting at 0, steps of 1 or 3, exactly (255) // 2 of them 3.
All inputs are finite; a program needn't handle non-finite values.
Results may differ from a plain program's by a relative error of at most 0.013.
Values may be sent and summed in bfloat16 or wider, within the bound.
No kernel may reach another device: no remote copies, remote signals or barrier semaphores. Data moves between devices by JAX's collectives and lax.ppermute only.
A program may use at most 128 MiB of HBM per device.

v0:
```python
import jax
import jax.numpy as jnp
from jax import lax
from jax.sharding import PartitionSpec as P

HEADS = 4
HEAD_DIM = 16


def merged(value, axis, join):
    pieces = jax.tree.map(lambda part: lax.all_gather(part, axis), value)
    head = jax.tree.map(lambda part: part[0], pieces)
    tail = jax.tree.map(lambda part: part[1:], pieces)
    so_far, _ = lax.scan(lambda so_far, share: (join(so_far, share), None), head, tail)
    return so_far


def layer_norm(x, gain):
    mean = jnp.mean(x, -1, keepdims=True)
    cent = x - mean
    var = jnp.mean(cent * cent, -1, keepdims=True)
    return cent * lax.rsqrt(var + 1e-05) * gain


def high_dot(a, b):
    return jnp.einsum("...c,cd->...d", a, b, precision=lax.Precision.HIGHEST)


def relative(res_rows, res_all, table):
    half = table.shape[0] // 2
    offset = jnp.clip(res_rows[:, None] - res_all[None, :], -half, half - 1) + half
    bins = jnp.arange(table.shape[0], dtype=jnp.int32)
    onehot = (offset[:, :, None] == bins[None, None, :]).astype(jnp.bfloat16)
    return jnp.dot(onehot, table, preferred_element_type=jnp.float32)


def project(ln_b, weight, mask_rows, mask_all):
    raw = jnp.dot(ln_b, weight, preferred_element_type=jnp.float32)
    return (raw * mask_rows[:, None, None] * mask_all[None, :, None]).astype(jnp.bfloat16)


def post_block(ln, z_in, tri, gate_w, out_w, tri_gain, pair_gain, kv_w):
    gate = jax.nn.sigmoid(high_dot(ln, gate_w))
    update = gate * high_dot(layer_norm(tri, tri_gain), out_w)
    return high_dot(layer_norm(z_in + update, pair_gain), kv_w)


def query_heads(query, gain, weight):
    return high_dot(layer_norm(query, gain), weight) * HEAD_DIM ** (-0.5)


def softmax_combine(first, second):
    top = jnp.maximum(first[0], second[0])
    scale_a = jnp.exp(first[0] - top)
    scale_b = jnp.exp(second[0] - top)
    return (
        top,
        first[1] * scale_a + second[1] * scale_b,
        first[2] * scale_a[..., None] + second[2] * scale_b[..., None],
    )


def local(
    template_pair,
    template_mask,
    residue_index,
    query_pair,
    relpos_table,
    norm_gain,
    left_weight,
    right_weight,
    gate_weight,
    out_weight,
    tri_gain,
    pair_gain,
    kv_weight,
    query_gain,
    query_weight,
    attn_out_weight,
    cotangent,
):
    f32 = jnp.float32
    rows = template_pair.shape[1]
    width = template_pair.shape[2]
    heads = HEADS
    hsize = HEAD_DIM
    hdim = heads * hsize
    tmpl_id = lax.axis_index("tmpl")
    row_start = lax.axis_index("row") * rows
    masks_f = template_mask.astype(f32)
    mask_all = lax.dynamic_index_in_dim(masks_f, tmpl_id, 0, keepdims=False)
    mask_rows = lax.dynamic_slice_in_dim(mask_all, row_start, rows, 0)
    res_rows = lax.dynamic_slice_in_dim(residue_index, row_start, rows, 0)
    gate_f, out_f, kv_f = (gate_weight.astype(f32), out_weight.astype(f32), kv_weight.astype(f32))
    z_in = template_pair[0].astype(f32) + relative(res_rows, residue_index, relpos_table)
    ln, ln_back = jax.vjp(lambda x: layer_norm(x, norm_gain), z_in)
    ln_b = ln.astype(jnp.bfloat16)
    left = project(ln_b, left_weight, mask_rows, mask_all)
    right = project(ln_b, right_weight, mask_rows, mask_all)
    right_all = lax.all_gather(right, "row", axis=0, tiled=True)
    tri = jnp.einsum("ikc,jkc->ijc", left, right_all, preferred_element_type=f32)
    kv, post_back = jax.vjp(
        lambda a, b, c: post_block(a, b, c, gate_f, out_f, tri_gain, pair_gain, kv_f), ln, z_in, tri
    )
    kv_b = kv.astype(jnp.bfloat16)
    qh, query_back = jax.vjp(
        lambda x: query_heads(x, query_gain, query_weight.astype(f32)), query_pair.astype(f32)
    )
    qh4 = qh.reshape(rows, width, heads, hsize)
    d_o = jnp.dot(cotangent, attn_out_weight.T, preferred_element_type=f32).reshape(
        rows, width, heads, hsize
    )
    kv_own = kv_b.astype(f32)
    key = kv_own[..., :hdim].reshape(rows, width, heads, hsize)
    value = kv_own[..., hdim:].reshape(rows, width, heads, hsize)
    pair = mask_rows[:, None] * mask_all[None, :]
    bias = (pair - 1.0) * 1000000000.0
    score = jnp.sum(qh4 * key, -1) * pair[:, :, None] + bias[:, :, None]
    top, total, weighted = merged((score, jnp.ones_like(score), value), "tmpl", softmax_combine)
    prob = jnp.exp(score - top) / total
    attended = weighted / total[..., None]
    delta = jnp.sum(d_o * attended, -1)
    d_score = prob * (jnp.sum(d_o * value, -1) - delta) * pair[:, :, None]
    d_qh = lax.psum((d_score[..., None] * key).reshape(rows, width, hdim), "tmpl")
    d_key = (d_score[..., None] * qh4).reshape(rows, width, hdim)
    d_value = (prob[..., None] * d_o).reshape(rows, width, hdim)
    d_kv = jnp.concatenate([d_key, d_value], -1)
    query_grad = query_back(d_qh)[0]
    d_ln_a, d_zin_a, d_tri = post_back(d_kv)
    d_tri_b = d_tri.astype(jnp.bfloat16)
    mask2 = mask_rows[:, None, None] * mask_all[None, :, None]
    d_left = (
        jnp.einsum("ijc,jkc->ikc", d_tri_b, right_all, preferred_element_type=f32) * mask2
    ).astype(jnp.bfloat16)
    right_sum = lax.psum_scatter(
        jnp.einsum("ijc,ikc->jkc", d_tri_b, left, preferred_element_type=f32),
        "row",
        scatter_dimension=0,
        tiled=True,
    )
    d_right = (right_sum * mask2).astype(jnp.bfloat16)
    d_ln_b = jnp.dot(d_left, left_weight.T, preferred_element_type=f32) + jnp.dot(
        d_right, right_weight.T, preferred_element_type=f32
    )
    grad_left = jnp.einsum("ikc,ikd->cd", ln_b, d_left, preferred_element_type=f32)
    grad_right = jnp.einsum("ikc,ikd->cd", ln_b, d_right, preferred_element_type=f32)
    projection_grad = lax.psum(jnp.stack([grad_left, grad_right]), ("tmpl", "row"))
    template_grad = ln_back(d_ln_a + d_ln_b)[0] + d_zin_a
    return (template_grad[None], query_grad, projection_grad)


def solution(mesh):
    in_specs = (
        P("tmpl", "row", None, None),
        P(),
        P(),
        P("row", None, None),
        P(),
        P(),
        P(),
        P(),
        P(),
        P(),
        P(),
        P(),
        P(),
        P(),
        P(),
        P(),
        P("row", None, None),
    )
    out_specs = (P("tmpl", "row", None, None), P("row", None, None), P())
    return jax.shard_map(local, mesh=mesh, in_specs=in_specs, out_specs=out_specs, check_vma=False)
```

profile of v0, /device:TPU:0, one launch (start us, length us, event | category | flops | bytes accessed | tf_op | source)
XLA Modules:
  0.0 560.6 jit_solution(12323553973357452924)
XLA Ops:
  7.2 0.8 dynamic_slice.25
  8.0 0.7 convert_element_type.45
  8.7 0.8 clamp_add_fusion
  9.5 1.5 fusion.104
  11.2 0.8 fusion.54
  12.0 1.7 fusion.31
  13.8 1.0 fusion.30
  14.8 168.5 %all-gather.3.cloned.1.call-done = bf16[256,256,64]{1,2,0:T(8,128)(2,1)} async-done(((bf16[8,256,64]{1,2,0:T(8,128)(2,1)}), bf16[256,256,64]{1,2,0:T(8,128)(2,1)}) %all-gather.3.cloned.1.call-update) | async-done | bytes 8388624 | tf_op jit(solution)/shard_map/all_gather | solution.py:100
  183.3 8.0 %fusion.105 = (f32[8,256]{1,0:T(8,128)S(1)}, f32[8,256,64]{1,0,2:T(8,128)S(1)}) fusion(bf16[8,256,64]{1,2,0:T(8,128)(2,1)S(1)} %fusion.30, bf16[256,256,64]{1,2,0:T(8,128)(2,1)} %all-gather.3.cloned.1.call-done), kind=kOutput, calls=%fused_computation.169 | convolution fusion | flops 67237888 | bytes 9183232 | tf_op jit(solution)/shard_map/ikc,jkc->ijc/dot_general | solution.py:101
  192.2 1.4 fusion.103
  193.7 0.7 fusion.11
  194.4 1.0 copy-done.1
  195.4 0.8 slice.28
  196.9 2.6 bitcast_reduce_fusion
  199.6 6.9 %all_gather.12 = f32[4,8,256,4]{2,1,3,0:T(8,128)S(1)} all-gather(f32[1,8,256,4]{2,1,3,0:T(8,128)S(1)} %copy.73), channel_id=1, replica_groups=mesh['tmpl'=4,'row'=32] {'tmpl'}, dimensions={0}, use_global_device_ids=true | all-gather | bytes 163840 | tf_op jit(solution)/shard_map/all_gather | solution.py:11
  206.6 0.6 slice.30
  207.2 17.2 %all-gather.5.cloned.1.call-done = f32[4,8,256,4,16]{2,4,3,1,0:T(8,128)} async-done(((f32[1,8,256,4,16]{2,4,3,1,0:T(8,128)}), f32[4,8,256,4,16]{2,4,3,1,0:T(8,128)}) %all-gather.5.cloned.1.call-update) | async-done | bytes 2097168 | tf_op jit(solution)/shard_map/all_gather | solution.py:11
  224.4 1.1 slice_bitcast_fusion
  225.5 2.8 slice.31
  228.3 6.4 %while.16 = (s32[]{:T(128)}, f32[8,256,4]{1,2,0:T(4,128)S(1)}, f32[8,256,4]{1,2,0:T(4,128)S(1)}, f32[8,256,4,16]{1,3,2,0:T(8,128)S(1)}, f32[3,8,256,4]{2,1,3,0:T...) while((s32[]{:T(128)}, f32[8,256,4]{1,2,0:T(4,128)S(1)}, ...), condition=%wide.region_10.11_spmd.clone, body=%wide.region_9.10_spmd.clone.sunk | while | flops 442371 | bytes 1933423 | solution.py:14
  228.3 0.8 constant_dynamic-slice_fusion.3
  229.1 1.3 fusion.114
  230.4 0.8 constant_dynamic-slice_fusion.3
  231.3 1.3 fusion.114
  232.6 0.8 constant_dynamic-slice_fusion.3
  233.4 1.3 fusion.114
  234.7 1.5 multiply_reduce_fusion.3
  236.2 0.7 multiply_multiply_fusion.3
  236.9 2.4 bitcast_multiply_fusion.1
  239.6 1.6 multiply_reduce_fusion.2
  241.2 0.7 multiply_multiply_fusion.7
  241.9 0.8 fusion.102
  242.8 1.5 fusion.44
  245.0 0.8 copy-done.2
  245.8 9.0 %convolution_bitcast_fusion = f32[256,256,64]{1,0,2:T(8,128)} fusion(bf16[8,256,64]{1,2,0:T(8,128)(2,1)} %copy-done.6, f32[8,256,64]{1,0,2:T(8,128)S(1)} %get-tuple-element.124, f32[8,256]{1,0:T(8,128)S(1)} %negate_multiply_fusion.2), kind=kOutput, calls=%fused_computation.9 | convolution fusion | flops 67371008 | bytes 17571840 | tf_op jit(solution)/shard_map/ijc,ikc->jkc/dot_general | solution.py:136
  254.9 1.0 copy-done.3
  255.9 8.0 %fusion.27 = bf16[8,256,64]{1,0,2:T(8,128)(2,1)S(1)} fusion(bf16[256,256,64]{1,2,0:T(8,128)(2,1)} %all-gather.3.cloned.1.call-done, f32[8,256]{1,0:T(8,128)S(1)} %get-tuple-element.133, f32[8,256,64]{1,0,2:T(8,128)S(1)} %copy-done.3, f32[8,256]{1,0:T(8,128)S(1)} %negate_multiply_fusion.2), kind=kOutput, calls=%fused_computation.41 | convolution fusion | flops 67633152 | bytes 9191424 | tf_op jit(solution)/shard_map/ijc,jkc->ikc/dot_general | solution.py:133
  264.1 1.0 fusion.72
  265.2 15.7 %all-reduce.2.cloned.1.call-done = f32[8,256,64]{1,2,0:T(8,128)} async-done(((f32[8,256,64]{1,2,0:T(8,128)}), f32[8,256,64]{1,2,0:T(8,128)}) %all-reduce.2.cloned.1.call-update) | async-done | bytes 524304 | tf_op jit(solution)/shard_map/psum | solution.py:124
  280.8 1.8 fusion.35
  283.0 1.3 broadcast_add_fusion
  284.2 2.5 copy.85
  286.8 198.6 %reduce-scatter.2.cloned.1.call-done = f32[8,256,64]{1,0,2:T(8,128)} async-done(((f32[256,256,64]{1,0,2:T(8,128)}), f32[8,256,64]{1,0,2:T(8,128)}) %reduce-scatter.2.cloned.1.call-update) | async-done | bytes 524304 | tf_op jit(solution)/shard_map/reduce_scatter | solution.py:135
  485.4 1.1 multiply_convert_fusion
  486.7 1.2 convolution_add_fusion
  488.0 1.6 multiply_reduce_fusion
  489.6 63.4 %psum.15 = f32[2,64,64]{2,1,0:T(8,128)} all-reduce(f32[2,64,64]{2,1,0:T(8,128)S(1)} %pad_maximum_fusion), channel_id=1, replica_groups=mesh['tmpl'=4,'row'=32] {'tmpl','row'}, use_global_device_ids=true, to_apply=%region_23.24 | all-reduce | flops 8192 | bytes 65536 | tf_op jit(solution)/shard_map/psum | solution.py:147
  553.1 1.0 add_bitcast_fusion
  (112 shorter events, 3.9 us)
Async XLA Ops:
  7.2 227.5 %copy-start = (bf16[8,256,128]{2,1,0:T(8,128)(2,1)S(1)}, bf16[8,256,128]{2,1,0:T(8,128)(2,1)}, u32[]{:S(2)}) copy-start(bf16[8,256,128]{2,1,0:T(8,128)(2,1)} %param.35) | copy-start | bytes 1572868
  7.2 184.2 %copy-start.28 = (f32[64]{0:T(128)S(1)}, f32[64]{0:T(128)}, u32[]{:S(2)}) copy-start(f32[64]{0:T(128)} %param.29) | copy-start | bytes 772
  7.2 176.1 %all-gather.3.cloned.1.call-start = ((), (), s32[]{:S(2)}) async-start(), calls=%async_computation.1 | async-start | bytes 8650752 | tf_op jit(solution)/shard_map/all_gather | solution.py:100
  11.0 180.6 %copy-start.22 = (bf16[64,64]{1,0:T(8,128)(2,1)S(1)}, bf16[64,64]{1,0:T(8,128)(2,1)}, u32[]{:S(2)}) copy-start(bf16[64,64]{1,0:T(8,128)(2,1)} %param.28) | copy-start | bytes 24580
  11.1 181.0 %copy-start.13 = (f32[8,256]{1,0:T(8,128)}, f32[8,256]{1,0:T(8,128)S(1)}, u32[]{:S(2)}) copy-start(f32[8,256]{1,0:T(8,128)S(1)} %multiply_reduce_fusion.7) | copy-start | bytes 24580
  12.0 180.2 %copy-start.26 = (bf16[64,64]{1,0:T(8,128)(2,1)S(1)}, bf16[64,64]{1,0:T(8,128)(2,1)}, u32[]{:S(2)}) copy-start(bf16[64,64]{1,0:T(8,128)(2,1)} %param.27) | copy-start | bytes 24580
  12.0 180.2 %copy-start.31 = (f32[64]{0:T(128)S(1)}, f32[64]{0:T(128)}, u32[]{:S(2)}) copy-start(f32[64]{0:T(128)} %param.24) | copy-start | bytes 772
  13.7 210.7 %all-gather.5.cloned.1.call-start = ((), (), s32[]{:S(2)}) async-start(), calls=%async_computation.2 | async-start | bytes 2621440 | tf_op jit(solution)/shard_map/all_gather | solution.py:11
  14.8 178.9 %copy-start.6 = (bf16[8,256,64]{1,2,0:T(8,128)(2,1)}, bf16[8,256,64]{1,2,0:T(8,128)(2,1)S(1)}, u32[]{:S(2)}) copy-start(bf16[8,256,64]{1,2,0:T(8,128)(2,1)S(1)} %fusion.30) | copy-start | bytes 786436
  14.8 178.9 %copy-start.21 = (bf16[64,128]{1,0:T(8,128)(2,1)S(1)}, bf16[64,128]{1,0:T(8,128)(2,1)}, u32[]{:S(2)}) copy-start(bf16[64,128]{1,0:T(8,128)(2,1)} %param.31) | copy-start | bytes 49156
  14.8 178.9 %copy-start.30 = (f32[64]{0:T(128)S(1)}, f32[64]{0:T(128)}, u32[]{:S(2)}) copy-start(f32[64]{0:T(128)} %param.30) | copy-start | bytes 772
  14.8 181.5 %copy-start.7 = (bf16[8,256,128]{2,1,0:T(8,128)(2,1)S(1)}, bf16[8,256,128]{2,1,0:T(8,128)(2,1)}, u32[]{:S(2)}) copy-start(bf16[8,256,128]{2,1,0:T(8,128)(2,1)} %param.22) | copy-start | bytes 1572868
  191.4 5.5 copy-start.17
  191.4 2.2 copy-start.10
  192.2 4.1 copy-start.5
  193.7 3.2 copy-start.19
  193.7 3.1 copy-start.12
  194.4 1.0 copy-start.1
  196.3 84.6 %all-reduce.2.cloned.1.call-start = ((), (), s32[]{:S(2)}) async-start(), calls=%async_computation.4 | async-start | bytes 1048576 | tf_op jit(solution)/shard_map/psum | solution.py:124
  196.8 2.8 copy-start.15
  196.9 2.7 copy-start.8
  196.9 2.6 copy-start.20
  236.9 7.4 %copy-start.29 = (f32[64]{0:T(128)S(1)}, f32[64]{0:T(128)}, u32[]{:S(2)}) copy-start(f32[64]{0:T(128)} %param.29) | copy-start | bytes 772
  236.9 7.7 %copy-start.18 = (f32[8,256]{1,0:T(8,128)S(1)}, f32[8,256]{1,0:T(8,128)}, u32[]{:S(2)}) copy-start(f32[8,256]{1,0:T(8,128)} %copy-done.17) | copy-start | bytes 24580
  236.9 7.7 %copy-start.11 = (f32[8,256]{1,0:T(8,128)S(1)}, f32[8,256]{1,0:T(8,128)}, u32[]{:S(2)}) copy-start(f32[8,256]{1,0:T(8,128)} %copy-done.10) | copy-start | bytes 24580
  239.4 246.0 %reduce-scatter.2.cloned.1.call-start = ((), (), s32[]{:S(2)}) async-start(), calls=%async_computation.3 | async-start | bytes 17301504 | tf_op jit(solution)/shard_map/reduce_scatter | solution.py:135
  245.0 0.8 copy-start.2
  254.9 1.0 copy-start.3
  255.9 8.2 %copy-start.24 = (bf16[64,64]{1,0:T(8,128)(2,1)S(1)}, bf16[64,64]{1,0:T(8,128)(2,1)}, u32[]{:S(2)}) copy-start(bf16[64,64]{1,0:T(8,128)(2,1)} %param.25) | copy-start | bytes 24580
  255.9 24.9 %copy-start.23 = (bf16[128,64]{0,1:T(8,128)(2,1)S(1)}, bf16[128,64]{0,1:T(8,128)(2,1)}, u32[]{:S(2)}) copy-start(bf16[128,64]{0,1:T(8,128)(2,1)} %param.33) | copy-start | bytes 49156
  255.9 26.8 %copy-start.16 = (f32[8,256]{1,0:T(8,128)S(1)}, f32[8,256]{1,0:T(8,128)}, u32[]{:S(2)}) copy-start(f32[8,256]{1,0:T(8,128)} %copy-done.15) | copy-start | bytes 24580
  255.9 26.8 %copy-start.9 = (f32[8,256]{1,0:T(8,128)S(1)}, f32[8,256]{1,0:T(8,128)}, u32[]{:S(2)}) copy-start(f32[8,256]{1,0:T(8,128)} %copy-done.8) | copy-start | bytes 24580
  263.9 222.8 %copy-start.25 = (bf16[64,64]{1,0:T(8,128)(2,1)S(1)}, bf16[64,64]{1,0:T(8,128)(2,1)}, u32[]{:S(2)}) copy-start(bf16[64,64]{1,0:T(8,128)(2,1)} %param.26) | copy-start | bytes 24580
  263.9 224.1 %copy-start.4 = (f32[8,256,64]{1,2,0:T(8,128)S(1)}, f32[8,256,64]{1,2,0:T(8,128)}, u32[]{:S(2)}) copy-start(f32[8,256,64]{1,2,0:T(8,128)} %get-tuple-element.139) | copy-start | bytes 1572868
  263.9 224.1 %copy-start.27 = (bf16[64,64]{1,0:T(8,128)(2,1)S(1)}, bf16[64,64]{1,0:T(8,128)(2,1)}, u32[]{:S(2)}) copy-start(bf16[64,64]{1,0:T(8,128)(2,1)} %param.27) | copy-start | bytes 24580
  263.9 224.1 %copy-start.32 = (f32[64]{0:T(128)S(1)}, f32[64]{0:T(128)}, u32[]{:S(2)}) copy-start(f32[64]{0:T(128)} %param.24) | copy-start | bytes 772
  263.9 225.7 %copy-start.14 = (f32[8,256]{1,0:T(8,128)S(1)}, f32[8,256]{1,0:T(8,128)}, u32[]{:S(2)}) copy-start(f32[8,256]{1,0:T(8,128)} %copy-done.13) | copy-start | bytes 24580
Sparse Core Ops, SparseCore 0:
  13.8 169.4 all-gather.2
  196.4 28.0 all-gather.4
  239.5 41.3 all-reduce.1
  283.1 202.2 reduce-scatter.1
where the time goes:
time: 562 us; the launch traced here: 561 us
  waiting for transfers between devices  400 us (71%)
  blocking collectives  70.3 us (13%)
  matrix products  45.2 us (8%)
  other arithmetic  16.1 us (3%)
  between operations  14.4 us (3%)
  local copies, waits for them, and re-layouts  14.2 us (3%)
    reduce_scatter x1, waiting for transfers between devices, local(): lax.psum_scatter(jnp.einsum('ijc,ikc->jkc', d_tri_b, left, preferred_elem...  199 us
    all_gather x1, waiting for transfers between devices, local(): right_all = lax.all_gather(right, 'row', axis=0, tiled=True)  168 us
    psum x1, blocking collectives, local(): lax.psum(jnp.stack([grad_left, grad_right]), ('tmpl', 'row'))  63.4 us
    all_gather x1, waiting for transfers between devices, merged(): pieces = jax.tree.map(lambda part: lax.all_gather(part, axis), value)  17.2 us
    psum x1, waiting for transfers between devices, local(): lax.psum((d_score[..., None] * key).reshape(rows, width, hdim), 'tmpl')  15.7 us
    dot_general x8, matrix products, high_dot(): return jnp.einsum('...c,cd->...d', a, b, precision=lax.Precision.HIGHEST)  11.9 us
  transfers between devices with their start and end apart: 4, of which 4 were waited for; matrix products, arithmetic and copies ran while one was open for 6% of the time, Pallas kernels for 0%

commit v1 on v0

v1 whole, which is shorter than its diff:
```python
import functools

import jax
import jax.numpy as jnp
from jax import lax
from jax.experimental import pallas as pl
from jax.experimental.pallas import tpu as pltpu
from jax.sharding import PartitionSpec as P

F32 = jnp.float32
BF16 = jnp.bfloat16
HEADS = 4
HEAD_DIM = 16
C = 64
ROWS = 8
N = 256
SHARDS = 32
VMEM = pl.BlockSpec(memory_space=pltpu.VMEM)
SMEM = pl.BlockSpec(memory_space=pltpu.SMEM)


def dot(a, b, contract=((1,), (0,))):
    return lax.dot_general(a, b, (contract, ((), ())), preferred_element_type=F32)


def flip(x):
    return x.astype(F32).T


def column(row, lanes=N):
    tall = jnp.broadcast_to(row, (128, row.shape[1])).T
    return jnp.concatenate([tall] * (lanes // 128), axis=1)


def hat(x):
    mean = jnp.mean(x, 0, keepdims=True)
    cent = x - mean
    var = jnp.mean(cent * cent, 0, keepdims=True)
    rstd = lax.rsqrt(var + 1e-05)
    return cent * rstd, rstd


def hat_back(dy, xhat, rstd):
    return rstd * (dy - jnp.mean(dy, 0, keepdims=True) - xhat * jnp.mean(dy * xhat, 0, keepdims=True))


def put_rows(spread, first, step, x):
    for half in range(2):
        spread[half, pl.ds(first, x.shape[0], stride=step), :] = x[:, 128 * half : 128 * half + 128]


def take_rows(wide, first, step):
    return jnp.concatenate([wide[half, pl.ds(first, SHARDS, stride=step), :] for half in range(2)], axis=1)


def pack(spread, out):
    for half in range(2):
        out[:, :, 128 * half : 128 * half + 128] = spread[half].reshape(out.shape[0], out.shape[1], 128).astype(BF16)


def unpack(x, wide):
    for half in range(2):
        wide[half] = x[:, :, 128 * half : 128 * half + 128].astype(F32).reshape(wide.shape[1], 128)


def place(rows_ref):
    t = lax.axis_index("tmpl")
    start = lax.axis_index("row") * ROWS
    mask_row = rows_ref[pl.ds(t, 1), :].astype(F32)
    return t, start, mask_row


def project_kernel(pair, mask, mask_s, res, res_s, table, gain, wl, wr, lr_out, z_out, spread):
    t, start, mask_row = place(mask)
    weight = jnp.concatenate([flip(wl[...]), flip(wr[...])], axis=0).astype(BF16)
    table_t = flip(table[...]).astype(BF16)
    g = column(gain[...])
    residues = res[...]
    bins = lax.broadcasted_iota(jnp.int32, (128, N), 0)

    def body(i, carry):
        offset = jnp.clip(res_s[start + i] - residues, -64, 63) + 64
        onehot = jnp.where(bins == offset, 1.0, 0.0).astype(BF16)
        z = flip(pair[i]) + dot(table_t, onehot)
        z_out[i] = z
        ln_b = (hat(z)[0] * g).astype(BF16)
        both = dot(weight, ln_b) * (mask_row * mask_s[t, start + i].astype(F32))
        for q in range(4):
            put_rows(spread, 8 * q + i, 32, both[32 * q : 32 * q + 32])
        return carry

    lax.fori_loop(0, ROWS, body, 0)
    pack(spread, lr_out)


def tri_kernel(lr, tri_out, mats_out):
    wide = lr[...].astype(F32)
    mats = [wide[:, 8 * q : 8 * q + 8, :].reshape(N, N).astype(BF16) for q in range(4)]
    for q in range(4):
        mats_out[q] = mats[q]
    parts = [dot(mats[cc], mats[2 + cc], ((1,), (1,))).reshape(SHARDS, 8, N) for cc in range(2)]
    tri_out[...] = jnp.concatenate(parts, axis=1).astype(BF16)


def heads_sum(x):
    return jnp.sum(x.reshape(HEADS, HEAD_DIM, N), axis=1)


def heads_spread(x):
    return jnp.broadcast_to(x[:, None, :], (HEADS, HEAD_DIM, N)).reshape(C, N)


def attend_kernel(
    tri, z, query, cot, mask, mask_s, norm_gain, wg, wo, tri_gain, pair_gain, wkv, q_gain, wq, wao,
    sg_out, that_out, yhat_out, gate_out, upd_out, qh_out, do_out, kv_out, rstd_out, wide,
):
    t, start, mask_row = place(mask)
    unpack(tri, wide)
    wg_t = flip(wg[...]).astype(BF16)
    wo_t = flip(wo[...]).astype(BF16)
    wkv_t = flip(wkv[...]).astype(BF16)
    wq_t = flip(wq[...]).astype(BF16)
    wao_v = wao[...]
    g_norm, g_tri, g_pair = column(norm_gain[...]), column(tri_gain[...]), column(pair_gain[...])
    g_query = q_gain[...]

    def body(i, carry):
        x = query[i].astype(F32)
        cent = x - jnp.mean(x, -1, keepdims=True)
        var = jnp.mean(cent * cent, -1, keepdims=True)
        qn = (cent * lax.rsqrt(var + 1e-05) * g_query).astype(BF16)
        qh = dot(wq_t, qn, ((1,), (1,))) * HEAD_DIM ** (-0.5)
        d_o = dot(wao_v, cot[i], ((1,), (1,)))
        qh_out[i] = qh
        do_out[i] = d_o

        tri_i = jnp.concatenate([take_rows(wide, i, 16), take_rows(wide, 8 + i, 16)], axis=0)
        that, rstd_t = hat(tri_i)
        upd = dot(wo_t, (that * g_tri).astype(BF16))
        z_i = z[i]
        gate = jax.nn.sigmoid(dot(wg_t, (hat(z_i)[0] * g_norm).astype(BF16)))
        yhat, rstd_y = hat(z_i + gate * upd)
        kv = dot(wkv_t, (yhat * g_pair).astype(BF16)).astype(BF16)
        kv_f = kv.astype(F32)
        pm = mask_row * mask_s[t, start + i].astype(F32)
        score = heads_sum(qh * kv_f[:C]) * pm + (pm - 1.0) * 1000000000.0
        dot_v = heads_sum(d_o * kv_f[C:])
        sg_out[i] = jnp.concatenate([score, dot_v], axis=0)
        that_out[i] = that
        yhat_out[i] = yhat
        gate_out[i] = gate
        upd_out[i] = upd
        kv_out[i] = kv
        rstd_out[i] = jnp.concatenate([jnp.broadcast_to(rstd_t, (4, N)), jnp.broadcast_to(rstd_y, (4, N))], axis=0)
        return carry

    lax.fori_loop(0, ROWS, body, 0)


def back_kernel(
    sg, that, yhat, gate, upd, qh, do, kv, rstd, mask, mask_s, wg, wo, tri_gain, pair_gain, wkv,
    dtri_out, dln_out, dzin_out, dqh_out, spread,
):
    t, start, mask_row = place(mask)
    g_tri, g_pair = column(tri_gain[...]), column(pair_gain[...])
    wg_v, wo_v, wkv_v = wg[...], wo[...], wkv[...]

    def body(i, carry):
        pm = mask_row * mask_s[t, start + i].astype(F32)
        every = [sg[s, i] for s in range(4)]
        own = sg[t, i]
        top = jnp.maximum(jnp.maximum(every[0][:4], every[1][:4]), jnp.maximum(every[2][:4], every[3][:4]))
        expo = [jnp.exp(e[:4] - top) for e in every]
        inv = 1.0 / (expo[0] + expo[1] + expo[2] + expo[3])
        delta = sum(ex * e[4:] for ex, e in zip(expo, every)) * inv
        prob = jnp.exp(own[:4] - top) * inv
        ds = heads_spread(pm * prob * (own[4:] - delta))
        p = heads_spread(prob)
        d_kv = jnp.concatenate([ds * qh[i], p * do[i]], axis=0).astype(BF16)
        dqh_out[i] = (ds * kv[i].astype(F32)[:C]).astype(BF16)
        rs = rstd[i]
        d_y = hat_back(dot(wkv_v, d_kv) * g_pair, yhat[i], rs[4:5])
        gate_i = gate[i]
        d_gpre = d_y * upd[i] * gate_i * (1.0 - gate_i)
        dln_out[i] = dot(wg_v, d_gpre.astype(BF16))
        dzin_out[i] = d_y
        d_tn = dot(wo_v, (d_y * gate_i).astype(BF16)) * g_tri
        d_tri = hat_back(d_tn, that[i], rs[0:1])
        put_rows(spread, i, 16, d_tri[:32])
        put_rows(spread, 8 + i, 16, d_tri[32:])
        return carry

    lax.fori_loop(0, ROWS, body, 0)
    pack(spread, dtri_out)


def tri_back_kernel(dtri, mats, out):
    wide = dtri[...].astype(F32)
    d = [wide[:, 8 * cc : 8 * cc + 8, :].reshape(N, N).astype(BF16) for cc in range(2)]
    parts = [dot(d[cc], mats[2 + cc]) for cc in range(2)]
    parts += [dot(d[cc], mats[cc], ((0,), (0,))) for cc in range(2)]
    out[...] = jnp.concatenate([p.reshape(SHARDS, 8, N) for p in parts], axis=1).astype(BF16)


def final_kernel(dlr, z, dln, dzin, mask, mask_s, norm_gain, wl, wr, grad_out, proj_out, wide):
    t, start, mask_row = place(mask)
    unpack(dlr, wide)
    g = column(norm_gain[...])
    weight = jnp.concatenate([wl[...], wr[...]], axis=1)

    def body(i, total):
        pm = mask_row * mask_s[t, start + i].astype(F32)
        parts = [take_rows(wide, 8 * q + i, 32) for q in range(4)]
        d = (jnp.concatenate(parts, axis=0) * pm).astype(BF16)
        zhat, rstd = hat(z[i])
        total = total + dot((zhat * g).astype(BF16), d, ((1,), (1,)))
        dy = (dln[i] + dot(weight, d)) * g
        grad_out[i] = (dzin[i] + hat_back(dy, zhat, rstd)).T
        return total

    proj_out[...] = lax.fori_loop(0, ROWS, body, jnp.zeros((C, 2 * C), F32))


def query_kernel(query, dqh, gain, wq, out):
    g = gain[...] * HEAD_DIM ** (-0.5)
    wq_v = wq[...]

    def body(i, carry):
        x = query[i].astype(F32)
        cent = x - jnp.mean(x, -1, keepdims=True)
        var = jnp.mean(cent * cent, -1, keepdims=True)
        rstd = lax.rsqrt(var + 1e-05)
        xhat = cent * rstd
        dy = dot(dqh[i].astype(BF16), wq_v, ((0,), (1,))) * g
        out[i] = rstd * (dy - jnp.mean(dy, -1, keepdims=True) - xhat * jnp.mean(dy * xhat, -1, keepdims=True))
        return carry

    lax.fori_loop(0, ROWS, body, 0)


def call(kernel, outs, specs, scratch=()):
    return pl.pallas_call(
        kernel,
        out_shape=[jax.ShapeDtypeStruct(s, d) for s, d in outs],
        in_specs=specs,
        out_specs=[VMEM] * len(outs),
        scratch_shapes=[pltpu.VMEM(s, F32) for s in scratch],
        compiler_params=pltpu.CompilerParams(vmem_limit_bytes=40 * 1024 * 1024),
    )


def swap(x, axis, size, bit):
    return lax.ppermute(x, axis, [(i, i ^ bit) for i in range(size)])


def local(
    template_pair, template_mask, residue_index, query_pair, relpos_table, norm_gain, left_weight, right_weight,
    gate_weight, out_weight, tri_gain, pair_gain, kv_weight, query_gain, query_weight, attn_out_weight, cotangent,
):
    pair = template_pair[0]
    row = lambda x: x.reshape(1, -1)
    every = functools.partial(lax.all_to_all, axis_name="row", split_axis=0, concat_axis=0, tiled=True)
    lr, z = call(
        project_kernel,
        [((SHARDS, 32, N), BF16), ((ROWS, C, N), F32)],
        [VMEM, VMEM, SMEM, VMEM, SMEM] + [VMEM] * 4,
        [(2, SHARDS * 32, 128)],
    )(
        pair, template_mask, template_mask, row(residue_index), residue_index, relpos_table, row(norm_gain),
        left_weight, right_weight,
    )
    lr = every(lr)
    tri, mats = call(tri_kernel, [((SHARDS, 16, N), BF16), ((4, N, N), BF16)], [VMEM])(lr)
    tri = every(tri)
    sg, that, yhat, gate, upd, qh, do, kv, rstd = call(
        attend_kernel,
        [((ROWS, 8, N), F32)] + [((ROWS, C, N), F32)] * 6 + [((ROWS, 2 * C, N), BF16), ((ROWS, 8, N), F32)],
        [VMEM] * 5 + [SMEM] + [VMEM] * 9,
        [(2, SHARDS * 16, 128)],
    )(
        tri, z, query_pair, cotangent, template_mask, template_mask, row(norm_gain), gate_weight, out_weight,
        row(tri_gain), row(pair_gain), kv_weight, row(query_gain), query_weight, attn_out_weight,
    )
    sg = lax.all_gather(sg, "tmpl")
    dtri, dln, dzin, dqh = call(
        back_kernel,
        [((SHARDS, 16, N), BF16), ((ROWS, C, N), F32), ((ROWS, C, N), F32), ((ROWS, C, N), BF16)],
        [VMEM] * 10 + [SMEM] + [VMEM] * 5,
        [(2, SHARDS * 16, 128)],
    )(
        sg, that, yhat, gate, upd, qh, do, kv, rstd, template_mask, template_mask, gate_weight, out_weight,
        row(tri_gain), row(pair_gain), kv_weight,
    )
    dtri = every(dtri)
    dqh = dqh + swap(dqh, "tmpl", 4, 1)
    (dlr,) = call(tri_back_kernel, [((SHARDS, 32, N), BF16)], [VMEM, VMEM])(dtri, mats)
    dlr = every(dlr)
    dqh = dqh + swap(dqh, "tmpl", 4, 2)
    grad, proj = call(
        final_kernel,
        [((ROWS, N, C), F32), ((C, 2 * C), F32)],
        [VMEM] * 5 + [SMEM] + [VMEM] * 3,
        [(2, SHARDS * 32, 128)],
    )(dlr, z, dln, dzin, template_mask, template_mask, row(norm_gain), left_weight, right_weight)
    (query_grad,) = call(query_kernel, [((ROWS, N, 2 * C), F32)], [VMEM] * 4)(
        query_pair, dqh, row(query_gain), query_weight
    )
    proj = proj + swap(proj, "tmpl", 4, 1)
    proj = proj + swap(proj, "tmpl", 4, 2)
    proj = jnp.sum(every(jnp.broadcast_to(proj[None], (SHARDS, C, 2 * C))), axis=0)
    return grad[None], query_grad, jnp.stack([proj[:, :C], proj[:, C:]])


def solution(mesh):
    in_specs = (
        P("tmpl", "row", None, None),
        P(),
        P(),
        P("row", None, None),
        *([P()] * 12),
        P("row", None, None),
    )
    out_specs = (P("tmpl", "row", None, None), P("row", None, None), P())
    return jax.shard_map(local, mesh=mesh, in_specs=in_specs, out_specs=out_specs, check_vma=False)
```

time: 562 us -> 133 us (0.24)
  waiting for transfers between devices: 400 us -> 30.1 us
  matrix products: 45.2 us -> 0 us
  Pallas kernels: 0 us -> 21.3 us
  starting transfers between devices: 0.35 us -> 15.6 us
  blocking collectives: 70.3 us -> 55.6 us
  other arithmetic: 16.1 us -> 2.08 us
  between operations: 14.4 us -> 0.88 us
  local copies, waits for them, and re-layouts: 14.2 us -> 5.82 us
    reduce_scatter x1 -> x0, waiting for transfers between devices: 199 us -> none  [local(): lax.psum_scatter(jnp.einsum('ijc,ikc->jkc', d_tri_b, left, preferred_elem...]
    all_gather x2 -> x0, waiting for transfers between devices: 186 us -> none  [the longest x1 168 us: local(): right_all = lax.all_gather(right, 'row', axis=0, tiled=True)]
    psum x1 -> x0, blocking collectives: 63.4 us -> none  [local(): lax.psum(jnp.stack([grad_left, grad_right]), ('tmpl', 'row'))]
    all_to_all x0 -> x3, blocking collectives: none -> 47.8 us  [the longest x1 20.1 us: local(): lr = every(lr)]
    dot_general x19 -> x0, matrix products: 45.2 us -> none  [the longest x8 11.9 us: high_dot(): return jnp.einsum('...c,cd->...d', a, b, precision=lax.Precision.HIGHEST)]
    pallas_call x0 -> x7, Pallas kernels: none -> 21.3 us  [the longest x1 4.39 us: local(): call(project_kernel, [((SHARDS, 32, N), BF16), ((ROWS, C, N), F32)], [VME...]
    ppermute x0 -> x4, waiting for transfers between devices: none -> 21 us  [swap(): return lax.ppermute(x, axis, [(i, i ^ bit) for i in range(size)])]
    psum x1 -> x0, waiting for transfers between devices: 15.7 us -> none  [local(): lax.psum((d_score[..., None] * key).reshape(rows, width, hdim), 'tmpl')]
  transfers between devices with their start and end apart: 4 -> 6, of which waited for: 4 -> 5; matrix products, arithmetic and copies ran while one was open for 6% -> 1% of each run, Pallas kernels for 0% -> 3%
where the time goes in v1:
time: 133 us; the launch traced here: 131 us
  blocking collectives  55.6 us (42%)
  waiting for transfers between devices  30.1 us (23%)
  Pallas kernels  21.3 us (16%)
  starting transfers between devices  15.6 us (12%)
  local copies, waits for them, and re-layouts  5.82 us (4%)
  other arithmetic  2.08 us (2%)
    ppermute x4, waiting for transfers between devices, swap(): return lax.ppermute(x, axis, [(i, i ^ bit) for i in range(size)])  21 us
    all_to_all x1, blocking collectives, local(): lr = every(lr)  20.1 us
    all_to_all x1, blocking collectives, local(): dlr = every(dlr)  14.7 us
    all_to_all x1, blocking collectives, local(): dtri = every(dtri)  13 us
    all_to_all x1, waiting for transfers between devices, local(): tri = every(tri)  9.06 us
    all_gather x1, blocking collectives, local(): sg = lax.all_gather(sg, 'tmpl')  7.84 us
    ppermute x4, starting transfers between devices, swap(): return lax.ppermute(x, axis, [(i, i ^ bit) for i in range(size)])  6.79 us
    all_to_all x1, starting transfers between devices, local(): every(jnp.broadcast_to(proj[None], (SHARDS, C, 2 * C)))  4.67 us
  transfers between devices with their start and end apart: 6, of which 5 were waited for; matrix products, arithmetic and copies ran while one was open for 1% of the time, Pallas kernels for 3%

profile of v1, /device:TPU:0, one launch (start us, length us, event | category | flops | bytes accessed | tf_op | source)
XLA Modules:
  0.0 131.5 jit_solution(272430444606355745)
XLA Ops:
  0.6 0.8 copy.31.table
  1.5 0.0 copy-start.6
  1.5 0.0 copy-start.7
  1.5 1.3 copy.30
  2.7 0.0 copy-start.2
  2.8 0.0 copy-start.9
  2.8 0.0 copy-start.10
  2.8 0.6 copy-done.2
  3.4 0.0 copy-done.10
  3.5 4.4 %shard_map.184 = (bf16[32,32,256]{2,1,0:T(8,128)(2,1)S(1)}, f32[8,64,256]{2,1,0:T(8,128)S(1)}) custom-call(bf16[8,256,64]{2,1,0:T(8,128)(2,1)S(1)} %bitcast.12, s32[4,256]{1,0:T(4,128)S(1)} %copy-done.2, s32[4,256]{1,0:T(4,128)S(1)} %copy-done.2, s32[1,256]{1,0:T(1,128)S(1)} %bitcast.18, s32[256]{0:T(256)S(1)} %copy-done.10, ...), custom_call_target="tpu_custom_call" | custom-call | tf_op jit(solution)/shard_map/pallas_call | solution.py:263
  7.9 0.0 copy-start.14
  7.9 0.0 copy-start.8
  7.9 20.1 %all_to_all.25.lr = bf16[32,32,256]{2,1,0:T(8,128)(2,1)S(1)} all-to-all(bf16[32,32,256]{2,1,0:T(8,128)(2,1)S(1)} %get-tuple-element.22), channel_id=1, replica_groups=mesh['tmpl'=4,'row'=32] {'row'}, dimensions={0} | all-to-all | bytes 1048576 | tf_op jit(solution)/shard_map/all_to_all | solution.py:272
  28.0 1.0 shard_map.185
  29.0 4.2 %all-to-all-start.1 = ((bf16[32,16,256]{2,1,0:T(8,128)(2,1)}), bf16[32,16,256]{2,1,0:T(8,128)(2,1)S(1)}, u32[]{:S(2)}, u32[]{:S(2)}) async-start(bf16[32,16,256]{2,1,0:T(8,128)(2,1)} %get-tuple-element.23), calls=%async_computation.1 | async-start | bytes 524288 | tf_op jit(solution)/shard_map/all_to_all | solution.py:274
  33.2 0.0 copy-start.3
  33.2 0.0 copy-start.4
  33.2 0.0 copy-start.5
  33.2 0.1 copy.32.wq
  33.4 9.1 %all-to-all-done.1.tri = bf16[32,16,256]{2,1,0:T(8,128)(2,1)S(1)} async-done(((bf16[32,16,256]{2,1,0:T(8,128)(2,1)}), bf16[32,16,256]{2,1,0:T(8,128)(2,1)S(1)}, u32[]{:S(2)}, u32[]{:S(2)}) %all-to-all-start.1) | async-done | bytes 262176 | tf_op jit(solution)/shard_map/all_to_all | solution.py:274
  42.5 0.6 copy-done.11
  43.1 0.0 copy-done.12
  43.1 0.0 copy-done.13
  43.1 4.4 %shard_map.186 = (f32[8,8,256]{2,1,0:T(8,128)S(1)}, f32[8,64,256]{2,1,0:T(8,128)S(1)}, f32[8,64,256]{2,1,0:T(8,128)S(1)}, f32[8,64,256]{2,1,0:T(8,128)S(1)}, f32...) custom-call(bf16[32,16,256]{2,1,0:T(8,128)(2,1)S(1)} %all-to-all-don, ...), custom_call_target="tpu_custom_call" | custom-call | tf_op jit(solution)/shard_map/pallas_call | solution.py:275
  47.5 7.8 %all-gather = f32[32,8,256]{2,1,0:T(8,128)S(1)} all-gather(f32[8,8,256]{2,1,0:T(8,128)S(1)} %get-tuple-element.25), channel_id=2, replica_groups=mesh['tmpl'=4,'row'=32] {'tmpl'}, dimensions={0}, use_global_device_ids=true | all-gather | bytes 327680 | tf_op jit(solution)/shard_map/all_gather | solution.py:284
  55.3 3.9 %shard_map.187 = (bf16[32,16,256]{2,1,0:T(8,128)(2,1)S(1)}, f32[8,64,256]{2,1,0:T(8,128)S(1)}, f32[8,64,256]{2,1,0:T(8,128)S(1)}, bf16[8,64,256]{2,1,0:T(8,128)(2,1)S(1)}) custom-call(f32[4,8,8,256]{3,2,1,0:T(8,128)S(1)} %bitcast.13, f32[8,64,256]{2,1,0:T(8,128)S(1)} %get-tuple-element.26.that, f32[8,64,256]{2,1,0:T(8,128)S(1)} %get-tuple-element.27.yhat, ...), custom_call_target="tpu_custom_call" | custom-call | tf_op jit(solution)/shard_map/pallas_call | solution.py:285
  59.3 13.0 %all_to_all.26.dtri = bf16[32,16,256]{2,1,0:T(8,128)(2,1)S(1)} all-to-all(bf16[32,16,256]{2,1,0:T(8,128)(2,1)S(1)} %get-tuple-element.34), channel_id=1, replica_groups=mesh['tmpl'=4,'row'=32] {'row'}, dimensions={0} | all-to-all | bytes 524288 | tf_op jit(solution)/shard_map/all_to_all | solution.py:294
  72.3 0.3 shard_map.188
  72.6 14.7 %all_to_all.27.dlr = bf16[32,32,256]{2,1,0:T(8,128)(2,1)S(1)} all-to-all(bf16[32,32,256]{2,1,0:T(8,128)(2,1)S(1)} %shard_map.188), channel_id=1, replica_groups=mesh['tmpl'=4,'row'=32] {'row'}, dimensions={0} | all-to-all | bytes 1048576 | tf_op jit(solution)/shard_map/all_to_all | solution.py:297
  87.3 3.6 %shard_map.189 = (f32[8,256,64]{2,1,0:T(8,128)S(1)}, f32[64,128]{1,0:T(8,128)S(1)}) custom-call(bf16[32,32,256]{2,1,0:T(8,128)(2,1)S(1)} %all_to_all.27.dlr, f32[8,64,256]{2,1,0:T(8,128)S(1)} %get-tuple-element.24.z, f32[8,64,256]{2,1,0:T(8,128)S(1)} %get-tuple-element.36.dln, f32[8,64,256]{2,1,0:T(8,128)S(1)} %get-tuple-element.37.dzin, ...), custom_call_target="tpu_custom_call" | custom-call | tf_op jit(solution)/shard_map/pallas_call | solution.py:299
  90.8 0.1 collective-permute-start.2
  90.9 1.2 collective-permute-done.2
  92.1 3.3 %collective-permute-start.3 = (f32[64,128]{1,0:T(8,128)S(1)}, f32[64,128]{1,0:T(8,128)S(1)}, u32[]{:S(2)}, u32[]{:S(2)}) collective-permute-start(f32[64,128]{1,0:T(8,128)S(1)} %add.14), channel_id=1, source_target_pairs={{0,64},{32,96},{64,0},{96,32},{1,65},{33,97},{65,1},{97,33},{2,66}... | collective-permute-start | bytes 98312 | tf_op jit(solution)/shard_map/ppermute | solution.py:253
  95.4 2.2 %collective-permute-done.3 = f32[64,128]{1,0:T(8,128)S(1)} collective-permute-done((f32[64,128]{1,0:T(8,128)S(1)}, f32[64,128]{1,0:T(8,128)S(1)}, u32[]{:S(2)}, u32[]{:S(2)}) %collective-permute-start.3) | collective-permute-done | bytes 32800 | tf_op jit(solution)/shard_map/ppermute | solution.py:253
  97.5 1.1 broadcast_in_dim.10
  98.6 4.7 %all-to-all-start.4 = ((f32[32,64,128]{2,1,0:T(8,128)}), f32[32,64,128]{2,1,0:T(8,128)}, u32[]{:S(2)}, u32[]{:S(2)}) async-start(f32[32,64,128]{2,1,0:T(8,128)} %broadcast_in_dim.10), calls=%async_computation.4 | async-start | bytes 2097152 | tf_op jit(solution)/shard_map/all_to_all | solution.py:310
  103.3 0.1 collective-permute-start
  103.4 1.5 %collective-permute-done = bf16[8,64,256]{2,1,0:T(8,128)(2,1)S(1)} collective-permute-done((bf16[8,64,256]{2,1,0:T(8,128)(2,1)S(1)}, bf16[8,64,256]{2,1,0:T(8,128)(2,1)S(1)}, u32[]{:S(2)}, u32[]{:S(2)}) %collective-permute-start) | collective-permute-done | bytes 262176 | tf_op jit(solution)/shard_map/ppermute | solution.py:253
  104.9 0.1 add.12
  105.0 3.3 %collective-permute-start.1 = (bf16[8,64,256]{2,1,0:T(8,128)(2,1)S(1)}, bf16[8,64,256]{2,1,0:T(8,128)(2,1)S(1)}, u32[]{:S(2)}, u32[]{:S(2)}) collective-permute-start(bf16[8,64,256]{2,1,0:T(8,128)(2,1)S(1)} %add.12), channel_id=1, source_target_pairs={{0,64},{32,96},{64,0},{96,32},{1,65},{33,97},{65,1},{97,33},{2,66}... | collective-permute-start | bytes 786440 | tf_op jit(solution)/shard_map/ppermute | solution.py:253
  108.3 16.1 %collective-permute-done.1 = bf16[8,64,256]{2,1,0:T(8,128)(2,1)S(1)} collective-permute-done((bf16[8,64,256]{2,1,0:T(8,128)(2,1)S(1)}, bf16[8,64,256]{2,1,0:T(8,128)(2,1)S(1)}, u32[]{:S(2)}, u32[]{:S(2)}) %collective-permute-start.1) | collective-permute-done | bytes 262176 | tf_op jit(solution)/shard_map/ppermute | solution.py:253
  124.5 0.1 add.13.dqh
  124.6 3.8 %shard_map.190 = f32[8,256,128]{2,1,0:T(8,128)} custom-call(bf16[8,256,128]{2,1,0:T(8,128)(2,1)S(1)} %copy-done, bf16[8,64,256]{2,1,0:T(8,128)(2,1)S(1)} %add.13.dqh, f32[1,128]{1,0:T(1,128)S(1)} %bitcast.24, bf16[128,64]{1,0:T(8,128)(2,1)S(1)} %copy.32.wq), custom_call_target="tpu_custom_call" | custom-call | tf_op jit(solution)/shard_map/pallas_call | solution.py:305
  128.4 1.1 copy.34
  129.5 0.0 all-to-all-done.4
  129.5 1.3 reduce_sum.9
  130.8 0.1 slice_bitcast_fusion.1
  130.8 0.6 pad_maximum_fusion
  (17 shorter events, 0.0 us)
Async XLA Ops:
  1.5 1.3 %copy-start.6 = (bf16[64,64]{1,0:T(8,128)(2,1)S(1)}, bf16[64,64]{1,0:T(8,128)(2,1)}, u32[]{:S(2)}) copy-start(bf16[64,64]{1,0:T(8,128)(2,1)} %wl.3) | copy-start | bytes 24580
  1.5 1.3 %copy-start.7 = (bf16[64,64]{1,0:T(8,128)(2,1)S(1)}, bf16[64,64]{1,0:T(8,128)(2,1)}, u32[]{:S(2)}) copy-start(bf16[64,64]{1,0:T(8,128)(2,1)} %wr.3) | copy-start | bytes 24580
  2.7 0.7 copy-start.2
  2.8 0.7 copy-start.9
  2.8 0.7 copy-start.10
  7.9 25.3 %copy-start.14 = (bf16[128,64]{0,1:T(8,128)(2,1)S(1)}, bf16[128,64]{0,1:T(8,128)(2,1)}, u32[]{:S(2)}) copy-start(bf16[128,64]{0,1:T(8,128)(2,1)} %param.31) | copy-start | bytes 49156
  7.9 34.6 %copy-start.8 = (bf16[64,128]{1,0:T(8,128)(2,1)S(1)}, bf16[64,128]{1,0:T(8,128)(2,1)}, u32[]{:S(2)}) copy-start(bf16[64,128]{1,0:T(8,128)(2,1)} %wao.1) | copy-start | bytes 49156
  28.0 14.4 %copy-start = (bf16[8,256,128]{2,1,0:T(8,128)(2,1)S(1)}, bf16[8,256,128]{2,1,0:T(8,128)(2,1)}, u32[]{:S(2)}) copy-start(bf16[8,256,128]{2,1,0:T(8,128)(2,1)} %query.3) | copy-start | bytes 1572868
  28.0 14.4 %copy-start.1 = (bf16[8,256,128]{2,1,0:T(8,128)(2,1)S(1)}, bf16[8,256,128]{2,1,0:T(8,128)(2,1)}, u32[]{:S(2)}) copy-start(bf16[8,256,128]{2,1,0:T(8,128)(2,1)} %cot.1) | copy-start | bytes 1572868
  29.0 13.4 %all-to-all-start.1 = ((bf16[32,16,256]{2,1,0:T(8,128)(2,1)}), bf16[32,16,256]{2,1,0:T(8,128)(2,1)S(1)}, u32[]{:S(2)}, u32[]{:S(2)}) async-start(bf16[32,16,256]{2,1,0:T(8,128)(2,1)} %get-tuple-element.23), calls=%async_computation.1 | async-start | bytes 524288 | tf_op jit(solution)/shard_map/all_to_all | solution.py:274
  33.2 9.3 %copy-start.3 = (bf16[64,64]{1,0:T(8,128)(2,1)S(1)}, bf16[64,64]{1,0:T(8,128)(2,1)}, u32[]{:S(2)}) copy-start(bf16[64,64]{1,0:T(8,128)(2,1)} %wg.3) | copy-start | bytes 24580
  33.2 9.2 %copy-start.4 = (bf16[64,64]{1,0:T(8,128)(2,1)S(1)}, bf16[64,64]{1,0:T(8,128)(2,1)}, u32[]{:S(2)}) copy-start(bf16[64,64]{1,0:T(8,128)(2,1)} %wo.3) | copy-start | bytes 24580
  33.2 9.2 %copy-start.5 = (bf16[64,128]{1,0:T(8,128)(2,1)S(1)}, bf16[64,128]{1,0:T(8,128)(2,1)}, u32[]{:S(2)}) copy-start(bf16[64,128]{1,0:T(8,128)(2,1)} %wkv.3) | copy-start | bytes 49156
  42.4 0.7 copy-start.11
  42.4 0.7 copy-start.12
  42.4 0.7 copy-start.13
  90.8 1.3 collective-permute-start.2
  92.1 5.4 %collective-permute-start.3 = (f32[64,128]{1,0:T(8,128)S(1)}, f32[64,128]{1,0:T(8,128)S(1)}, u32[]{:S(2)}, u32[]{:S(2)}) collective-permute-start(f32[64,128]{1,0:T(8,128)S(1)} %add.14), channel_id=1, source_target_pairs={{0,64},{32,96},{64,0},{96,32},{1,65},{33,97},{65,1},{97,33},{2,66}... | collective-permute-start | bytes 98312 | tf_op jit(solution)/shard_map/ppermute | solution.py:253
  98.6 30.8 %all-to-all-start.4 = ((f32[32,64,128]{2,1,0:T(8,128)}), f32[32,64,128]{2,1,0:T(8,128)}, u32[]{:S(2)}, u32[]{:S(2)}) async-start(f32[32,64,128]{2,1,0:T(8,128)} %broadcast_in_dim.10), calls=%async_computation.4 | async-start | bytes 2097152 | tf_op jit(solution)/shard_map/all_to_all | solution.py:310
  103.3 1.6 %collective-permute-start = (bf16[8,64,256]{2,1,0:T(8,128)(2,1)S(1)}, bf16[8,64,256]{2,1,0:T(8,128)(2,1)S(1)}, u32[]{:S(2)}, u32[]{:S(2)}) collective-permute-start(bf16[8,64,256]{2,1,0:T(8,128)(2,1)S(1)} %get-tuple-element.39), channel_id=1, source_target_pairs={{0,32},{32,0},{64,96},{96,64},{1,33},{33,1},{65,97},{97,65},{2,34}... | collective-permute-start | bytes 786440 | tf_op jit(solution)/shard_map/ppermute | solution.py:253
  105.0 19.5 %collective-permute-start.1 = (bf16[8,64,256]{2,1,0:T(8,128)(2,1)S(1)}, bf16[8,64,256]{2,1,0:T(8,128)(2,1)S(1)}, u32[]{:S(2)}, u32[]{:S(2)}) collective-permute-start(bf16[8,64,256]{2,1,0:T(8,128)(2,1)S(1)} %add.12), channel_id=1, source_target_pairs={{0,64},{32,96},{64,0},{96,32},{1,65},{33,97},{65,1},{97,33},{2,66}... | collective-permute-start | bytes 786440 | tf_op jit(solution)/shard_map/ppermute | solution.py:253

commit v2 on v1

v2 whole, which is shorter than its diff:
```python
import functools

import jax
import jax.numpy as jnp
from jax import lax
from jax.experimental import pallas as pl
from jax.experimental.pallas import tpu as pltpu
from jax.sharding import PartitionSpec as P

F32 = jnp.float32
BF16 = jnp.bfloat16
HEADS = 4
HEAD_DIM = 16
C = 64
ROWS = 8
N = 256
SHARDS = 32
UNROLL = 4
VMEM = pl.BlockSpec(memory_space=pltpu.VMEM)
SMEM = pl.BlockSpec(memory_space=pltpu.SMEM)


def dot(a, b, contract=((1,), (0,))):
    return lax.dot_general(a, b, (contract, ((), ())), preferred_element_type=F32)


def flip(x):
    return x.astype(F32).T


def column(row, lanes=N):
    tall = jnp.broadcast_to(row, (128, row.shape[1])).T
    return jnp.concatenate([tall] * (lanes // 128), axis=1)


def hat(x):
    mean = jnp.mean(x, 0, keepdims=True)
    cent = x - mean
    var = jnp.mean(cent * cent, 0, keepdims=True)
    rstd = lax.rsqrt(var + 1e-05)
    return cent * rstd, rstd


def hat_back(dy, xhat, rstd):
    return rstd * (dy - jnp.mean(dy, 0, keepdims=True) - xhat * jnp.mean(dy * xhat, 0, keepdims=True))


def put_rows(spread, first, step, x):
    for half in range(2):
        spread[half, pl.ds(first, x.shape[0], stride=step), :] = x[:, 128 * half : 128 * half + 128]


def take_rows(wide, first, step):
    return jnp.concatenate([wide[half, pl.ds(first, SHARDS, stride=step), :] for half in range(2)], axis=1)


def pack(spread, out):
    for half in range(2):
        out[:, :, 128 * half : 128 * half + 128] = spread[half].reshape(out.shape[0], out.shape[1], 128).astype(BF16)


def unpack(x, wide):
    for half in range(2):
        wide[half] = x[:, :, 128 * half : 128 * half + 128].astype(F32).reshape(wide.shape[1], 128)


def place(rows_ref):
    t = lax.axis_index("tmpl")
    start = lax.axis_index("row") * ROWS
    mask_row = rows_ref[pl.ds(t, 1), :].astype(F32)
    return t, start, mask_row


def each_row(body, carry=0, unroll=UNROLL):
    def step(s, carry):
        for u in range(unroll):
            carry = body(s * unroll + u, carry)
        return carry

    if unroll == ROWS:
        return step(0, carry)
    return lax.fori_loop(0, ROWS // unroll, step, carry)


def project_kernel(pair, mask, mask_s, res, res_s, table_t, gain, wl, wr, lr_out, z_out, ln_out, spread):
    t, start, mask_row = place(mask)
    weight = jnp.concatenate([flip(wl[...]), flip(wr[...])], axis=0).astype(BF16)
    table = table_t[...]
    g = column(gain[...])
    residues = res[...]
    bins = lax.broadcasted_iota(jnp.int32, (128, N), 0)

    def body(i, carry):
        offset = jnp.clip(res_s[start + i] - residues, -64, 63) + 64
        onehot = jnp.where(bins == offset, 1.0, 0.0).astype(BF16)
        z = pair[i].astype(F32) + dot(table, onehot)
        z_out[i] = z
        ln_b = (hat(z)[0] * g).astype(BF16)
        ln_out[i] = ln_b
        both = dot(weight, ln_b) * (mask_row * mask_s[t, start + i].astype(F32))
        for q in range(4):
            put_rows(spread, 8 * q + i, 32, both[32 * q : 32 * q + 32])
        return carry

    each_row(body)
    pack(spread, lr_out)


def query_kernel(query, cot, ln_b, wg, q_gain, wq_t, wao, qh_out, do_out, gate_out):
    wg_t = flip(wg[...]).astype(BF16)
    wq_v, wao_v, g_query = wq_t[...], wao[...], q_gain[...]

    def body(i, carry):
        x = query[i].astype(F32)
        cent = x - jnp.mean(x, -1, keepdims=True)
        var = jnp.mean(cent * cent, -1, keepdims=True)
        qn = (cent * lax.rsqrt(var + 1e-05) * g_query).astype(BF16)
        qh_out[i] = dot(wq_v, qn, ((1,), (1,))) * HEAD_DIM ** (-0.5)
        do_out[i] = dot(wao_v, cot[i], ((1,), (1,)))
        gate_out[i] = jax.nn.sigmoid(dot(wg_t, ln_b[i]))
        return carry

    each_row(body)


def tri_kernel(lr, tri_out, mats_out):
    wide = lr[...].astype(F32)
    mats = [wide[:, 8 * q : 8 * q + 8, :].reshape(N, N).astype(BF16) for q in range(4)]
    for q in range(4):
        mats_out[q] = mats[q]
    parts = [dot(mats[cc], mats[2 + cc], ((1,), (1,))).reshape(SHARDS, 8, N) for cc in range(2)]
    tri_out[...] = jnp.concatenate(parts, axis=1).astype(BF16)


def heads_sum(x):
    return jnp.sum(x.reshape(HEADS, HEAD_DIM, N), axis=1)


def heads_spread(x):
    return jnp.broadcast_to(x[:, None, :], (HEADS, HEAD_DIM, N)).reshape(C, N)


def attend_kernel(
    tri, z, qh, do, gate, mask, mask_s, wo, tri_gain, pair_gain, wkv,
    sg_out, that_out, yhat_out, upd_out, kv_out, rstd_out, wide,
):
    t, start, mask_row = place(mask)
    unpack(tri, wide)
    wo_t = flip(wo[...]).astype(BF16)
    wkv_t = flip(wkv[...]).astype(BF16)
    g_tri, g_pair = column(tri_gain[...]), column(pair_gain[...])

    def body(i, carry):
        tri_i = jnp.concatenate([take_rows(wide, i, 16), take_rows(wide, 8 + i, 16)], axis=0)
        that, rstd_t = hat(tri_i)
        upd = dot(wo_t, (that * g_tri).astype(BF16))
        yhat, rstd_y = hat(z[i] + gate[i] * upd)
        kv = dot(wkv_t, (yhat * g_pair).astype(BF16)).astype(BF16)
        kv_f = kv.astype(F32)
        pm = mask_row * mask_s[t, start + i].astype(F32)
        score = heads_sum(qh[i] * kv_f[:C]) * pm + (pm - 1.0) * 1000000000.0
        dot_v = heads_sum(do[i] * kv_f[C:])
        sg_out[i] = jnp.concatenate([score, dot_v], axis=0)
        that_out[i] = that
        yhat_out[i] = yhat
        upd_out[i] = upd
        kv_out[i] = kv
        rstd_out[i] = jnp.concatenate([jnp.broadcast_to(rstd_t, (4, N)), jnp.broadcast_to(rstd_y, (4, N))], axis=0)
        return carry

    each_row(body)


def back_kernel(
    sg, that, yhat, gate, upd, qh, do, rstd, mask, mask_s, wo, tri_gain, pair_gain, wkv,
    dtri_out, ds_out, dy_out, spread,
):
    t, start, mask_row = place(mask)
    g_tri, g_pair = column(tri_gain[...]), column(pair_gain[...])
    wo_v, wkv_v = wo[...], wkv[...]

    def body(i, carry):
        pm = mask_row * mask_s[t, start + i].astype(F32)
        every = [sg[s, i] for s in range(4)]
        own = sg[t, i]
        top = jnp.maximum(jnp.maximum(every[0][:4], every[1][:4]), jnp.maximum(every[2][:4], every[3][:4]))
        expo = [jnp.exp(e[:4] - top) for e in every]
        inv = 1.0 / (expo[0] + expo[1] + expo[2] + expo[3])
        delta = sum(ex * e[4:] for ex, e in zip(expo, every)) * inv
        prob = jnp.exp(own[:4] - top) * inv
        ds_head = pm * prob * (own[4:] - delta)
        ds_out[i] = ds_head
        d_kv = jnp.concatenate([heads_spread(ds_head) * qh[i], heads_spread(prob) * do[i]], axis=0).astype(BF16)
        rs = rstd[i]
        d_y = hat_back(dot(wkv_v, d_kv) * g_pair, yhat[i], rs[4:5])
        dy_out[i] = d_y
        d_tn = dot(wo_v, (d_y * gate[i]).astype(BF16)) * g_tri
        d_tri = hat_back(d_tn, that[i], rs[0:1])
        put_rows(spread, i, 16, d_tri[:32])
        put_rows(spread, 8 + i, 16, d_tri[32:])
        return carry

    each_row(body)
    pack(spread, dtri_out)


def side_kernel(ds, kv, d_y, upd, gate, z, norm_gain, wg, dqh_out, base_out):
    g = column(norm_gain[...])
    wg_v = wg[...]

    def body(i, carry):
        dqh_out[i] = (heads_spread(ds[i]) * kv[i].astype(F32)[:C]).astype(BF16)
        gate_i, d_y_i = gate[i], d_y[i]
        d_gpre = d_y_i * upd[i] * gate_i * (1.0 - gate_i)
        zhat, rstd = hat(z[i])
        base_out[i] = d_y_i + hat_back(dot(wg_v, d_gpre.astype(BF16)) * g, zhat, rstd)
        return carry

    each_row(body)


def tri_back_kernel(dtri, mats, out):
    wide = dtri[...].astype(F32)
    d = [wide[:, 8 * cc : 8 * cc + 8, :].reshape(N, N).astype(BF16) for cc in range(2)]
    parts = [dot(d[cc], mats[2 + cc]) for cc in range(2)]
    parts += [dot(d[cc], mats[cc], ((0,), (0,))) for cc in range(2)]
    out[...] = jnp.concatenate([p.reshape(SHARDS, 8, N) for p in parts], axis=1).astype(BF16)


def weight_kernel(dlr, ln_b, mask, mask_s, proj_out, d_out, wide):
    t, start, mask_row = place(mask)
    unpack(dlr, wide)

    def body(i, total):
        pm = mask_row * mask_s[t, start + i].astype(F32)
        parts = [take_rows(wide, 8 * q + i, 32) for q in range(4)]
        d = (jnp.concatenate(parts, axis=0) * pm).astype(BF16)
        d_out[i] = d
        return total + dot(ln_b[i], d, ((1,), (1,)))

    proj_out[...] = each_row(body, jnp.zeros((C, 2 * C), F32))


def pair_grad_kernel(d, z, base, norm_gain, wl, wr, grad_out):
    g = column(norm_gain[...])
    weight = jnp.concatenate([wl[...], wr[...]], axis=1)

    def body(i, carry):
        zhat, rstd = hat(z[i])
        grad_out[i] = base[i] + hat_back(dot(weight, d[i]) * g, zhat, rstd)
        return carry

    each_row(body)


def query_grad_kernel(query, dqh, dqh_far, gain, wq_t, out):
    g = gain[...] * HEAD_DIM ** (-0.5)
    wq_v = wq_t[...]

    def body(i, carry):
        x = query[i].astype(F32)
        cent = x - jnp.mean(x, -1, keepdims=True)
        var = jnp.mean(cent * cent, -1, keepdims=True)
        rstd = lax.rsqrt(var + 1e-05)
        xhat = cent * rstd
        both = (dqh[i].astype(F32) + dqh_far[i].astype(F32)).astype(BF16)
        dy = dot(both, wq_v, ((0,), (0,))) * g
        out[i] = rstd * (dy - jnp.mean(dy, -1, keepdims=True) - xhat * jnp.mean(dy * xhat, -1, keepdims=True))
        return carry

    each_row(body)


def sum_kernel(parts, out):
    total = jnp.sum(parts[...].astype(F32), axis=0)
    out[0] = total[:, :C]
    out[1] = total[:, C:]


def call(kernel, outs, specs, scratch=(), us=3):
    return pl.pallas_call(
        kernel,
        out_shape=[jax.ShapeDtypeStruct(s, d) for s, d in outs],
        in_specs=specs,
        out_specs=[VMEM] * len(outs),
        scratch_shapes=[pltpu.VMEM(s, F32) for s in scratch],
        compiler_params=pltpu.CompilerParams(vmem_limit_bytes=40 * 1024 * 1024),
        cost_estimate=pl.CostEstimate(flops=us * 10**9, bytes_accessed=us * 3 * 10**6, transcendentals=0),
    )


def swap(x, bit):
    return lax.ppermute(x, "tmpl", [(i, i ^ bit) for i in range(4)])


def after(x, *others):
    return lax.optimization_barrier((x, *others))


def local(
    template_pair, template_mask, residue_index, query_pair, relpos_table, norm_gain, left_weight, right_weight,
    gate_weight, out_weight, tri_gain, pair_gain, kv_weight, query_gain, query_weight, attn_out_weight, cotangent,
):
    pair = jnp.swapaxes(template_pair[0], 1, 2)
    row = lambda x: x.reshape(1, -1)
    every = functools.partial(lax.all_to_all, axis_name="row", split_axis=0, concat_axis=0, tiled=True)
    plane, half = (ROWS, C, N), (ROWS, 2 * C, N)
    masks = (template_mask, template_mask)
    lr, z, ln_b = call(
        project_kernel,
        [((SHARDS, 32, N), BF16), (plane, F32), (plane, BF16)],
        [VMEM, VMEM, SMEM, VMEM, SMEM] + [VMEM] * 4,
        [(2, SHARDS * 32, 128)],
    )(
        pair, *masks, row(residue_index), residue_index, relpos_table.T, row(norm_gain), left_weight, right_weight,
    )
    lr_all = every(lr)
    qh, do, gate = call(query_kernel, [(plane, F32)] * 3, [VMEM] * 7)(
        query_pair, cotangent, ln_b, gate_weight, row(query_gain), query_weight.T, attn_out_weight
    )
    lr_all, qh, do, gate = after(lr_all, qh, do, gate)
    tri, mats = call(tri_kernel, [((SHARDS, 16, N), BF16), ((4, N, N), BF16)], [VMEM], us=1)(lr_all)
    tri = every(tri)
    sg, that, yhat, upd, kv, rstd = call(
        attend_kernel,
        [((ROWS, 8, N), F32)] + [(plane, F32)] * 3 + [(half, BF16), ((ROWS, 8, N), F32)],
        [VMEM] * 6 + [SMEM] + [VMEM] * 4,
        [(2, SHARDS * 16, 128)],
    )(tri, z, qh, do, gate, *masks, out_weight, row(tri_gain), row(pair_gain), kv_weight)
    sg = lax.all_gather(sg, "tmpl")
    dtri, ds, d_y = call(
        back_kernel,
        [((SHARDS, 16, N), BF16), ((ROWS, HEADS, N), F32), (plane, F32)],
        [VMEM] * 9 + [SMEM] + [VMEM] * 4,
        [(2, SHARDS * 16, 128)],
    )(sg, that, yhat, gate, upd, qh, do, rstd, *masks, out_weight, row(tri_gain), row(pair_gain), kv_weight)
    dtri = every(dtri)
    dqh, base = call(side_kernel, [(plane, BF16), (plane, F32)], [VMEM] * 8)(
        ds, kv, d_y, upd, gate, z, row(norm_gain), gate_weight
    )
    dqh = dqh + swap(dqh, 1)
    dtri, dqh, base = after(dtri, dqh, base)
    (dlr,) = call(tri_back_kernel, [((SHARDS, 32, N), BF16)], [VMEM, VMEM], us=1)(dtri, mats)
    dlr = every(dlr)
    dqh_far = swap(dqh, 2)
    dlr, dqh_far = after(dlr, dqh_far)
    proj, d = call(
        weight_kernel,
        [((C, 2 * C), F32), (half, BF16)],
        [VMEM] * 3 + [SMEM],
        [(2, SHARDS * 32, 128)],
    )(dlr, ln_b, *masks)
    near = swap(proj, 1)
    (grad,) = call(pair_grad_kernel, [(plane, F32)], [VMEM] * 6)(d, z, base, row(norm_gain), left_weight, right_weight)
    proj = proj + near
    proj = (proj + swap(proj, 2)).astype(BF16)
    parts = every(jnp.broadcast_to(proj[None], (SHARDS, C, 2 * C)))
    (query_grad,) = call(query_grad_kernel, [((ROWS, N, 2 * C), F32)], [VMEM] * 5)(
        query_pair, dqh, dqh_far, row(query_gain), query_weight.T
    )
    parts, query_grad = after(parts, query_grad)
    (proj,) = call(sum_kernel, [((2, C, C), F32)], [VMEM], us=1)(parts)
    return jnp.swapaxes(grad, 1, 2)[None], query_grad, proj


def solution(mesh):
    in_specs = (
        P("tmpl", "row", None, None),
        P(),
        P(),
        P("row", None, None),
        *([P()] * 12),
        P("row", None, None),
    )
    out_specs = (P("tmpl", "row", None, None), P("row", None, None), P())
    return jax.shard_map(local, mesh=mesh, in_specs=in_specs, out_specs=out_specs, check_vma=False)
```

time: 133 us -> 119 us (0.89)
  blocking collectives: 55.6 us -> 21.2 us
  starting transfers between devices: 15.6 us -> 29.8 us
  waiting for transfers between devices: 30.1 us -> 40.5 us
  Pallas kernels: 21.3 us -> 18.3 us
  other arithmetic: 2.08 us -> 0.08 us
  local copies, waits for them, and re-layouts: 5.82 us -> 7.6 us
    all_to_all x3 -> x1, blocking collectives: 47.8 us -> 13.3 us  [local(): tri = every(tri)]
    all_to_all x2 -> x4, waiting for transfers between devices: 9.07 us -> 25 us  [the longest x1 9.74 us: local(): dtri = every(dtri)]
    all_to_all x2 -> x4, starting transfers between devices: 8.86 us -> 24 us  [the longest x1 8.89 us: local(): lr_all = every(lr)]
    ppermute x4, waiting for transfers between devices: 21 us -> 15.5 us  [swap(): return lax.ppermute(x, 'tmpl', [(i, i ^ bit) for i in range(4)])]
    pallas_call x7 -> x11, Pallas kernels: 21.3 us -> 18.3 us  [the longest x1 3.36 us: local(): call(project_kernel, [((SHARDS, 32, N), BF16), (plane, F32), (plane, BF16...]
    unnamed x34 -> x48, local copies, waits for them, and re-layouts: 4.66 us -> 6.64 us
  transfers between devices with their start and end apart: 6 -> 8, of which waited for: 5 -> 6; matrix products, arithmetic and copies ran while one was open for 1% -> 0% of each run, Pallas kernels for 3% -> 5%
where the time goes in v2:
time: 119 us; the launch traced here: 118 us
  waiting for transfers between devices  40.5 us (34%)
  starting transfers between devices  29.8 us (25%)
  blocking collectives  21.2 us (18%)
  Pallas kernels  18.3 us (15%)
  local copies, waits for them, and re-layouts  7.6 us (6%)
    ppermute x4, waiting for transfers between devices, swap(): return lax.ppermute(x, 'tmpl', [(i, i ^ bit) for i in range(4)])  15.5 us
    all_to_all x1, blocking collectives, local(): tri = every(tri)  13.3 us
    all_to_all x1, waiting for transfers between devices, local(): dtri = every(dtri)  9.74 us
    all_to_all x1, starting transfers between devices, local(): lr_all = every(lr)  8.89 us
    all_to_all x1, waiting for transfers between devices, local(): lr_all = every(lr)  8.84 us
    all_gather x1, blocking collectives, local(): sg = lax.all_gather(sg, 'tmpl')  7.84 us
    all_to_all x1, starting transfers between devices, local(): parts = every(jnp.broadcast_to(proj[None], (SHARDS, C, 2 * C)))  7.36 us
    unnamed x48, local copies, waits for them, and re-layouts  6.64 us
  transfers between devices with their start and end apart: 8, of which 6 were waited for; matrix products, arithmetic and copies ran while one was open for 0% of the time, Pallas kernels for 5%

profile of v2, /device:TPU:0, one launch (start us, length us, event | category | flops | bytes accessed | tf_op | source)
XLA Modules:
  0.0 118.3 jit_solution(1886324210471265806)
XLA Ops:
  0.7 0.7 copy-done.13
  1.3 0.0 copy-done.14
  1.3 0.9 copy-done.2
  2.3 0.7 copy-done.3
  3.0 0.7 copy-done.9
  3.7 0.7 copy-done.11
  4.4 3.4 %shard_map.184 = (bf16[32,32,256]{2,1,0:T(8,128)(2,1)}, f32[8,64,256]{2,1,0:T(8,128)S(1)}, bf16[8,64,256]{2,1,0:T(8,128)(2,1)S(1)}) custom-call(bf16[8,64,256]{2,1,0:T(8,128)(2,1)S(1)} %bitcast.15, s32[4,256]{1,0:T(4,128)S(1)} %copy-done.13, s32[4,256]{1,0:T(4,128)S(1)} %copy-done.13, s32[1,256]{1,0:T(1,128)S(1)} %bitcast.19, s32[256]{0:T(256)S(1)} %copy-done.14, ...), custom_call_target="tpu_custom_call" | custom-call | flops 3000000000 | bytes 9000000 | tf_op jit(solution)/shard_map/pallas_call | solution.py:309
  7.8 0.8 copy-done.21
  8.6 8.9 %all-to-all-start = ((bf16[32,32,256]{2,1,0:T(8,128)(2,1)}), bf16[32,32,256]{2,1,0:T(8,128)(2,1)S(1)}, u32[]{:S(2)}, u32[]{:S(2)}) async-start(bf16[32,32,256]{2,1,0:T(8,128)(2,1)} %get-tuple-element.35), calls=%async_computation | async-start | bytes 1048576 | tf_op jit(solution)/shard_map/all_to_all | solution.py:317
  17.5 0.0 copy-start.17
  17.5 0.6 copy-done.17
  18.1 1.3 %shard_map.185 = (f32[8,64,256]{2,1,0:T(8,128)S(1)}, f32[8,64,256]{2,1,0:T(8,128)S(1)}, f32[8,64,256]{2,1,0:T(8,128)S(1)}) custom-call(bf16[8,256,128]{2,1,0:T(8,128)(2,1)S(1)} %copy-done.1, bf16[8,256,128]{2,1,0:T(8,128)(2,1)S(1)} %copy-done, bf16[8,64,256]{2,1,0:T(8,128)(2,1)S(1)} %get-tuple-element.36.ln_b, bf16[64,64]{1,0:T(8,128)(2,1)S(1)} %copy-done.7, ...), custom_call_target="tpu_custom_call" | custom-call | flops 3000000000 | bytes 9000000 | tf_op jit(solution)/shard_map/pallas_call | solution.py:318
  19.4 0.0 copy-start.19
  19.4 0.8 copy-done.19
  20.2 8.8 %all-to-all-done.lr = bf16[32,32,256]{2,1,0:T(8,128)(2,1)S(1)} async-done(((bf16[32,32,256]{2,1,0:T(8,128)(2,1)}), bf16[32,32,256]{2,1,0:T(8,128)(2,1)S(1)}, u32[]{:S(2)}, u32[]{:S(2)}) %all-to-all-start) | async-done | bytes 524320 | tf_op jit(solution)/shard_map/all_to_all | solution.py:317
  29.1 0.3 shard_map.186
  29.4 0.0 copy-start.5
  29.4 0.0 copy-start.6
  29.4 13.3 %all_to_all.25.tri = bf16[32,16,256]{2,1,0:T(8,128)(2,1)S(1)} all-to-all(bf16[32,16,256]{2,1,0:T(8,128)(2,1)S(1)} %get-tuple-element.41), channel_id=1, replica_groups=mesh['tmpl'=4,'row'=32] {'row'}, dimensions={0} | all-to-all | bytes 524288 | tf_op jit(solution)/shard_map/all_to_all | solution.py:323
  42.8 0.6 copy-done.15
  43.4 0.0 copy-done.16
  43.4 2.1 %shard_map.187 = (f32[8,8,256]{2,1,0:T(8,128)S(1)}, f32[8,64,256]{2,1,0:T(8,128)S(1)}, f32[8,64,256]{2,1,0:T(8,128)S(1)}, f32[8,64,256]{2,1,0:T(8,128)S(1)}, bf1...) custom-call(bf16[32,16,256]{2,1,0:T(8,128)(2,1)S(1)} %all_to_all.25.tri, f32[8,64,256]{2,1,0:T(8,128)S(1)} %copy-done.22, ...), custom_call_target="tpu_custom_call" | custom-call | flops 3000000000 | bytes 9000000 | tf_op jit(solution)/shard_map/pallas_call | solution.py:324
  45.5 7.8 %all-gather = f32[32,8,256]{2,1,0:T(8,128)S(1)} all-gather(f32[8,8,256]{2,1,0:T(8,128)S(1)} %get-tuple-element.46), channel_id=2, replica_groups=mesh['tmpl'=4,'row'=32] {'tmpl'}, dimensions={0}, use_global_device_ids=true | all-gather | bytes 327680 | tf_op jit(solution)/shard_map/all_gather | solution.py:330
  53.4 2.8 %shard_map.188 = (bf16[32,16,256]{2,1,0:T(8,128)(2,1)}, f32[8,4,256]{2,1,0:T(4,128)S(1)}, f32[8,64,256]{2,1,0:T(8,128)S(1)}) custom-call(f32[4,8,8,256]{3,2,1,0:T(8,128)S(1)} %bitcast.14, f32[8,64,256]{2,1,0:T(8,128)S(1)} %get-tuple-element.47.that, f32[8,64,256]{2,1,0:T(8,128)S(1)} %get-tuple-element.48.yhat, f32[8,64,256]{2,1,0:T(8,128)S(1)} %get-tuple-element.45.gate, ...), custom_call_target="tpu_custom_call" | custom-call | flops 3000000000 | bytes 9000000 | tf_op jit(solution)/shard_map/pallas_call | solution.py:331
  56.2 0.7 shard_map.189
  56.9 0.4 collective-permute-start
  57.3 3.9 %all-to-all-start.2 = ((bf16[32,16,256]{2,1,0:T(8,128)(2,1)}), bf16[32,16,256]{2,1,0:T(8,128)(2,1)S(1)}, u32[]{:S(2)}, u32[]{:S(2)}) async-start(bf16[32,16,256]{2,1,0:T(8,128)(2,1)} %get-tuple-element.51), calls=%async_computation.2 | async-start | bytes 524288 | tf_op jit(solution)/shard_map/all_to_all | solution.py:337
  61.2 0.0 collective-permute-done
  61.2 0.1 add.9.dqh
  61.3 9.7 %all-to-all-done.2.dtri = bf16[32,16,256]{2,1,0:T(8,128)(2,1)S(1)} async-done(((bf16[32,16,256]{2,1,0:T(8,128)(2,1)}), bf16[32,16,256]{2,1,0:T(8,128)(2,1)S(1)}, u32[]{:S(2)}, u32[]{:S(2)}) %all-to-all-start.2) | async-done | bytes 262176 | tf_op jit(solution)/shard_map/all_to_all | solution.py:337
  71.0 1.1 shard_map.190
  72.1 3.9 %all-to-all-start.3 = ((bf16[32,32,256]{2,1,0:T(8,128)(2,1)}), bf16[32,32,256]{2,1,0:T(8,128)(2,1)S(1)}, u32[]{:S(2)}, u32[]{:S(2)}) async-start(bf16[32,32,256]{2,1,0:T(8,128)(2,1)} %shard_map.190), calls=%async_computation.3 | async-start | bytes 1048576 | tf_op jit(solution)/shard_map/all_to_all | solution.py:344
  76.0 3.1 %collective-permute-start.1 = (bf16[8,64,256]{2,1,0:T(8,128)(2,1)S(1)}, bf16[8,64,256]{2,1,0:T(8,128)(2,1)S(1)}, u32[]{:S(2)}, u32[]{:S(2)}) collective-permute-start(bf16[8,64,256]{2,1,0:T(8,128)(2,1)S(1)} %add.9.dqh), channel_id=1, source_target_pairs={{0,64},{32,96},{64,0},{96,32},{1,65},{33,97},{65,1},{97,33},{2,66}... | collective-permute-start | bytes 786440 | tf_op jit(solution)/shard_map/ppermute | solution.py:293
  79.1 11.0 %collective-permute-done.1.dqh_far = bf16[8,64,256]{2,1,0:T(8,128)(2,1)S(1)} collective-permute-done((bf16[8,64,256]{2,1,0:T(8,128)(2,1)S(1)}, bf16[8,64,256]{2,1,0:T(8,128)(2,1)S(1)}, u32[]{:S(2)}, u32[]{:S(2)}) %collective-permute-start.1) | collective-permute-done | bytes 262176 | tf_op jit(solution)/shard_map/ppermute | solution.py:293
  90.2 0.0 all-to-all-done.3.dlr
  90.2 1.5 %shard_map.191 = (f32[64,128]{1,0:T(8,128)S(1)}, bf16[8,128,256]{2,1,0:T(8,128)(2,1)S(1)}) custom-call(bf16[32,32,256]{2,1,0:T(8,128)(2,1)S(1)} %all-to-all-done.3.dlr, bf16[8,64,256]{2,1,0:T(8,128)(2,1)S(1)} %get-tuple-element.36.ln_b, s32[4,256]{1,0:T(4,128)S(1)} %copy-done.13, s32[4,256]{1,0:T(4,128)S(1)} %copy-done.13), custom_call_target="tpu_custom_call" | custom-call | flops 3000000000 | bytes 9000000 | tf_op jit(solution)/shard_map/pallas_call | solution.py:347
  91.7 0.1 collective-permute-start.2
  91.8 1.2 %collective-permute-done.2 = f32[64,128]{1,0:T(8,128)S(1)} collective-permute-done((f32[64,128]{1,0:T(8,128)S(1)}, f32[64,128]{1,0:T(8,128)S(1)}, u32[]{:S(2)}, u32[]{:S(2)}) %collective-permute-start.2) | collective-permute-done | bytes 32800 | tf_op jit(solution)/shard_map/ppermute | solution.py:293
  93.0 2.2 %collective-permute-start.3 = (f32[64,128]{1,0:T(8,128)S(1)}, f32[64,128]{1,0:T(8,128)S(1)}, u32[]{:S(2)}, u32[]{:S(2)}) collective-permute-start(f32[64,128]{1,0:T(8,128)S(1)} %add.10), channel_id=1, source_target_pairs={{0,64},{32,96},{64,0},{96,32},{1,65},{33,97},{65,1},{97,33},{2,66}... | collective-permute-start | bytes 98312 | tf_op jit(solution)/shard_map/ppermute | solution.py:293
  95.2 3.3 %collective-permute-done.3 = f32[64,128]{1,0:T(8,128)S(1)} collective-permute-done((f32[64,128]{1,0:T(8,128)S(1)}, f32[64,128]{1,0:T(8,128)S(1)}, u32[]{:S(2)}, u32[]{:S(2)}) %collective-permute-start.3) | collective-permute-done | bytes 32800 | tf_op jit(solution)/shard_map/ppermute | solution.py:293
  98.4 1.0 broadcast_in_dim.10
  99.4 7.4 %all-to-all-start.4 = ((bf16[32,64,128]{2,1,0:T(8,128)(2,1)}), bf16[32,64,128]{2,1,0:T(8,128)(2,1)S(1)}, u32[]{:S(2)}, u32[]{:S(2)}) async-start(bf16[32,64,128]{2,1,0:T(8,128)(2,1)} %broadcast_in_dim.10), calls=%async_computation.4 | async-start | bytes 1048576 | tf_op jit(solution)/shard_map/all_to_all | solution.py:357
  106.8 0.0 copy-start.10
  106.8 0.0 copy-start.12
  106.8 2.9 %shard_map.193 = f32[8,256,128]{2,1,0:T(8,128)} custom-call(bf16[8,256,128]{2,1,0:T(8,128)(2,1)S(1)} %copy-done.1, bf16[8,64,256]{2,1,0:T(8,128)(2,1)S(1)} %add.9.dqh, bf16[8,64,256]{2,1,0:T(8,128)(2,1)S(1)} %collective-permute-done.1.dqh_far, f32[1,128]{1,0:T(1,128)S(1)} %bitcast.25, bf16[64,128]{1,0:T(8,128)(2,1)S(1)} %bitcast.18), custom_call_target="tpu_custom_call" | custom-call | flops 3000000000 | bytes 9000000 | tf_op jit(solution)/shard_map/pallas_call | solution.py:358
  109.7 1.4 %shard_map.192 = f32[8,64,256]{2,1,0:T(8,128)} custom-call(bf16[8,128,256]{2,1,0:T(8,128)(2,1)S(1)} %get-tuple-element.61.d, f32[8,64,256]{2,1,0:T(8,128)S(1)} %copy-done.23, f32[8,64,256]{2,1,0:T(8,128)S(1)} %get-tuple-element.62.base, f32[1,64]{1,0:T(1,128)S(1)} %bitcast.28, bf16[64,64]{1,0:T(8,128)(2,1)S(1)} %copy-done.10, bf16[64,64]{1,0:T(8,128)(2,1)S(1)} %copy-done.12), custom_call_target="tpu_custom_call" | custom-call | flops 3000000000 | bytes 9000000 | tf_op jit(solution)/shard_map/pallas_call | solution.py:354
  111.1 6.4 %all-to-all-done.4.parts = bf16[32,64,128]{2,1,0:T(8,128)(2,1)S(1)} async-done(((bf16[32,64,128]{2,1,0:T(8,128)(2,1)}), bf16[32,64,128]{2,1,0:T(8,128)(2,1)S(1)}, u32[]{:S(2)}, u32[]{:S(2)}) %all-to-all-start.4) | async-done | bytes 524320 | tf_op jit(solution)/shard_map/all_to_all | solution.py:357
  117.5 0.8 shard_map.194
  (33 shorter events, 0.1 us)
Async XLA Ops:
  0.6 0.7 copy-start.13
  0.6 0.7 copy-start.14
  0.7 0.7 copy-start.18
  1.3 1.0 copy-start.2
  2.3 0.7 copy-start.3
  3.0 0.7 copy-start.9
  3.7 0.7 copy-start.11
  4.4 13.1 %copy-start.4 = (bf16[64,128]{1,0:T(8,128)(2,1)S(1)}, bf16[64,128]{1,0:T(8,128)(2,1)}, u32[]{:S(2)}) copy-start(bf16[64,128]{1,0:T(8,128)(2,1)} %wao.1) | copy-start | bytes 49156
  4.4 13.1 %copy-start.7 = (bf16[64,64]{1,0:T(8,128)(2,1)S(1)}, bf16[64,64]{1,0:T(8,128)(2,1)}, u32[]{:S(2)}) copy-start(bf16[64,64]{1,0:T(8,128)(2,1)} %wg.3) | copy-start | bytes 24580
  4.4 13.1 %copy-start.8 = (bf16[128,64]{0,1:T(8,128)(2,1)S(1)}, bf16[128,64]{0,1:T(8,128)(2,1)}, u32[]{:S(2)}) copy-start(bf16[128,64]{0,1:T(8,128)(2,1)} %param.31) | copy-start | bytes 49156
  7.8 0.8 copy-start.21
  8.6 8.9 %copy-start = (bf16[8,256,128]{2,1,0:T(8,128)(2,1)S(1)}, bf16[8,256,128]{2,1,0:T(8,128)(2,1)}, u32[]{:S(2)}) copy-start(bf16[8,256,128]{2,1,0:T(8,128)(2,1)} %cot.1) | copy-start | bytes 1572868
  8.6 9.0 %copy-start.1 = (bf16[8,256,128]{2,1,0:T(8,128)(2,1)S(1)}, bf16[8,256,128]{2,1,0:T(8,128)(2,1)}, u32[]{:S(2)}) copy-start(bf16[8,256,128]{2,1,0:T(8,128)(2,1)} %query.3) | copy-start | bytes 1572868
  8.6 20.5 %all-to-all-start = ((bf16[32,32,256]{2,1,0:T(8,128)(2,1)}), bf16[32,32,256]{2,1,0:T(8,128)(2,1)S(1)}, u32[]{:S(2)}, u32[]{:S(2)}) async-start(bf16[32,32,256]{2,1,0:T(8,128)(2,1)} %get-tuple-element.35), calls=%async_computation | async-start | bytes 1048576 | tf_op jit(solution)/shard_map/all_to_all | solution.py:317
  17.5 0.7 copy-start.17
  19.4 0.8 copy-start.19
  29.1 13.6 %copy-start.20 = (f32[8,64,256]{2,1,0:T(8,128)S(1)}, f32[8,64,256]{2,1,0:T(8,128)}, u32[]{:S(2)}) copy-start(f32[8,64,256]{2,1,0:T(8,128)} %copy-done.19) | copy-start | bytes 1572868
  29.1 13.7 %copy-start.22 = (f32[8,64,256]{2,1,0:T(8,128)S(1)}, f32[8,64,256]{2,1,0:T(8,128)}, u32[]{:S(2)}) copy-start(f32[8,64,256]{2,1,0:T(8,128)} %copy-done.21) | copy-start | bytes 1572868
  29.4 13.4 %copy-start.5 = (bf16[64,64]{1,0:T(8,128)(2,1)S(1)}, bf16[64,64]{1,0:T(8,128)(2,1)}, u32[]{:S(2)}) copy-start(bf16[64,64]{1,0:T(8,128)(2,1)} %wo.3) | copy-start | bytes 24580
  29.4 13.4 %copy-start.6 = (bf16[64,128]{1,0:T(8,128)(2,1)S(1)}, bf16[64,128]{1,0:T(8,128)(2,1)}, u32[]{:S(2)}) copy-start(bf16[64,128]{1,0:T(8,128)(2,1)} %wkv.3) | copy-start | bytes 49156
  42.7 0.7 copy-start.15
  42.7 0.7 copy-start.16
  56.9 4.3 %collective-permute-start = (bf16[8,64,256]{2,1,0:T(8,128)(2,1)S(1)}, bf16[8,64,256]{2,1,0:T(8,128)(2,1)S(1)}, u32[]{:S(2)}, u32[]{:S(2)}) collective-permute-start(bf16[8,64,256]{2,1,0:T(8,128)(2,1)S(1)} %get-tuple-element.55), channel_id=1, source_target_pairs={{0,32},{32,0},{64,96},{96,64},{1,33},{33,1},{65,97},{97,65},{2,34}... | collective-permute-start | bytes 786440 | tf_op jit(solution)/shard_map/ppermute | solution.py:293
  57.3 13.7 %all-to-all-start.2 = ((bf16[32,16,256]{2,1,0:T(8,128)(2,1)}), bf16[32,16,256]{2,1,0:T(8,128)(2,1)S(1)}, u32[]{:S(2)}, u32[]{:S(2)}) async-start(bf16[32,16,256]{2,1,0:T(8,128)(2,1)} %get-tuple-element.51), calls=%async_computation.2 | async-start | bytes 524288 | tf_op jit(solution)/shard_map/all_to_all | solution.py:337
  72.1 18.1 %all-to-all-start.3 = ((bf16[32,32,256]{2,1,0:T(8,128)(2,1)}), bf16[32,32,256]{2,1,0:T(8,128)(2,1)S(1)}, u32[]{:S(2)}, u32[]{:S(2)}) async-start(bf16[32,32,256]{2,1,0:T(8,128)(2,1)} %shard_map.190), calls=%async_computation.3 | async-start | bytes 1048576 | tf_op jit(solution)/shard_map/all_to_all | solution.py:344
  76.0 14.2 %collective-permute-start.1 = (bf16[8,64,256]{2,1,0:T(8,128)(2,1)S(1)}, bf16[8,64,256]{2,1,0:T(8,128)(2,1)S(1)}, u32[]{:S(2)}, u32[]{:S(2)}) collective-permute-start(bf16[8,64,256]{2,1,0:T(8,128)(2,1)S(1)} %add.9.dqh), channel_id=1, source_target_pairs={{0,64},{32,96},{64,0},{96,32},{1,65},{33,97},{65,1},{97,33},{2,66}... | collective-permute-start | bytes 786440 | tf_op jit(solution)/shard_map/ppermute | solution.py:293
  91.7 1.3 %collective-permute-start.2 = (f32[64,128]{1,0:T(8,128)S(1)}, f32[64,128]{1,0:T(8,128)S(1)}, u32[]{:S(2)}, u32[]{:S(2)}) collective-permute-start(f32[64,128]{1,0:T(8,128)S(1)} %get-tuple-element.63), channel_id=1, source_target_pairs={{0,32},{32,0},{64,96},{96,64},{1,33},{33,1},{65,97},{97,65},{2,34}... | collective-permute-start | bytes 98312 | tf_op jit(solution)/shard_map/ppermute | solution.py:293
  93.0 5.4 %collective-permute-start.3 = (f32[64,128]{1,0:T(8,128)S(1)}, f32[64,128]{1,0:T(8,128)S(1)}, u32[]{:S(2)}, u32[]{:S(2)}) collective-permute-start(f32[64,128]{1,0:T(8,128)S(1)} %add.10), channel_id=1, source_target_pairs={{0,64},{32,96},{64,0},{96,32},{1,65},{33,97},{65,1},{97,33},{2,66}... | collective-permute-start | bytes 98312 | tf_op jit(solution)/shard_map/ppermute | solution.py:293
  99.4 18.1 %all-to-all-start.4 = ((bf16[32,64,128]{2,1,0:T(8,128)(2,1)}), bf16[32,64,128]{2,1,0:T(8,128)(2,1)S(1)}, u32[]{:S(2)}, u32[]{:S(2)}) async-start(bf16[32,64,128]{2,1,0:T(8,128)(2,1)} %broadcast_in_dim.10), calls=%async_computation.4 | async-start | bytes 1048576 | tf_op jit(solution)/shard_map/all_to_all | solution.py:357
  106.8 3.0 %copy-start.10 = (bf16[64,64]{1,0:T(8,128)(2,1)S(1)}, bf16[64,64]{1,0:T(8,128)(2,1)}, u32[]{:S(2)}) copy-start(bf16[64,64]{1,0:T(8,128)(2,1)} %wl.3) | copy-start | bytes 24580
  106.8 3.0 %copy-start.12 = (bf16[64,64]{1,0:T(8,128)(2,1)S(1)}, bf16[64,64]{1,0:T(8,128)(2,1)}, u32[]{:S(2)}) copy-start(bf16[64,64]{1,0:T(8,128)(2,1)} %wr.3) | copy-start | bytes 24580
  106.8 2.9 %copy-start.23 = (f32[8,64,256]{2,1,0:T(8,128)S(1)}, f32[8,64,256]{2,1,0:T(8,128)}, u32[]{:S(2)}) copy-start(f32[8,64,256]{2,1,0:T(8,128)} %copy-done.21) | copy-start | bytes 1572868

commit v3 on v2

v3 whole, which is shorter than its diff:
```python
import functools

import jax
import jax.numpy as jnp
from jax import lax
from jax.experimental import pallas as pl
from jax.experimental.pallas import tpu as pltpu
from jax.sharding import PartitionSpec as P

F32 = jnp.float32
BF16 = jnp.bfloat16
HEADS = 4
HEAD_DIM = 16
C = 64
ROWS = 8
N = 256
SHARDS = 32
UNROLL = 4
HALF = ROWS // 2
ANY = pl.BlockSpec(memory_space=pltpu.HBM)
VMEM = pl.BlockSpec(memory_space=pltpu.VMEM)


def dot(a, b, contract=((1,), (0,))):
    return lax.dot_general(a, b, (contract, ((), ())), preferred_element_type=F32)


def flip(x):
    return x.astype(F32).T


def column(row):
    return jnp.broadcast_to(row, (128, row.shape[1])).T


def twice(x):
    return jnp.concatenate([x, x], axis=1)


def slab(weights, n, width=C):
    return weights[:, 128 * n : 128 * n + width]


def hat(x):
    mean = jnp.mean(x, 0, keepdims=True)
    cent = x - mean
    var = jnp.mean(cent * cent, 0, keepdims=True)
    rstd = lax.rsqrt(var + 1e-05)
    return cent * rstd, rstd


def hat_back(dy, xhat, rstd):
    return rstd * (dy - jnp.mean(dy, 0, keepdims=True) - xhat * jnp.mean(dy * xhat, 0, keepdims=True))


def put_rows(spread, first, step, x):
    for half in range(2):
        spread[half, pl.ds(first, x.shape[0], stride=step), :] = x[:, 128 * half : 128 * half + 128]


def take_rows(wide, first, step):
    return jnp.concatenate([wide[half, pl.ds(first, SHARDS, stride=step), :] for half in range(2)], axis=1)


def pack(spread, out):
    for half in range(2):
        out[:, :, 128 * half : 128 * half + 128] = spread[half].reshape(out.shape[0], out.shape[1], 128).astype(BF16)


def unpack(x, wide):
    for half in range(2):
        wide[half] = x[:, :, 128 * half : 128 * half + 128].astype(F32).reshape(wide.shape[1], 128)


def place(rows_ref):
    t = lax.axis_index("tmpl")
    start = lax.axis_index("row") * ROWS
    mask_row = rows_ref[pl.ds(t, 1), :].astype(F32)
    return t, start, mask_row


def each_row(body, carry=0, rows=ROWS, unroll=UNROLL):
    def step(s, carry):
        for u in range(unroll):
            carry = body(s * unroll + u, carry)
        return carry

    if unroll == rows:
        return step(0, carry)
    return lax.fori_loop(0, rows // unroll, step, carry)


def fetch(sources, places, sems):
    copies = [pltpu.make_async_copy(src, dst, sems.at[n]) for n, (src, dst) in enumerate(zip(sources, places))]
    for copy in copies:
        copy.start()
    for copy in copies:
        copy.wait()


def relative(res_s, residues, table, at):
    bins = lax.broadcasted_iota(jnp.int32, (128, N), 0)
    offset = jnp.clip(res_s[at] - residues, -64, 63) + 64
    return dot(table, jnp.where(bins == offset, 1.0, 0.0).astype(BF16))


def project_kernel(*refs):
    sources, outs, (spread, sems), places = refs[:14], refs[14:19], refs[19:21], refs[21:]
    lr_out, z_out, pm_out, weights_out, gains_out = outs
    fetch(sources, places, sems)
    pair, res, res_s, table_t, mask, mask_s, wl, wr, wg, wo, wkv, norm_gain, tri_gain, pair_gain = places
    t, start, mask_row = place(mask)
    weight = jnp.concatenate([flip(wl[...]), flip(wr[...])], axis=0).astype(BF16)
    table, residues, gain = table_t[...], res[...], column(norm_gain[...])
    g = twice(gain)

    def body(i, carry):
        z = pair[i].astype(F32) + relative(res_s, residues, table, start + i)
        z_out[i] = z
        pm = mask_row * mask_s[t, start + i].astype(F32)
        pm_out[i] = pm
        both = dot(weight, (hat(z)[0] * g).astype(BF16)) * pm
        for q in range(4):
            put_rows(spread, 8 * q + i, 32, both[32 * q : 32 * q + 32])
        return carry

    each_row(body)
    pack(spread, lr_out)
    blank = jnp.zeros((C, C), BF16)
    wkv_t = flip(wkv[...]).astype(BF16)
    parts = [wkv[...], wl[...], wr[...], flip(wo[...]).astype(BF16), blank, wo[...], blank, wg[...], blank]
    parts += [wkv_t[:C], blank, wkv_t[C:], blank, flip(wg[...]).astype(BF16), blank]
    weights_out[...] = jnp.concatenate(parts, axis=1)
    gains_out[0] = gain
    gains_out[1] = column(tri_gain[...])
    gains_out[2] = column(pair_gain[...])


def prepare_kernel(z, weights, gains, query, cot, q_gain, wq_t, wao, ln_out, qh_out, do_out, gate_out):
    wg_t, g = slab(weights, 7), twice(gains[0])
    wq_v, wao_v, g_query = wq_t[...], wao[...], q_gain[...]

    def body(i, carry):
        ln_b = (hat(z[i])[0] * g).astype(BF16)
        ln_out[i] = ln_b
        x = query[i].astype(F32)
        cent = x - jnp.mean(x, -1, keepdims=True)
        var = jnp.mean(cent * cent, -1, keepdims=True)
        qn = (cent * lax.rsqrt(var + 1e-05) * g_query).astype(BF16)
        qh_out[i] = dot(wq_v, qn, ((1,), (1,))) * HEAD_DIM ** (-0.5)
        do_out[i] = dot(wao_v, cot[i], ((1,), (1,)))
        gate_out[i] = jax.nn.sigmoid(dot(wg_t, ln_b))
        return carry

    each_row(body)


def tri_kernel(lr, tri_out, mats_out):
    wide = lr[...].astype(F32)
    mats = [wide[:, 8 * q : 8 * q + 8, :].reshape(N, N).astype(BF16) for q in range(4)]
    for q in range(4):
        mats_out[q] = mats[q]
    parts = [dot(mats[cc], mats[2 + cc], ((1,), (1,))).reshape(SHARDS, 8, N) for cc in range(2)]
    tri_out[...] = jnp.concatenate(parts, axis=1).astype(BF16)


def heads_sum(x):
    return jnp.sum(x.reshape(HEADS, HEAD_DIM, N), axis=1)


def heads_spread(x):
    return jnp.broadcast_to(x[:, None, :], (HEADS, HEAD_DIM, N)).reshape(C, N)


def attend_kernel(
    tri, z, qh, do, gate, pm, weights, gains, sg_out, that_out, yhat_out, upd_out, kv_out, rstd_out, wide
):
    unpack(tri, wide)
    wo_t = slab(weights, 2)
    wkv_t = jnp.concatenate([slab(weights, 5), slab(weights, 6)], axis=0)
    g_tri, g_pair = twice(gains[1]), twice(gains[2])

    def body(i, carry):
        tri_i = jnp.concatenate([take_rows(wide, i, 16), take_rows(wide, 8 + i, 16)], axis=0)
        that, rstd_t = hat(tri_i)
        upd = dot(wo_t, (that * g_tri).astype(BF16))
        yhat, rstd_y = hat(z[i] + gate[i] * upd)
        kv = dot(wkv_t, (yhat * g_pair).astype(BF16)).astype(BF16)
        kv_f = kv.astype(F32)
        score = heads_sum(qh[i] * kv_f[:C]) * pm[i] + (pm[i] - 1.0) * 1000000000.0
        dot_v = heads_sum(do[i] * kv_f[C:])
        sg_out[i] = jnp.concatenate([score, dot_v], axis=0)
        that_out[i] = that
        yhat_out[i] = yhat
        upd_out[i] = upd
        kv_out[i] = kv
        rstd_out[i] = jnp.concatenate([jnp.broadcast_to(rstd_t, (4, N)), jnp.broadcast_to(rstd_y, (4, N))], axis=0)
        return carry

    each_row(body)


def back_kernel(
    sg, that, yhat, gate, upd, qh, do, kv, rstd, pm, z, weights, gains,
    dtri_out, keep_out, send_out, base_out, spread,
):
    t = lax.axis_index("tmpl")
    core = t % 2
    g_norm, g_tri, g_pair = twice(gains[0]), twice(gains[1]), twice(gains[2])
    wkv_v, wo_v, wg_v = slab(weights, 0, 2 * C), slab(weights, 3), slab(weights, 4)

    def row(i, dqh_out, n):
        every = [sg[s, i] for s in range(4)]
        own = sg[t, i]
        top = jnp.maximum(jnp.maximum(every[0][:4], every[1][:4]), jnp.maximum(every[2][:4], every[3][:4]))
        expo = [jnp.exp(e[:4] - top) for e in every]
        inv = 1.0 / (expo[0] + expo[1] + expo[2] + expo[3])
        delta = sum(ex * e[4:] for ex, e in zip(expo, every)) * inv
        prob = jnp.exp(own[:4] - top) * inv
        ds = heads_spread(pm[i] * prob * (own[4:] - delta))
        dqh_out[n] = (ds * kv[i].astype(F32)[:C]).astype(BF16)
        d_kv = jnp.concatenate([ds * qh[i], heads_spread(prob) * do[i]], axis=0).astype(BF16)
        rs = rstd[i]
        d_y = hat_back(dot(wkv_v, d_kv) * g_pair, yhat[i], rs[4:5])
        gate_i = gate[i]
        d_upd = d_y * gate_i
        d_gate = (d_upd * upd[i] * (1.0 - gate_i)).astype(BF16)
        zhat, rstd_z = hat(z[i])
        base_out[i] = d_y + hat_back(dot(wg_v, d_gate) * g_norm, zhat, rstd_z)
        d_tri = hat_back(dot(wo_v, d_upd.astype(BF16)) * g_tri, that[i], rs[0:1])
        put_rows(spread, i, 16, d_tri[:32])
        put_rows(spread, 8 + i, 16, d_tri[32:])

    def body(n, carry):
        row(core * HALF + n, keep_out, n)
        row((1 - core) * HALF + n, send_out, n)
        return carry

    each_row(body, rows=HALF, unroll=UNROLL // 2)
    pack(spread, dtri_out)


def tri_back_kernel(dtri, mats, out):
    wide = dtri[...].astype(F32)
    d = [wide[:, 8 * cc : 8 * cc + 8, :].reshape(N, N).astype(BF16) for cc in range(2)]
    parts = [dot(d[cc], mats[2 + cc]) for cc in range(2)]
    parts += [dot(d[cc], mats[cc], ((0,), (0,))) for cc in range(2)]
    out[...] = jnp.concatenate([p.reshape(SHARDS, 8, N) for p in parts], axis=1).astype(BF16)


def weight_kernel(dlr, ln_b, pm, proj_out, d_out, wide):
    unpack(dlr, wide)

    def body(i, total):
        parts = [take_rows(wide, 8 * q + i, 32) for q in range(4)]
        d = (jnp.concatenate(parts, axis=0) * pm[i]).astype(BF16)
        d_out[i] = d
        return total + dot(ln_b[i], d, ((1,), (1,)))

    proj_out[...] = each_row(body, jnp.zeros((C, 2 * C), F32))


def pair_grad_kernel(d, z, base, weights, gains, grad_out):
    g = twice(gains[0])
    weight = slab(weights, 1, 2 * C)

    def body(i, carry):
        zhat, rstd = hat(z[i])
        grad_out[i] = base[i] + hat_back(dot(weight, d[i]) * g, zhat, rstd)
        return carry

    each_row(body)


def query_grad_kernel(own, other, query_h, gain_h, wq_h, out, sems, query, gain, wq_t):
    fetch((query_h, gain_h, wq_h), (query, gain, wq_t), sems)
    core = lax.axis_index("tmpl") % 2
    g = gain[...] * HEAD_DIM ** (-0.5)
    wq_v = wq_t[...]

    def body(i, d_qh):
        x = query[i].astype(F32)
        cent = x - jnp.mean(x, -1, keepdims=True)
        var = jnp.mean(cent * cent, -1, keepdims=True)
        rstd = lax.rsqrt(var + 1e-05)
        xhat = cent * rstd
        dy = dot(d_qh, wq_v, ((0,), (0,))) * g
        out[i] = rstd * (dy - jnp.mean(dy, -1, keepdims=True) - xhat * jnp.mean(dy * xhat, -1, keepdims=True))

    for i in range(HALF):
        body(core * HALF + i, own[i])
        body((1 - core) * HALF + i, other[i])


def fan_kernel(own, far, out):
    total = (own[...] + far[...]).astype(BF16)
    for s in range(SHARDS):
        out[s] = total


def sum_kernel(parts, out):
    total = jnp.sum(parts[...].astype(F32), axis=0)
    out[0] = total[:, :C]
    out[1] = total[:, C:]


def call(kernel, outs, specs, scratch=(), vmem=40):
    return pl.pallas_call(
        kernel,
        out_shape=[jax.ShapeDtypeStruct(s, d) for s, d in outs],
        in_specs=specs,
        out_specs=[VMEM] * len(outs),
        scratch_shapes=list(scratch),
        compiler_params=pltpu.CompilerParams(vmem_limit_bytes=vmem * 1024 * 1024),
    )


def wide_scratch(rows):
    return pltpu.VMEM((2, rows, 128), F32)


def fetched(*arrays):
    return [pltpu.SemaphoreType.DMA((len(arrays),))] + [pltpu.VMEM(a.shape, a.dtype) for a in arrays]


def swap(x, bit):
    return lax.ppermute(x, "tmpl", [(i, i ^ bit) for i in range(4)])


def after(x, *others):
    return lax.optimization_barrier((x, *others))


def local(
    template_pair, template_mask, residue_index, query_pair, relpos_table, norm_gain, left_weight, right_weight,
    gate_weight, out_weight, tri_gain, pair_gain, kv_weight, query_gain, query_weight, attn_out_weight, cotangent,
):
    pair = jnp.swapaxes(template_pair[0], 1, 2)
    row = lambda x: x.reshape(1, -1)
    every = functools.partial(lax.all_to_all, axis_name="row", split_axis=0, concat_axis=0, tiled=True)
    plane, half = (ROWS, C, N), (ROWS, 2 * C, N)
    sources = (
        pair, row(residue_index), residue_index, relpos_table.T, template_mask, template_mask, left_weight,
        right_weight, gate_weight, out_weight, kv_weight, row(norm_gain), row(tri_gain), row(pair_gain),
    )
    scratch = fetched(*sources)
    for n in (2, 5):
        scratch[1 + n] = pltpu.SMEM(sources[n].shape, sources[n].dtype)
    lr, z, pm, weights, gains = call(
        project_kernel,
        [((SHARDS, 32, N), BF16), (plane, F32), ((ROWS, 1, N), F32), ((C, 8 * 128), BF16), ((3, C, 128), F32)],
        [ANY] * 14,
        [wide_scratch(SHARDS * 32)] + scratch,
        vmem=62,
    )(*sources)
    lr_all = every(lr)
    prepared = call(prepare_kernel, [(plane, BF16)] + [(plane, F32)] * 3, [VMEM] * 8)(
        z, weights, gains, query_pair, cotangent, row(query_gain), query_weight.T, attn_out_weight
    )
    lr_all, ln_b, qh, do, gate = after(lr_all, *prepared)
    tri, mats = call(tri_kernel, [((SHARDS, 16, N), BF16), ((4, N, N), BF16)], [VMEM])(lr_all)
    tri = every(tri)
    sg, that, yhat, upd, kv, rstd = call(
        attend_kernel,
        [((ROWS, 8, N), F32)] + [(plane, F32)] * 3 + [(half, BF16), ((ROWS, 8, N), F32)],
        [VMEM] * 8,
        [wide_scratch(SHARDS * 16)],
    )(tri, z, qh, do, gate, pm, weights, gains)
    sg = lax.all_gather(sg, "tmpl")
    dtri, keep, send, base = call(
        back_kernel,
        [((SHARDS, 16, N), BF16)] + [((HALF, C, N), BF16)] * 2 + [(plane, F32)],
        [VMEM] * 13,
        [wide_scratch(SHARDS * 16)],
    )(sg, that, yhat, gate, upd, qh, do, kv, rstd, pm, z, weights, gains)
    dtri, keep = after(dtri, keep + swap(send, 1))
    dtri = every(dtri)
    (dlr,) = call(tri_back_kernel, [((SHARDS, 32, N), BF16)], [VMEM, VMEM])(dtri, mats)
    dlr, keep = after(every(dlr), keep)
    proj, d = call(
        weight_kernel, [((C, 2 * C), F32), (half, BF16)], [VMEM] * 3, [wide_scratch(SHARDS * 32)]
    )(dlr, ln_b, pm)
    near = swap(proj, 1)
    (grad,) = call(pair_grad_kernel, [(plane, F32)], [VMEM] * 5)(d, z, base, weights, gains)
    proj = proj + near
    (fan,) = call(fan_kernel, [((SHARDS, C, 2 * C), BF16)], [VMEM] * 2)(proj, swap(proj, 2))
    fan, grad, own = after(fan, grad, keep + swap(keep, 2))
    parts = every(fan)
    sources = (query_pair, row(query_gain), query_weight.T)
    (query_grad,) = call(
        query_grad_kernel, [((ROWS, N, 2 * C), F32)], [VMEM] * 2 + [ANY] * 3, fetched(*sources)
    )(own, swap(own, 1), *sources)
    parts, query_grad = after(parts, query_grad)
    (proj,) = call(sum_kernel, [((2, C, C), F32)], [VMEM])(parts)
    return jnp.swapaxes(grad, 1, 2)[None], query_grad, proj


def solution(mesh):
    in_specs = (
        P("tmpl", "row", None, None),
        P(),
        P(),
        P("row", None, None),
        *([P()] * 12),
        P("row", None, None),
    )
    out_specs = (P("tmpl", "row", None, None), P("row", None, None), P())
    return jax.shard_map(local, mesh=mesh, in_specs=in_specs, out_specs=out_specs, check_vma=False)
```

time: 119 us -> 108 us (0.908)
  blocking collectives: 21.2 us -> 48.8 us
  waiting for transfers between devices: 40.5 us -> 21.9 us
  starting transfers between devices: 29.8 us -> 17.1 us
  local copies, waits for them, and re-layouts: 7.6 us -> 2.37 us
  Pallas kernels: 18.3 us -> 16 us
    all_to_all x0 -> x2, blocking collectives: none -> 27.8 us  [the longest x1 14.8 us: local(): dlr, keep = after(every(dlr), keep)]
    all_to_all x3 -> x1, starting transfers between devices: 15.1 us -> 4.11 us  [local(): parts = every(fan)]
    all_to_all x3 -> x1, waiting for transfers between devices: 16.2 us -> 6.51 us  [local(): parts = every(fan)]
    ppermute x4 -> x5, waiting for transfers between devices: 15.5 us -> 7.41 us  [swap(): return lax.ppermute(x, 'tmpl', [(i, i ^ bit) for i in range(4)])]
    unnamed x48 -> x22, local copies, waits for them, and re-layouts: 6.64 us -> 2.37 us
    ppermute x4 -> x5, starting transfers between devices: 5.78 us -> 4.12 us  [swap(): return lax.ppermute(x, 'tmpl', [(i, i ^ bit) for i in range(4)])]
    pallas_call x10, Pallas kernels: 16.1 us -> 14.5 us  [the longest x1 4.04 us: local(): call(project_kernel, [((SHARDS, 32, N), BF16), (plane, F32), ((ROWS, 1, N...]
  transfers between devices with their start and end apart: 8 -> 7, of which waited for: 6 -> 6; matrix products, arithmetic and copies ran while one was open for 0% -> 0% of each run, Pallas kernels for 5% -> 7%
where the time goes in v3:
time: 108 us; the launch traced here: 107 us
  blocking collectives  48.8 us (45%)
  waiting for transfers between devices  21.9 us (20%)
  starting transfers between devices  17.1 us (16%)
  Pallas kernels  16 us (15%)
  local copies, waits for them, and re-layouts  2.37 us (2%)
    all_to_all x1, blocking collectives, local(): dlr, keep = after(every(dlr), keep)  14.8 us
    all_to_all x1, blocking collectives, local(): tri = every(tri)  13.2 us
    all_to_all x1, blocking collectives, local(): dtri = every(dtri)  13 us
    all_to_all x1, starting transfers between devices, local(): lr_all = every(lr)  8.9 us
    all_to_all x1, waiting for transfers between devices, local(): lr_all = every(lr)  7.96 us
    all_gather x1, blocking collectives, local(): sg = lax.all_gather(sg, 'tmpl')  7.84 us
    ppermute x5, waiting for transfers between devices, swap(): return lax.ppermute(x, 'tmpl', [(i, i ^ bit) for i in range(4)])  7.41 us
    all_to_all x1, waiting for transfers between devices, local(): parts = every(fan)  6.51 us
  transfers between devices with their start and end apart: 7, of which 6 were waited for; matrix products, arithmetic and copies ran while one was open for 0% of the time, Pallas kernels for 7%

profile of v3, /device:TPU:0, one launch (start us, length us, event | category | flops | bytes accessed | tf_op | source)
XLA Modules:
  0.0 107.2 jit_solution(15296289089003666588)
XLA Ops:
  0.6 0.0 copy-start.2
  0.6 4.0 %shard_map.184 = (bf16[32,32,256]{2,1,0:T(8,128)(2,1)}, f32[8,64,256]{2,1,0:T(8,128)}, f32[8,1,256]{2,1,0:T(1,128)}, bf16[64,1024]{1,0:T(8,128)(2,1)}, f32[3,64,128]{2,1,0:T(8,128)}) custom-call(bf16[8,64,256]{2,1,0:T(8,128)(2,1)} %bitcast.20, s32[1,256]{1,0:T(1,128)} %bitcast.22, s32[256]{0:T(256)} %refs_2_.1, bf16[64,128]{1,0:T(8,128)(2,1)} %bitcast.21, ...), custom_call_target="tpu_custom_call" | custom-call | tf_op jit(solution)/shard_map/pallas_call | solution.py:349
  4.7 0.0 copy-start
  4.7 0.0 copy-start.1
  4.7 0.0 copy-start.3
  4.7 0.0 copy-start.8
  4.7 0.0 copy-start.9
  4.8 8.9 %all-to-all-start = ((bf16[32,32,256]{2,1,0:T(8,128)(2,1)}), bf16[32,32,256]{2,1,0:T(8,128)(2,1)S(1)}, u32[]{:S(2)}, u32[]{:S(2)}) async-start(bf16[32,32,256]{2,1,0:T(8,128)(2,1)} %get-tuple-element.40), calls=%async_computation | async-start | bytes 1048576 | tf_op jit(solution)/shard_map/all_to_all | solution.py:356
  13.7 0.0 copy-start.10
  13.7 0.0 copy-done.2
  13.7 0.0 copy-done
  13.7 0.0 copy-done.1
  13.7 0.0 copy-done.3
  13.7 0.0 copy-done.8
  13.7 0.0 copy-done.9
  13.7 0.6 copy-done.10
  14.3 1.0 copy-done.4
  15.4 1.2 %shard_map.185 = (bf16[8,64,256]{2,1,0:T(8,128)(2,1)S(1)}, f32[8,64,256]{2,1,0:T(8,128)S(1)}, f32[8,64,256]{2,1,0:T(8,128)S(1)}, f32[8,64,256]{2,1,0:T(8,128)S(1)}) custom-call(f32[8,64,256]{2,1,0:T(8,128)S(1)} %copy-done, bf16[64,1024]{1,0:T(8,128)(2,1)S(1)} %copy-done.1, f32[3,64,128]{2,1,0:T(8,128)S(1)} %copy-done.3, bf16[8,256,128]{2,1,0:T(8,128)(2,1)S(1)} %copy-done.2, ...), custom_call_target="tpu_custom_call" | custom-call | tf_op jit(solution)/shard_map/pallas_call | solution.py:357
  16.6 0.0 copy-start.5
  16.6 0.7 copy-done.5
  17.3 8.0 %all-to-all-done.lr = bf16[32,32,256]{2,1,0:T(8,128)(2,1)S(1)} async-done(((bf16[32,32,256]{2,1,0:T(8,128)(2,1)}), bf16[32,32,256]{2,1,0:T(8,128)(2,1)S(1)}, u32[]{:S(2)}, u32[]{:S(2)}) %all-to-all-start) | async-done | bytes 524320 | tf_op jit(solution)/shard_map/all_to_all | solution.py:356
  25.3 0.3 shard_map.186
  25.5 0.0 copy-start.7
  25.5 13.2 %all_to_all.25.tri = bf16[32,16,256]{2,1,0:T(8,128)(2,1)S(1)} all-to-all(bf16[32,16,256]{2,1,0:T(8,128)(2,1)S(1)} %get-tuple-element.49), channel_id=1, replica_groups=mesh['tmpl'=4,'row'=32] {'row'}, dimensions={0} | all-to-all | bytes 524288 | tf_op jit(solution)/shard_map/all_to_all | solution.py:362
  38.8 1.5 %shard_map.187 = (f32[8,8,256]{2,1,0:T(8,128)S(1)}, f32[8,64,256]{2,1,0:T(8,128)S(1)}, f32[8,64,256]{2,1,0:T(8,128)S(1)}, f32[8,64,256]{2,1,0:T(8,128)S(1)}, bf1...) custom-call(bf16[32,16,256]{2,1,0:T(8,128)(2,1)S(1)} %all_to_all.25.tri, f32[8,64,256]{2,1,0:T(8,128)S(1)} %copy-done, ...), custom_call_target="tpu_custom_call" | custom-call | tf_op jit(solution)/shard_map/pallas_call | solution.py:363
  40.2 7.8 %all-gather = f32[32,8,256]{2,1,0:T(8,128)S(1)} all-gather(f32[8,8,256]{2,1,0:T(8,128)S(1)} %get-tuple-element.54), channel_id=2, replica_groups=mesh['tmpl'=4,'row'=32] {'tmpl'}, dimensions={0}, use_global_device_ids=true | all-gather | bytes 327680 | tf_op jit(solution)/shard_map/all_gather | solution.py:369
  48.1 1.9 %shard_map.188 = (bf16[32,16,256]{2,1,0:T(8,128)(2,1)S(1)}, bf16[4,64,256]{2,1,0:T(8,128)(2,1)S(1)}, bf16[4,64,256]{2,1,0:T(8,128)(2,1)S(1)}, f32[8,64,256]{2,1,0:T(8,128)S(1)}) custom-call(f32[4,8,8,256]{3,2,1,0:T(8,128)S(1)} %bitcast.14, f32[8,64,256]{2,1,0:T(8,128)S(1)} %get-tuple-element.55.that, f32[8,64,256]{2,1,0:T(8,128)S(1)} %get-tuple-element.56.yhat, ...), custom_call_target="tpu_custom_call" | custom-call | tf_op jit(solution)/shard_map/pallas_call | solution.py:370
  50.0 0.4 collective-permute-start
  50.4 1.0 collective-permute-done
  51.5 13.0 %all_to_all.26.dtri = bf16[32,16,256]{2,1,0:T(8,128)(2,1)S(1)} all-to-all(bf16[32,16,256]{2,1,0:T(8,128)(2,1)S(1)} %get-tuple-element.63), channel_id=1, replica_groups=mesh['tmpl'=4,'row'=32] {'row'}, dimensions={0} | all-to-all | bytes 524288 | tf_op jit(solution)/shard_map/all_to_all | solution.py:377
  64.5 0.3 shard_map.189
  64.8 0.0 copy-start.6
  64.8 14.8 %all_to_all.27.dlr = bf16[32,32,256]{2,1,0:T(8,128)(2,1)S(1)} all-to-all(bf16[32,32,256]{2,1,0:T(8,128)(2,1)S(1)} %shard_map.189), channel_id=1, replica_groups=mesh['tmpl'=4,'row'=32] {'row'}, dimensions={0} | all-to-all | bytes 1048576 | tf_op jit(solution)/shard_map/all_to_all | solution.py:379
  79.6 3.3 %collective-permute-start.3 = (bf16[4,64,256]{2,1,0:T(8,128)(2,1)S(1)}, bf16[4,64,256]{2,1,0:T(8,128)(2,1)S(1)}, u32[]{:S(2)}, u32[]{:S(2)}) collective-permute-start(bf16[4,64,256]{2,1,0:T(8,128)(2,1)S(1)} %add.9), channel_id=1, source_target_pairs={{0,64},{32,96},{64,0},{96,32},{1,65},{33,97},{65,1},{97,33},{2,66}... | collective-permute-start | bytes 393224 | tf_op jit(solution)/shard_map/ppermute | solution.py:327
  82.9 0.9 shard_map.190
  83.8 0.1 collective-permute-start.1
  83.9 1.2 %collective-permute-done.1 = f32[64,128]{1,0:T(8,128)S(1)} collective-permute-done((f32[64,128]{1,0:T(8,128)S(1)}, f32[64,128]{1,0:T(8,128)S(1)}, u32[]{:S(2)}, u32[]{:S(2)}) %collective-permute-start.1) | collective-permute-done | bytes 32800 | tf_op jit(solution)/shard_map/ppermute | solution.py:327
  85.1 0.2 collective-permute-start.2
  85.4 1.3 %shard_map.192 = f32[8,64,256]{2,1,0:T(8,128)} custom-call(bf16[8,128,256]{2,1,0:T(8,128)(2,1)S(1)} %get-tuple-element.69.d, f32[8,64,256]{2,1,0:T(8,128)S(1)} %copy-done, f32[8,64,256]{2,1,0:T(8,128)S(1)} %get-tuple-element.70.base, bf16[64,1024]{1,0:T(8,128)(2,1)S(1)} %copy-done.1, f32[3,64,128]{2,1,0:T(8,128)S(1)} %copy-done.3), custom_call_target="tpu_custom_call" | custom-call | tf_op jit(solution)/shard_map/pallas_call | solution.py:384
  86.6 3.9 %collective-permute-done.2.far = f32[64,128]{1,0:T(8,128)S(1)} collective-permute-done((f32[64,128]{1,0:T(8,128)S(1)}, f32[64,128]{1,0:T(8,128)S(1)}, u32[]{:S(2)}, u32[]{:S(2)}) %collective-permute-start.2) | collective-permute-done | bytes 32800 | tf_op jit(solution)/shard_map/ppermute | solution.py:327
  90.5 0.9 shard_map.191
  91.4 0.0 collective-permute-done.3
  91.4 4.1 %all-to-all-start.4 = ((bf16[32,64,128]{2,1,0:T(8,128)(2,1)}), bf16[32,64,128]{2,1,0:T(8,128)(2,1)S(1)}, u32[]{:S(2)}, u32[]{:S(2)}) async-start(bf16[32,64,128]{2,1,0:T(8,128)(2,1)} %shard_map.191), calls=%async_computation.4 | async-start | bytes 1048576 | tf_op jit(solution)/shard_map/all_to_all | solution.py:388
  95.6 0.1 collective-permute-start.4
  95.6 1.3 %collective-permute-done.4.other = bf16[4,64,256]{2,1,0:T(8,128)(2,1)S(1)} collective-permute-done((bf16[4,64,256]{2,1,0:T(8,128)(2,1)S(1)}, bf16[4,64,256]{2,1,0:T(8,128)(2,1)S(1)}, u32[]{:S(2)}, u32[]{:S(2)}) %collective-permute-start.4) | collective-permute-done | bytes 131104 | tf_op jit(solution)/shard_map/ppermute | solution.py:327
  97.0 2.9 %shard_map.193 = f32[8,256,128]{2,1,0:T(8,128)} custom-call(bf16[4,64,256]{2,1,0:T(8,128)(2,1)S(1)} %add.11.own, bf16[4,64,256]{2,1,0:T(8,128)(2,1)S(1)} %collective-permute-done.4.other, bf16[8,256,128]{2,1,0:T(8,128)(2,1)S(1)} %copy-done.2, f32[1,128]{1,0:T(1,128)S(1)} %bitcast.18, bf16[64,128]{1,0:T(8,128)(2,1)S(1)} %bitcast.16), custom_call_target="tpu_custom_call" | custom-call | tf_op jit(solution)/shard_map/pallas_call | solution.py:390
  99.9 6.5 %all-to-all-done.4.parts = bf16[32,64,128]{2,1,0:T(8,128)(2,1)S(1)} async-done(((bf16[32,64,128]{2,1,0:T(8,128)(2,1)}), bf16[32,64,128]{2,1,0:T(8,128)(2,1)S(1)}, u32[]{:S(2)}, u32[]{:S(2)}) %all-to-all-start.4) | async-done | bytes 524320 | tf_op jit(solution)/shard_map/all_to_all | solution.py:388
  106.4 0.8 shard_map.194
  (6 shorter events, 0.1 us)
Async XLA Ops:
  0.6 13.0 %copy-start.2 = (bf16[8,256,128]{2,1,0:T(8,128)(2,1)S(1)}, bf16[8,256,128]{2,1,0:T(8,128)(2,1)}, u32[]{:S(2)}) copy-start(bf16[8,256,128]{2,1,0:T(8,128)(2,1)} %query_h.1) | copy-start | bytes 1572868
  4.7 9.0 %copy-start = (f32[8,64,256]{2,1,0:T(8,128)S(1)}, f32[8,64,256]{2,1,0:T(8,128)}, u32[]{:S(2)}) copy-start(f32[8,64,256]{2,1,0:T(8,128)} %get-tuple-element.41.z) | copy-start | bytes 1572868
  4.7 9.0 %copy-start.1 = (bf16[64,1024]{1,0:T(8,128)(2,1)S(1)}, bf16[64,1024]{1,0:T(8,128)(2,1)}, u32[]{:S(2)}) copy-start(bf16[64,1024]{1,0:T(8,128)(2,1)} %get-tuple-element.42.weights) | copy-start | bytes 393220
  4.7 9.0 %copy-start.3 = (f32[3,64,128]{2,1,0:T(8,128)S(1)}, f32[3,64,128]{2,1,0:T(8,128)}, u32[]{:S(2)}) copy-start(f32[3,64,128]{2,1,0:T(8,128)} %get-tuple-element.43.gains) | copy-start | bytes 294916
  4.7 9.0 %copy-start.8 = (bf16[128,64]{0,1:T(8,128)(2,1)S(1)}, bf16[128,64]{0,1:T(8,128)(2,1)}, u32[]{:S(2)}) copy-start(bf16[128,64]{0,1:T(8,128)(2,1)} %param.31) | copy-start | bytes 49156
  4.7 9.0 %copy-start.9 = (bf16[64,128]{1,0:T(8,128)(2,1)S(1)}, bf16[64,128]{1,0:T(8,128)(2,1)}, u32[]{:S(2)}) copy-start(bf16[64,128]{1,0:T(8,128)(2,1)} %wao.1) | copy-start | bytes 49156
  4.8 20.5 %all-to-all-start = ((bf16[32,32,256]{2,1,0:T(8,128)(2,1)}), bf16[32,32,256]{2,1,0:T(8,128)(2,1)S(1)}, u32[]{:S(2)}, u32[]{:S(2)}) async-start(bf16[32,32,256]{2,1,0:T(8,128)(2,1)} %get-tuple-element.40), calls=%async_computation | async-start | bytes 1048576 | tf_op jit(solution)/shard_map/all_to_all | solution.py:356
  13.7 0.7 copy-start.10
  14.3 1.0 copy-start.4
  16.6 0.7 copy-start.5
  25.5 13.2 %copy-start.7 = (f32[8,1,256]{2,1,0:T(1,128)S(1)}, f32[8,1,256]{2,1,0:T(1,128)}, u32[]{:S(2)}) copy-start(f32[8,1,256]{2,1,0:T(1,128)} %get-tuple-element.53.pm) | copy-start | bytes 24580
  50.0 1.4 %collective-permute-start = (bf16[4,64,256]{2,1,0:T(8,128)(2,1)S(1)}, bf16[4,64,256]{2,1,0:T(8,128)(2,1)S(1)}, u32[]{:S(2)}, u32[]{:S(2)}) collective-permute-start(bf16[4,64,256]{2,1,0:T(8,128)(2,1)S(1)} %get-tuple-element.62), channel_id=1, source_target_pairs={{0,32},{32,0},{64,96},{96,64},{1,33},{33,1},{65,97},{97,65},{2,34}... | collective-permute-start | bytes 393224 | tf_op jit(solution)/shard_map/ppermute | solution.py:327
  64.8 18.1 %copy-start.6 = (bf16[8,64,256]{2,1,0:T(8,128)(2,1)S(1)}, bf16[8,64,256]{2,1,0:T(8,128)(2,1)}, u32[]{:S(2)}) copy-start(bf16[8,64,256]{2,1,0:T(8,128)(2,1)} %copy-done.5) | copy-start | bytes 786436
  79.6 11.8 %collective-permute-start.3 = (bf16[4,64,256]{2,1,0:T(8,128)(2,1)S(1)}, bf16[4,64,256]{2,1,0:T(8,128)(2,1)S(1)}, u32[]{:S(2)}, u32[]{:S(2)}) collective-permute-start(bf16[4,64,256]{2,1,0:T(8,128)(2,1)S(1)} %add.9), channel_id=1, source_target_pairs={{0,64},{32,96},{64,0},{96,32},{1,65},{33,97},{65,1},{97,33},{2,66}... | collective-permute-start | bytes 393224 | tf_op jit(solution)/shard_map/ppermute | solution.py:327
  83.8 1.3 %collective-permute-start.1 = (f32[64,128]{1,0:T(8,128)S(1)}, f32[64,128]{1,0:T(8,128)S(1)}, u32[]{:S(2)}, u32[]{:S(2)}) collective-permute-start(f32[64,128]{1,0:T(8,128)S(1)} %get-tuple-element.68), channel_id=1, source_target_pairs={{0,32},{32,0},{64,96},{96,64},{1,33},{33,1},{65,97},{97,65},{2,34}... | collective-permute-start | bytes 98312 | tf_op jit(solution)/shard_map/ppermute | solution.py:327
  85.1 5.4 %collective-permute-start.2 = (f32[64,128]{1,0:T(8,128)S(1)}, f32[64,128]{1,0:T(8,128)S(1)}, u32[]{:S(2)}, u32[]{:S(2)}) collective-permute-start(f32[64,128]{1,0:T(8,128)S(1)} %add.10.own), channel_id=1, source_target_pairs={{0,64},{32,96},{64,0},{96,32},{1,65},{33,97},{65,1},{97,33},{2,66}... | collective-permute-start | bytes 98312 | tf_op jit(solution)/shard_map/ppermute | solution.py:327
  91.4 15.0 %all-to-all-start.4 = ((bf16[32,64,128]{2,1,0:T(8,128)(2,1)}), bf16[32,64,128]{2,1,0:T(8,128)(2,1)S(1)}, u32[]{:S(2)}, u32[]{:S(2)}) async-start(bf16[32,64,128]{2,1,0:T(8,128)(2,1)} %shard_map.191), calls=%async_computation.4 | async-start | bytes 1048576 | tf_op jit(solution)/shard_map/all_to_all | solution.py:388
  95.6 1.4 %collective-permute-start.4 = (bf16[4,64,256]{2,1,0:T(8,128)(2,1)S(1)}, bf16[4,64,256]{2,1,0:T(8,128)(2,1)S(1)}, u32[]{:S(2)}, u32[]{:S(2)}) collective-permute-start(bf16[4,64,256]{2,1,0:T(8,128)(2,1)S(1)} %add.11.own), channel_id=1, source_target_pairs={{0,32},{32,0},{64,96},{96,64},{1,33},{33,1},{65,97},{97,65},{2,34}... | collective-permute-start | bytes 393224 | tf_op jit(solution)/shard_map/ppermute | solution.py:327

commit v4 on v3

--- a/solution.py
+++ b/solution.py
@@ -15,7 +15,7 @@
 ROWS = 8
 N = 256
 SHARDS = 32
-UNROLL = 4
+UNROLL = 8
 HALF = ROWS // 2
 ANY = pl.BlockSpec(memory_space=pltpu.HBM)
 VMEM = pl.BlockSpec(memory_space=pltpu.VMEM)
@@ -53,18 +53,31 @@
     return rstd * (dy - jnp.mean(dy, 0, keepdims=True) - xhat * jnp.mean(dy * xhat, 0, keepdims=True))
 
 
+def owner_rows(left, right):
+    rows = jnp.concatenate([left, right], axis=0)
+    rows = jnp.concatenate([rows, rows], axis=1)
+    sub = lax.broadcasted_iota(jnp.int32, (8, 128), 0)
+    lane = lax.broadcasted_iota(jnp.int32, (8, 128), 1) // C
+    tiles = []
+    for pair in range(ROWS // 2):
+        mine = (sub == 2 * pair + lane)[None, None]
+        spread = jnp.broadcast_to(rows.reshape(4, SHARDS, 1, 128), (4, SHARDS, 8, 128))
+        tiles.append(jnp.where(mine, spread, 0.0))
+    return tiles
+
+
 def put_rows(spread, first, step, x):
     for half in range(2):
         spread[half, pl.ds(first, x.shape[0], stride=step), :] = x[:, 128 * half : 128 * half + 128]
 
 
-def take_rows(wide, first, step):
-    return jnp.concatenate([wide[half, pl.ds(first, SHARDS, stride=step), :] for half in range(2)], axis=1)
-
-
 def pack(spread, out):
     for half in range(2):
         out[:, :, 128 * half : 128 * half + 128] = spread[half].reshape(out.shape[0], out.shape[1], 128).astype(BF16)
+
+
+def take_rows(wide, first, step):
+    return jnp.concatenate([wide[half, pl.ds(first, SHARDS, stride=step), :] for half in range(2)], axis=1)
 
 
 def unpack(x, wide):
@@ -90,11 +103,15 @@
     return lax.fori_loop(0, rows // unroll, step, carry)
 
 
-def fetch(sources, places, sems):
-    copies = [pltpu.make_async_copy(src, dst, sems.at[n]) for n, (src, dst) in enumerate(zip(sources, places))]
-    for copy in copies:
+def copies(sources, places, sems, first=0):
+    started = [pltpu.make_async_copy(src, dst, sems.at[first + n]) for n, (src, dst) in enumerate(zip(sources, places))]
+    for copy in started:
         copy.start()
-    for copy in copies:
+    return started
+
+
+def arrive(started):
+    for copy in started:
         copy.wait()
 
 
@@ -105,35 +122,43 @@
 
 
 def project_kernel(*refs):
-    sources, outs, (spread, sems), places = refs[:14], refs[14:19], refs[19:21], refs[21:]
+    sources, outs, places = refs[:14], refs[14:19], refs[28:]
+    lhs, normed, lr, z, pm, weights, gains, out_sems, sems = refs[19:28]
     lr_out, z_out, pm_out, weights_out, gains_out = outs
-    fetch(sources, places, sems)
-    pair, res, res_s, table_t, mask, mask_s, wl, wr, wg, wo, wkv, norm_gain, tri_gain, pair_gain = places
+    arriving = copies(sources, places, sems)
+    wl, wr, norm_gain, table_t, res, res_s, mask, mask_s, pair, wg, wo, wkv, tri_gain, pair_gain = places
+    arrive(arriving[:2])
+    for pair_of, tile in enumerate(owner_rows(flip(wl[...]), flip(wr[...]))):
+        for q in range(4):
+            lhs[:, 8 * q : 8 * q + 8, 128 * pair_of : 128 * pair_of + 128] = tile[q].astype(BF16)
+    arrive(arriving[2:9])
     t, start, mask_row = place(mask)
-    weight = jnp.concatenate([flip(wl[...]), flip(wr[...])], axis=0).astype(BF16)
     table, residues, gain = table_t[...], res[...], column(norm_gain[...])
     g = twice(gain)
 
     def body(i, carry):
-        z = pair[i].astype(F32) + relative(res_s, residues, table, start + i)
-        z_out[i] = z
-        pm = mask_row * mask_s[t, start + i].astype(F32)
-        pm_out[i] = pm
-        both = dot(weight, (hat(z)[0] * g).astype(BF16)) * pm
-        for q in range(4):
-            put_rows(spread, 8 * q + i, 32, both[32 * q : 32 * q + 32])
+        z_i = pair[i].astype(F32) + relative(res_s, residues, table, start + i)
+        z[i] = z_i
+        pm_i = mask_row * mask_s[t, start + i].astype(F32)
+        pm[i] = pm_i
+        normed[i * C : i * C + C, :] = (hat(z_i)[0] * g).astype(BF16)
         return carry
 
     each_row(body)
-    pack(spread, lr_out)
+    both = dot(lhs[...].reshape(SHARDS * 32, ROWS * C), normed[...]).reshape(SHARDS * 4, ROWS, N)
+    lr[...] = (both * pm[...].reshape(1, ROWS, N)).reshape(SHARDS, 32, N).astype(BF16)
+    leaving = copies((lr, z, pm), (lr_out, z_out, pm_out), out_sems)
+    arrive(arriving[9:])
     blank = jnp.zeros((C, C), BF16)
     wkv_t = flip(wkv[...]).astype(BF16)
     parts = [wkv[...], wl[...], wr[...], flip(wo[...]).astype(BF16), blank, wo[...], blank, wg[...], blank]
     parts += [wkv_t[:C], blank, wkv_t[C:], blank, flip(wg[...]).astype(BF16), blank]
-    weights_out[...] = jnp.concatenate(parts, axis=1)
-    gains_out[0] = gain
-    gains_out[1] = column(tri_gain[...])
-    gains_out[2] = column(pair_gain[...])
+    weights[...] = jnp.concatenate(parts, axis=1)
+    gains[0] = gain
+    gains[1] = column(tri_gain[...])
+    gains[2] = column(pair_gain[...])
+    leaving += copies((weights, gains), (weights_out, gains_out), out_sems, 3)
+    arrive(leaving)
 
 
 def prepare_kernel(z, weights, gains, query, cot, q_gain, wq_t, wao, ln_out, qh_out, do_out, gate_out):
@@ -201,15 +226,15 @@
 
 
 def back_kernel(
-    sg, that, yhat, gate, upd, qh, do, kv, rstd, pm, z, weights, gains,
-    dtri_out, keep_out, send_out, base_out, spread,
+    sg, that, yhat, gate, upd, qh, do, kv, rstd, pm, weights, gains,
+    dtri_out, dqh_out, dy_out, dgate_out, spread,
 ):
     t = lax.axis_index("tmpl")
     core = t % 2
-    g_norm, g_tri, g_pair = twice(gains[0]), twice(gains[1]), twice(gains[2])
-    wkv_v, wo_v, wg_v = slab(weights, 0, 2 * C), slab(weights, 3), slab(weights, 4)
-
-    def row(i, dqh_out, n):
+    g_tri, g_pair = twice(gains[1]), twice(gains[2])
+    wkv_v, wo_v = slab(weights, 0, 2 * C), slab(weights, 3)
+
+    def row(i, n):
         every = [sg[s, i] for s in range(4)]
         own = sg[t, i]
         top = jnp.maximum(jnp.maximum(every[0][:4], every[1][:4]), jnp.maximum(every[2][:4], every[3][:4]))
@@ -225,22 +250,23 @@
         gate_i = gate[i]
         d_upd = d_y * gate_i
         d_gate = (d_upd * upd[i] * (1.0 - gate_i)).astype(BF16)
-        zhat, rstd_z = hat(z[i])
-        base_out[i] = d_y + hat_back(dot(wg_v, d_gate) * g_norm, zhat, rstd_z)
+        dy_out[i] = d_y
+        dgate_out[i] = d_gate
         d_tri = hat_back(dot(wo_v, d_upd.astype(BF16)) * g_tri, that[i], rs[0:1])
         put_rows(spread, i, 16, d_tri[:32])
         put_rows(spread, 8 + i, 16, d_tri[32:])
 
     def body(n, carry):
-        row(core * HALF + n, keep_out, n)
-        row((1 - core) * HALF + n, send_out, n)
+        row(core * HALF + n, n)
+        row((1 - core) * HALF + n, HALF + n)
         return carry
 
     each_row(body, rows=HALF, unroll=UNROLL // 2)
     pack(spread, dtri_out)
 
 
-def tri_back_kernel(dtri, mats, out):
+def tri_back_kernel(dtri, mats, dqh, near, out, keep_out):
+    keep_out[...] = (dqh[:HALF].astype(F32) + near[HALF:].astype(F32)).astype(BF16)
     wide = dtri[...].astype(F32)
     d = [wide[:, 8 * cc : 8 * cc + 8, :].reshape(N, N).astype(BF16) for cc in range(2)]
     parts = [dot(d[cc], mats[2 + cc]) for cc in range(2)]
@@ -260,20 +286,21 @@
     proj_out[...] = each_row(body, jnp.zeros((C, 2 * C), F32))
 
 
-def pair_grad_kernel(d, z, base, weights, gains, grad_out):
+def pair_grad_kernel(d, z, d_y, d_gate, weights, gains, grad_out):
     g = twice(gains[0])
-    weight = slab(weights, 1, 2 * C)
+    weight = jnp.concatenate([slab(weights, 1, 2 * C), slab(weights, 4)], axis=1)
 
     def body(i, carry):
         zhat, rstd = hat(z[i])
-        grad_out[i] = base[i] + hat_back(dot(weight, d[i]) * g, zhat, rstd)
+        d_ln = dot(weight, jnp.concatenate([d[i], d_gate[i]], axis=0))
+        grad_out[i] = d_y[i] + hat_back(d_ln * g, zhat, rstd)
         return carry
 
     each_row(body)
 
 
 def query_grad_kernel(own, other, query_h, gain_h, wq_h, out, sems, query, gain, wq_t):
-    fetch((query_h, gain_h, wq_h), (query, gain, wq_t), sems)
+    arrive(copies((query_h, gain_h, wq_h), (query, gain, wq_t), sems))
     core = lax.axis_index("tmpl") % 2
     g = gain[...] * HEAD_DIM ** (-0.5)
     wq_v = wq_t[...]
@@ -304,12 +331,12 @@
     out[1] = total[:, C:]
 
 
-def call(kernel, outs, specs, scratch=(), vmem=40):
+def call(kernel, outs, specs, scratch=(), vmem=40, home=VMEM):
     return pl.pallas_call(
         kernel,
         out_shape=[jax.ShapeDtypeStruct(s, d) for s, d in outs],
         in_specs=specs,
-        out_specs=[VMEM] * len(outs),
+        out_specs=[home] * len(outs),
         scratch_shapes=list(scratch),
         compiler_params=pltpu.CompilerParams(vmem_limit_bytes=vmem * 1024 * 1024),
     )
@@ -340,18 +367,21 @@
     every = functools.partial(lax.all_to_all, axis_name="row", split_axis=0, concat_axis=0, tiled=True)
     plane, half = (ROWS, C, N), (ROWS, 2 * C, N)
     sources = (
-        pair, row(residue_index), residue_index, relpos_table.T, template_mask, template_mask, left_weight,
-        right_weight, gate_weight, out_weight, kv_weight, row(norm_gain), row(tri_gain), row(pair_gain),
+        left_weight, right_weight, row(norm_gain), relpos_table.T, row(residue_index), residue_index, template_mask,
+        template_mask, pair, gate_weight, out_weight, kv_weight, row(tri_gain), row(pair_gain),
     )
     scratch = fetched(*sources)
-    for n in (2, 5):
+    for n in (5, 7):
         scratch[1 + n] = pltpu.SMEM(sources[n].shape, sources[n].dtype)
+    outs = [((SHARDS, 32, N), BF16), (plane, F32), ((ROWS, 1, N), F32), ((C, 8 * 128), BF16), ((3, C, 128), F32)]
+    held = [pltpu.VMEM(*o) for o in outs] + [pltpu.SemaphoreType.DMA((len(outs),))]
     lr, z, pm, weights, gains = call(
         project_kernel,
-        [((SHARDS, 32, N), BF16), (plane, F32), ((ROWS, 1, N), F32), ((C, 8 * 128), BF16), ((3, C, 128), F32)],
+        outs,
         [ANY] * 14,
-        [wide_scratch(SHARDS * 32)] + scratch,
+        [pltpu.VMEM((SHARDS, 32, ROWS * C), BF16), pltpu.VMEM((ROWS * C, N), BF16)] + held + scratch,
         vmem=62,
+        home=ANY,
     )(*sources)
     lr_all = every(lr)
     prepared = call(prepare_kernel, [(plane, BF16)] + [(plane, F32)] * 3, [VMEM] * 8)(
@@ -367,21 +397,21 @@
         [wide_scratch(SHARDS * 16)],
     )(tri, z, qh, do, gate, pm, weights, gains)
     sg = lax.all_gather(sg, "tmpl")
-    dtri, keep, send, base = call(
+    dtri, dqh, d_y, d_gate = call(
         back_kernel,
-        [((SHARDS, 16, N), BF16)] + [((HALF, C, N), BF16)] * 2 + [(plane, F32)],
-        [VMEM] * 13,
+        [((SHARDS, 16, N), BF16), (plane, BF16), (plane, F32), (plane, BF16)],
+        [VMEM] * 12,
         [wide_scratch(SHARDS * 16)],
-    )(sg, that, yhat, gate, upd, qh, do, kv, rstd, pm, z, weights, gains)
-    dtri, keep = after(dtri, keep + swap(send, 1))
-    dtri = every(dtri)
-    (dlr,) = call(tri_back_kernel, [((SHARDS, 32, N), BF16)], [VMEM, VMEM])(dtri, mats)
+    )(sg, that, yhat, gate, upd, qh, do, kv, rstd, pm, weights, gains)
+    dlr, keep = call(tri_back_kernel, [((SHARDS, 32, N), BF16), ((HALF, C, N), BF16)], [VMEM] * 4)(
+        every(dtri), mats, dqh, swap(dqh, 1)
+    )
     dlr, keep = after(every(dlr), keep)
     proj, d = call(
         weight_kernel, [((C, 2 * C), F32), (half, BF16)], [VMEM] * 3, [wide_scratch(SHARDS * 32)]
     )(dlr, ln_b, pm)
     near = swap(proj, 1)
-    (grad,) = call(pair_grad_kernel, [(plane, F32)], [VMEM] * 5)(d, z, base, weights, gains)
+    (grad,) = call(pair_grad_kernel, [(plane, F32)], [VMEM] * 6)(d, z, d_y, d_gate, weights, gains)
     proj = proj + near
     (fan,) = call(fan_kernel, [((SHARDS, C, 2 * C), BF16)], [VMEM] * 2)(proj, swap(proj, 2))
     fan, grad, own = after(fan, grad, keep + swap(keep, 2))

time: 108 us -> 104 us (0.963)
  Pallas kernels: 16 us -> 13.6 us
    pallas_call x4, Pallas kernels: 7.56 us -> 5.7 us  [the longest x1 3.16 us: local(): call(project_kernel, outs, [ANY] * 14, [pltpu.VMEM((SHARDS, 32, ROWS * C)...]
  transfers between devices with their start and end apart: 7 -> 7, of which waited for: 6 -> 5; matrix products, arithmetic and copies ran while one was open for 0% -> 0% of each run, Pallas kernels for 7% -> 7%
where the time goes in v4:
time: 104 us
  blocking collectives  48.3 us (46%)
  waiting for transfers between devices  21.1 us (20%)
  starting transfers between devices  17.1 us (16%)
  Pallas kernels  13.6 us (13%)
  local copies, waits for them, and re-layouts  2.46 us (2%)
    all_to_all x1, blocking collectives, local(): dlr, keep = after(every(dlr), keep)  14.5 us
    all_to_all x1, blocking collectives, local(): tri = every(tri)  13.2 us
    all_to_all x1, blocking collectives, local(): every(dtri)  12.8 us
    all_to_all x1, starting transfers between devices, local(): lr_all = every(lr)  8.9 us
    all_to_all x1, waiting for transfers between devices, local(): lr_all = every(lr)  8.12 us
    all_gather x1, blocking collectives, local(): sg = lax.all_gather(sg, 'tmpl')  7.84 us
    all_to_all x1, waiting for transfers between devices, local(): parts = every(fan)  6.51 us
    ppermute x5, waiting for transfers between devices, swap(): return lax.ppermute(x, 'tmpl', [(i, i ^ bit) for i in range(4)])  6.45 us
  transfers between devices with their start and end apart: 7, of which 5 were waited for; matrix products, arithmetic and copies ran while one was open for 0% of the time, Pallas kernels for 7%

profile of v4, /device:TPU:0, one launch (start us, length us, event | category | flops | bytes accessed | tf_op | source)
XLA Modules:
  0.0 103.5 jit_solution(3020566012054605446)
XLA Ops:
  0.6 0.0 copy-start.2
  0.6 3.2 %shard_map.184 = (bf16[32,32,256]{2,1,0:T(8,128)(2,1)}, f32[8,64,256]{2,1,0:T(8,128)}, f32[8,1,256]{2,1,0:T(1,128)}, bf16[64,1024]{1,0:T(8,128)(2,1)}, f32[3,64,128]{2,1,0:T(8,128)}) custom-call(bf16[64,64]{1,0:T(8,128)(2,1)} %refs_0_.1, bf16[64,64]{1,0:T(8,128)(2,1)} %refs_1_.1, f32[1,64]{1,0:T(1,128)} %bitcast.23, bf16[64,128]{1,0:T(8,128)(2,1)} %bitcast.21, ...), custom_call_target="tpu_custom_call" | custom-call | tf_op jit(solution)/shard_map/pallas_call | solution.py:378
  3.8 0.0 copy-start
  3.8 0.0 copy-start.1
  3.8 0.0 copy-start.5
  3.8 0.0 copy-start.8
  3.9 0.0 copy-start.9
  3.9 8.9 %all-to-all-start = ((bf16[32,32,256]{2,1,0:T(8,128)(2,1)}), bf16[32,32,256]{2,1,0:T(8,128)(2,1)S(1)}, u32[]{:S(2)}, u32[]{:S(2)}) async-start(bf16[32,32,256]{2,1,0:T(8,128)(2,1)} %get-tuple-element.40), calls=%async_computation | async-start | bytes 1048576 | tf_op jit(solution)/shard_map/all_to_all | solution.py:386
  12.8 0.0 copy-start.10
  12.8 0.0 copy-done.2
  12.8 0.0 copy-done
  12.8 0.0 copy-done.1
  12.8 0.0 copy-done.5
  12.8 0.0 copy-done.8
  12.8 0.0 copy-done.9
  12.9 0.6 copy-done.10
  13.4 1.0 %copy-done.6 = bf16[8,256,128]{2,1,0:T(8,128)(2,1)S(1)} copy-done((bf16[8,256,128]{2,1,0:T(8,128)(2,1)S(1)}, bf16[8,256,128]{2,1,0:T(8,128)(2,1)}, u32[]{:S(2)}) %copy-start.6) | copy-done | bytes 524312
  14.5 1.0 shard_map.185
  15.5 0.0 copy-start.3
  15.5 0.8 copy-done.3
  16.3 8.1 %all-to-all-done.lr = bf16[32,32,256]{2,1,0:T(8,128)(2,1)S(1)} async-done(((bf16[32,32,256]{2,1,0:T(8,128)(2,1)}), bf16[32,32,256]{2,1,0:T(8,128)(2,1)S(1)}, u32[]{:S(2)}, u32[]{:S(2)}) %all-to-all-start) | async-done | bytes 524320 | tf_op jit(solution)/shard_map/all_to_all | solution.py:386
  24.4 0.3 shard_map.186
  24.6 0.0 copy-start.7
  24.7 13.2 %all_to_all.25.tri = bf16[32,16,256]{2,1,0:T(8,128)(2,1)S(1)} all-to-all(bf16[32,16,256]{2,1,0:T(8,128)(2,1)S(1)} %get-tuple-element.49), channel_id=1, replica_groups=mesh['tmpl'=4,'row'=32] {'row'}, dimensions={0} | all-to-all | bytes 524288 | tf_op jit(solution)/shard_map/all_to_all | solution.py:392
  37.9 0.0 copy-done.4
  37.9 1.3 %shard_map.187 = (f32[8,8,256]{2,1,0:T(8,128)S(1)}, f32[8,64,256]{2,1,0:T(8,128)S(1)}, f32[8,64,256]{2,1,0:T(8,128)S(1)}, f32[8,64,256]{2,1,0:T(8,128)S(1)}, bf1...) custom-call(bf16[32,16,256]{2,1,0:T(8,128)(2,1)S(1)} %all_to_all.25.tri, f32[8,64,256]{2,1,0:T(8,128)S(1)} %copy-done, ...), custom_call_target="tpu_custom_call" | custom-call | tf_op jit(solution)/shard_map/pallas_call | solution.py:393
  39.2 7.8 %all-gather = f32[32,8,256]{2,1,0:T(8,128)S(1)} all-gather(f32[8,8,256]{2,1,0:T(8,128)S(1)} %get-tuple-element.54), channel_id=2, replica_groups=mesh['tmpl'=4,'row'=32] {'tmpl'}, dimensions={0}, use_global_device_ids=true | all-gather | bytes 327680 | tf_op jit(solution)/shard_map/all_gather | solution.py:399
  47.0 1.0 shard_map.188
  48.0 0.4 collective-permute-start
  48.4 12.8 %all_to_all.26.dtri = bf16[32,16,256]{2,1,0:T(8,128)(2,1)S(1)} all-to-all(bf16[32,16,256]{2,1,0:T(8,128)(2,1)S(1)} %get-tuple-element.60), channel_id=1, replica_groups=mesh['tmpl'=4,'row'=32] {'row'}, dimensions={0} | all-to-all | bytes 524288 | tf_op jit(solution)/shard_map/all_to_all | solution.py:407
  61.2 0.0 collective-permute-done.near
  61.2 0.3 shard_map.189
  61.6 14.5 %all_to_all.27.dlr = bf16[32,32,256]{2,1,0:T(8,128)(2,1)S(1)} all-to-all(bf16[32,32,256]{2,1,0:T(8,128)(2,1)S(1)} %get-tuple-element.63), channel_id=1, replica_groups=mesh['tmpl'=4,'row'=32] {'row'}, dimensions={0} | all-to-all | bytes 1048576 | tf_op jit(solution)/shard_map/all_to_all | solution.py:409
  76.0 3.3 %collective-permute-start.3 = (bf16[4,64,256]{2,1,0:T(8,128)(2,1)S(1)}, bf16[4,64,256]{2,1,0:T(8,128)(2,1)S(1)}, u32[]{:S(2)}, u32[]{:S(2)}) collective-permute-start(bf16[4,64,256]{2,1,0:T(8,128)(2,1)S(1)} %get-tuple-element.71), channel_id=1, source_target_pairs={{0,64},{32,96},{64,0},{96,32},{1,65},{33,97},{65,1},{97,33},{2,66}... | collective-permute-start | bytes 393224 | tf_op jit(solution)/shard_map/ppermute | solution.py:354
  79.3 0.8 shard_map.190
  80.1 0.1 collective-permute-start.1
  80.2 1.2 %collective-permute-done.1 = f32[64,128]{1,0:T(8,128)S(1)} collective-permute-done((f32[64,128]{1,0:T(8,128)S(1)}, f32[64,128]{1,0:T(8,128)S(1)}, u32[]{:S(2)}, u32[]{:S(2)}) %collective-permute-start.1) | collective-permute-done | bytes 32800 | tf_op jit(solution)/shard_map/ppermute | solution.py:354
  81.4 0.3 collective-permute-start.2
  81.7 1.2 %shard_map.192 = f32[8,64,256]{2,1,0:T(8,128)} custom-call(bf16[8,128,256]{2,1,0:T(8,128)(2,1)S(1)} %get-tuple-element.68.d, f32[8,64,256]{2,1,0:T(8,128)S(1)} %copy-done, f32[8,64,256]{2,1,0:T(8,128)S(1)} %get-tuple-element.69.d_y, bf16[8,64,256]{2,1,0:T(8,128)(2,1)S(1)} %get-tuple-element.70.d_gate, bf16[64,1024]{1,0:T(8,128)(2,1)S(1)} %copy-done.1, ...), custom_call_target="tpu_custom_call" | custom-call | tf_op jit(solution)/shard_map/pallas_call | solution.py:414
  82.9 3.9 %collective-permute-done.2.far = f32[64,128]{1,0:T(8,128)S(1)} collective-permute-done((f32[64,128]{1,0:T(8,128)S(1)}, f32[64,128]{1,0:T(8,128)S(1)}, u32[]{:S(2)}, u32[]{:S(2)}) %collective-permute-start.2) | collective-permute-done | bytes 32800 | tf_op jit(solution)/shard_map/ppermute | solution.py:354
  86.9 0.9 shard_map.191
  87.7 0.0 collective-permute-done.3
  87.8 4.1 %all-to-all-start.4 = ((bf16[32,64,128]{2,1,0:T(8,128)(2,1)}), bf16[32,64,128]{2,1,0:T(8,128)(2,1)S(1)}, u32[]{:S(2)}, u32[]{:S(2)}) async-start(bf16[32,64,128]{2,1,0:T(8,128)(2,1)} %shard_map.191), calls=%async_computation.4 | async-start | bytes 1048576 | tf_op jit(solution)/shard_map/all_to_all | solution.py:418
  91.9 0.1 collective-permute-start.4
  92.0 1.3 %collective-permute-done.4.other = bf16[4,64,256]{2,1,0:T(8,128)(2,1)S(1)} collective-permute-done((bf16[4,64,256]{2,1,0:T(8,128)(2,1)S(1)}, bf16[4,64,256]{2,1,0:T(8,128)(2,1)S(1)}, u32[]{:S(2)}, u32[]{:S(2)}) %collective-permute-start.4) | collective-permute-done | bytes 131104 | tf_op jit(solution)/shard_map/ppermute | solution.py:354
  93.3 2.9 %shard_map.193 = f32[8,256,128]{2,1,0:T(8,128)} custom-call(bf16[4,64,256]{2,1,0:T(8,128)(2,1)S(1)} %add.7.own, bf16[4,64,256]{2,1,0:T(8,128)(2,1)S(1)} %collective-permute-done.4.other, bf16[8,256,128]{2,1,0:T(8,128)(2,1)S(1)} %copy-done.2, f32[1,128]{1,0:T(1,128)S(1)} %bitcast.18, bf16[64,128]{1,0:T(8,128)(2,1)S(1)} %bitcast.16), custom_call_target="tpu_custom_call" | custom-call | tf_op jit(solution)/shard_map/pallas_call | solution.py:420
  96.2 6.5 %all-to-all-done.4.parts = bf16[32,64,128]{2,1,0:T(8,128)(2,1)S(1)} async-done(((bf16[32,64,128]{2,1,0:T(8,128)(2,1)}), bf16[32,64,128]{2,1,0:T(8,128)(2,1)S(1)}, u32[]{:S(2)}, u32[]{:S(2)}) %all-to-all-start.4) | async-done | bytes 524320 | tf_op jit(solution)/shard_map/all_to_all | solution.py:418
  102.7 0.8 shard_map.194
  (5 shorter events, 0.0 us)
Async XLA Ops:
  0.6 12.2 %copy-start.2 = (bf16[8,256,128]{2,1,0:T(8,128)(2,1)S(1)}, bf16[8,256,128]{2,1,0:T(8,128)(2,1)}, u32[]{:S(2)}) copy-start(bf16[8,256,128]{2,1,0:T(8,128)(2,1)} %query_h.1) | copy-start | bytes 1572868
  3.8 9.0 %copy-start = (f32[8,64,256]{2,1,0:T(8,128)S(1)}, f32[8,64,256]{2,1,0:T(8,128)}, u32[]{:S(2)}) copy-start(f32[8,64,256]{2,1,0:T(8,128)} %get-tuple-element.41.z) | copy-start | bytes 1572868
  3.8 9.0 %copy-start.1 = (bf16[64,1024]{1,0:T(8,128)(2,1)S(1)}, bf16[64,1024]{1,0:T(8,128)(2,1)}, u32[]{:S(2)}) copy-start(bf16[64,1024]{1,0:T(8,128)(2,1)} %get-tuple-element.42.weights) | copy-start | bytes 393220
  3.8 9.0 %copy-start.5 = (f32[3,64,128]{2,1,0:T(8,128)S(1)}, f32[3,64,128]{2,1,0:T(8,128)}, u32[]{:S(2)}) copy-start(f32[3,64,128]{2,1,0:T(8,128)} %get-tuple-element.43.gains) | copy-start | bytes 294916
  3.8 9.0 %copy-start.8 = (bf16[128,64]{0,1:T(8,128)(2,1)S(1)}, bf16[128,64]{0,1:T(8,128)(2,1)}, u32[]{:S(2)}) copy-start(bf16[128,64]{0,1:T(8,128)(2,1)} %param.31) | copy-start | bytes 49156
  3.9 9.0 %copy-start.9 = (bf16[64,128]{1,0:T(8,128)(2,1)S(1)}, bf16[64,128]{1,0:T(8,128)(2,1)}, u32[]{:S(2)}) copy-start(bf16[64,128]{1,0:T(8,128)(2,1)} %wao.1) | copy-start | bytes 49156
  3.9 20.5 %all-to-all-start = ((bf16[32,32,256]{2,1,0:T(8,128)(2,1)}), bf16[32,32,256]{2,1,0:T(8,128)(2,1)S(1)}, u32[]{:S(2)}, u32[]{:S(2)}) async-start(bf16[32,32,256]{2,1,0:T(8,128)(2,1)} %get-tuple-element.40), calls=%async_computation | async-start | bytes 1048576 | tf_op jit(solution)/shard_map/all_to_all | solution.py:386
  12.8 0.7 copy-start.10
  13.4 1.0 %copy-start.6 = (bf16[8,256,128]{2,1,0:T(8,128)(2,1)S(1)}, bf16[8,256,128]{2,1,0:T(8,128)(2,1)}, u32[]{:S(2)}) copy-start(bf16[8,256,128]{2,1,0:T(8,128)(2,1)} %cot.1) | copy-start | bytes 1572868
  15.5 0.8 copy-start.3
  24.4 13.5 %copy-start.4 = (f32[8,64,256]{2,1,0:T(8,128)S(1)}, f32[8,64,256]{2,1,0:T(8,128)}, u32[]{:S(2)}) copy-start(f32[8,64,256]{2,1,0:T(8,128)} %copy-done.3) | copy-start | bytes 1572868
  24.6 13.2 %copy-start.7 = (f32[8,1,256]{2,1,0:T(1,128)S(1)}, f32[8,1,256]{2,1,0:T(1,128)}, u32[]{:S(2)}) copy-start(f32[8,1,256]{2,1,0:T(1,128)} %get-tuple-element.53.pm) | copy-start | bytes 24580
  48.0 13.2 %collective-permute-start = (bf16[8,64,256]{2,1,0:T(8,128)(2,1)S(1)}, bf16[8,64,256]{2,1,0:T(8,128)(2,1)S(1)}, u32[]{:S(2)}, u32[]{:S(2)}) collective-permute-start(bf16[8,64,256]{2,1,0:T(8,128)(2,1)S(1)} %get-tuple-element.62.dqh), channel_id=1, source_target_pairs={{0,32},{32,0},{64,96},{96,64},{1,33},{33,1},{65,97},{97,65},{2,34}... | collective-permute-start | bytes 786440 | tf_op jit(solution)/shard_map/ppermute | solution.py:354
  76.0 11.7 %collective-permute-start.3 = (bf16[4,64,256]{2,1,0:T(8,128)(2,1)S(1)}, bf16[4,64,256]{2,1,0:T(8,128)(2,1)S(1)}, u32[]{:S(2)}, u32[]{:S(2)}) collective-permute-start(bf16[4,64,256]{2,1,0:T(8,128)(2,1)S(1)} %get-tuple-element.71), channel_id=1, source_target_pairs={{0,64},{32,96},{64,0},{96,32},{1,65},{33,97},{65,1},{97,33},{2,66}... | collective-permute-start | bytes 393224 | tf_op jit(solution)/shard_map/ppermute | solution.py:354
  80.1 1.3 %collective-permute-start.1 = (f32[64,128]{1,0:T(8,128)S(1)}, f32[64,128]{1,0:T(8,128)S(1)}, u32[]{:S(2)}, u32[]{:S(2)}) collective-permute-start(f32[64,128]{1,0:T(8,128)S(1)} %get-tuple-element.67), channel_id=1, source_target_pairs={{0,32},{32,0},{64,96},{96,64},{1,33},{33,1},{65,97},{97,65},{2,34}... | collective-permute-start | bytes 98312 | tf_op jit(solution)/shard_map/ppermute | solution.py:354
  81.4 5.4 %collective-permute-start.2 = (f32[64,128]{1,0:T(8,128)S(1)}, f32[64,128]{1,0:T(8,128)S(1)}, u32[]{:S(2)}, u32[]{:S(2)}) collective-permute-start(f32[64,128]{1,0:T(8,128)S(1)} %add.6.own), channel_id=1, source_target_pairs={{0,64},{32,96},{64,0},{96,32},{1,65},{33,97},{65,1},{97,33},{2,66}... | collective-permute-start | bytes 98312 | tf_op jit(solution)/shard_map/ppermute | solution.py:354
  87.8 15.0 %all-to-all-start.4 = ((bf16[32,64,128]{2,1,0:T(8,128)(2,1)}), bf16[32,64,128]{2,1,0:T(8,128)(2,1)S(1)}, u32[]{:S(2)}, u32[]{:S(2)}) async-start(bf16[32,64,128]{2,1,0:T(8,128)(2,1)} %shard_map.191), calls=%async_computation.4 | async-start | bytes 1048576 | tf_op jit(solution)/shard_map/all_to_all | solution.py:418
  91.9 1.4 %collective-permute-start.4 = (bf16[4,64,256]{2,1,0:T(8,128)(2,1)S(1)}, bf16[4,64,256]{2,1,0:T(8,128)(2,1)S(1)}, u32[]{:S(2)}, u32[]{:S(2)}) collective-permute-start(bf16[4,64,256]{2,1,0:T(8,128)(2,1)S(1)} %add.7.own), channel_id=1, source_target_pairs={{0,32},{32,0},{64,96},{96,64},{1,33},{33,1},{65,97},{97,65},{2,34}... | collective-permute-start | bytes 393224 | tf_op jit(solution)/shard_map/ppermute | solution.py:354

commit v5 on v4

--- a/solution.py
+++ b/solution.py
@@ -17,7 +17,8 @@
 SHARDS = 32
 UNROLL = 8
 HALF = ROWS // 2
-ANY = pl.BlockSpec(memory_space=pltpu.HBM)
+PIECES = 4
+HBM = pl.BlockSpec(memory_space=pltpu.HBM)
 VMEM = pl.BlockSpec(memory_space=pltpu.VMEM)
 
 
@@ -73,7 +74,8 @@
 
 def pack(spread, out):
     for half in range(2):
-        out[:, :, 128 * half : 128 * half + 128] = spread[half].reshape(out.shape[0], out.shape[1], 128).astype(BF16)
+        rows = spread[half, : out.shape[0] * out.shape[1]]
+        out[:, :, 128 * half : 128 * half + 128] = rows.reshape(out.shape[0], out.shape[1], 128).astype(BF16)
 
 
 def take_rows(wide, first, step):
@@ -81,8 +83,9 @@
 
 
 def unpack(x, wide):
+    rows = x.shape[0] * x.shape[1]
     for half in range(2):
-        wide[half] = x[:, :, 128 * half : 128 * half + 128].astype(F32).reshape(wide.shape[1], 128)
+        wide[half, :rows] = x[:, :, 128 * half : 128 * half + 128].astype(F32).reshape(rows, 128)
 
 
 def place(rows_ref):
@@ -122,15 +125,16 @@
 
 
 def project_kernel(*refs):
-    sources, outs, places = refs[:14], refs[14:19], refs[28:]
-    lhs, normed, lr, z, pm, weights, gains, out_sems, sems = refs[19:28]
-    lr_out, z_out, pm_out, weights_out, gains_out = outs
+    sources, outs, places = refs[:14], refs[14:19], refs[22:]
+    lhs, normed, sems = refs[19:22]
+    lr, z, pm, weights, gains = outs
     arriving = copies(sources, places, sems)
     wl, wr, norm_gain, table_t, res, res_s, mask, mask_s, pair, wg, wo, wkv, tri_gain, pair_gain = places
     arrive(arriving[:2])
     for pair_of, tile in enumerate(owner_rows(flip(wl[...]), flip(wr[...]))):
-        for q in range(4):
-            lhs[:, 8 * q : 8 * q + 8, 128 * pair_of : 128 * pair_of + 128] = tile[q].astype(BF16)
+        for side in range(2):
+            both = jnp.concatenate([tile[2 * side], tile[2 * side + 1]], axis=1)
+            lhs[:, 16 * side : 16 * side + 16, 128 * pair_of : 128 * pair_of + 128] = both.astype(BF16)
     arrive(arriving[2:9])
     t, start, mask_row = place(mask)
     table, residues, gain = table_t[...], res[...], column(norm_gain[...])
@@ -145,9 +149,6 @@
         return carry
 
     each_row(body)
-    both = dot(lhs[...].reshape(SHARDS * 32, ROWS * C), normed[...]).reshape(SHARDS * 4, ROWS, N)
-    lr[...] = (both * pm[...].reshape(1, ROWS, N)).reshape(SHARDS, 32, N).astype(BF16)
-    leaving = copies((lr, z, pm), (lr_out, z_out, pm_out), out_sems)
     arrive(arriving[9:])
     blank = jnp.zeros((C, C), BF16)
     wkv_t = flip(wkv[...]).astype(BF16)
@@ -157,8 +158,11 @@
     gains[0] = gain
     gains[1] = column(tri_gain[...])
     gains[2] = column(pair_gain[...])
-    leaving += copies((weights, gains), (weights_out, gains_out), out_sems, 3)
-    arrive(leaving)
+    some = SHARDS // PIECES
+    for p in range(PIECES):
+        owners = slice(p * some, (p + 1) * some)
+        both = dot(lhs[owners].reshape(some * 32, ROWS * C), normed[...]).reshape(some * 4, ROWS, N)
+        lr[owners] = (both * pm[...].reshape(1, ROWS, N)).reshape(some, 32, N).astype(BF16)
 
 
 def prepare_kernel(z, weights, gains, query, cot, q_gain, wq_t, wao, ln_out, qh_out, do_out, gate_out):
@@ -343,11 +347,15 @@
 
 
 def wide_scratch(rows):
-    return pltpu.VMEM((2, rows, 128), F32)
+    return pltpu.VMEM((2, rows + rows // SHARDS, 128), F32)
 
 
 def fetched(*arrays):
     return [pltpu.SemaphoreType.DMA((len(arrays),))] + [pltpu.VMEM(a.shape, a.dtype) for a in arrays]
+
+
+def stay(*arrays):
+    return [pltpu.with_memory_space_constraint(a, pltpu.HBM) for a in arrays]
 
 
 def swap(x, bit):
@@ -374,15 +382,12 @@
     for n in (5, 7):
         scratch[1 + n] = pltpu.SMEM(sources[n].shape, sources[n].dtype)
     outs = [((SHARDS, 32, N), BF16), (plane, F32), ((ROWS, 1, N), F32), ((C, 8 * 128), BF16), ((3, C, 128), F32)]
-    held = [pltpu.VMEM(*o) for o in outs] + [pltpu.SemaphoreType.DMA((len(outs),))]
     lr, z, pm, weights, gains = call(
         project_kernel,
         outs,
-        [ANY] * 14,
-        [pltpu.VMEM((SHARDS, 32, ROWS * C), BF16), pltpu.VMEM((ROWS * C, N), BF16)] + held + scratch,
-        vmem=62,
-        home=ANY,
-    )(*sources)
+        [HBM] * 14,
+        [pltpu.VMEM((SHARDS, 32, ROWS * C), BF16), pltpu.VMEM((ROWS * C, N), BF16)] + scratch,
+    )(*stay(*sources))
     lr_all = every(lr)
     prepared = call(prepare_kernel, [(plane, BF16)] + [(plane, F32)] * 3, [VMEM] * 8)(
         z, weights, gains, query_pair, cotangent, row(query_gain), query_weight.T, attn_out_weight
@@ -418,7 +423,7 @@
     parts = every(fan)
     sources = (query_pair, row(query_gain), query_weight.T)
     (query_grad,) = call(
-        query_grad_kernel, [((ROWS, N, 2 * C), F32)], [VMEM] * 2 + [ANY] * 3, fetched(*sources)
+        query_grad_kernel, [((ROWS, N, 2 * C), F32)], [VMEM] * 2 + [HBM] * 3, fetched(*sources)
     )(own, swap(own, 1), *sources)
     parts, query_grad = after(parts, query_grad)
     (proj,) = call(sum_kernel, [((2, C, C), F32)], [VMEM])(parts)

time: 104 us -> 104 us (level)
    unnamed x22 -> x14, local copies, waits for them, and re-layouts: 2.46 us -> 2.38 us
where the time goes in v5:
time: 104 us; the launch traced here: 103 us
  blocking collectives  48.4 us (47%)
  waiting for transfers between devices  21.2 us (20%)
  starting transfers between devices  17.1 us (16%)
  Pallas kernels  13.3 us (13%)
  local copies, waits for them, and re-layouts  2.38 us (2%)
    all_to_all x1, blocking collectives, local(): dlr, keep = after(every(dlr), keep)  14.6 us
    all_to_all x1, blocking collectives, local(): tri = every(tri)  13.2 us
    all_to_all x1, blocking collectives, local(): every(dtri)  12.8 us
    all_to_all x1, starting transfers between devices, local(): lr_all = every(lr)  8.9 us
    all_to_all x1, waiting for transfers between devices, local(): lr_all = every(lr)  8.21 us
    all_gather x1, blocking collectives, local(): sg = lax.all_gather(sg, 'tmpl')  7.84 us
    all_to_all x1, waiting for transfers between devices, local(): parts = every(fan)  6.51 us
    ppermute x5, waiting for transfers between devices, swap(): return lax.ppermute(x, 'tmpl', [(i, i ^ bit) for i in range(4)])  6.46 us
  transfers between devices with their start and end apart: 7, of which 5 were waited for; matrix products, arithmetic and copies ran while one was open for 0% of the time, Pallas kernels for 7%

profile of v5, /device:TPU:0, one launch (start us, length us, event | category | flops | bytes accessed | tf_op | source)
XLA Modules:
  0.0 103.3 jit_solution(4182895373408541176)
XLA Ops:
  0.6 2.9 %shard_map.184 = (bf16[32,32,256]{2,1,0:T(8,128)(2,1)}, f32[8,64,256]{2,1,0:T(8,128)S(1)}, f32[8,1,256]{2,1,0:T(1,128)S(1)}, bf16[64,1024]{1,0:T(8,128)(2,1)S(1)}, f32[3,64,128]{2,1,0:T(8,128)S(1)}) custom-call(bf16[64,64]{1,0:T(8,128)(2,1)} %refs_0_.1, bf16[64,64]{1,0:T(8,128)(2,1)} %refs_1_.1, f32[1,64]{1,0:T(1,128)} %bitcast.23, ...), custom_call_target="tpu_custom_call" | custom-call | tf_op jit(solution)/shard_map/pallas_call | solution.py:385
  3.5 0.0 copy-start
  3.5 0.0 copy-start.4
  3.5 0.0 copy-start.5
  3.5 8.9 %all-to-all-start = ((bf16[32,32,256]{2,1,0:T(8,128)(2,1)}), bf16[32,32,256]{2,1,0:T(8,128)(2,1)S(1)}, u32[]{:S(2)}, u32[]{:S(2)}) async-start(bf16[32,32,256]{2,1,0:T(8,128)(2,1)} %get-tuple-element.40), calls=%async_computation | async-start | bytes 1048576 | tf_op jit(solution)/shard_map/all_to_all | solution.py:391
  12.5 0.0 copy-start.6
  12.5 0.0 copy-done
  12.5 0.0 copy-done.4
  12.5 0.0 copy-done.5
  12.5 0.6 copy-done.6
  13.1 0.0 copy-start.1
  13.1 1.0 %copy-done.1 = bf16[8,256,128]{2,1,0:T(8,128)(2,1)S(1)} copy-done((bf16[8,256,128]{2,1,0:T(8,128)(2,1)S(1)}, bf16[8,256,128]{2,1,0:T(8,128)(2,1)}, u32[]{:S(2)}) %copy-start.1) | copy-done | bytes 524312
  14.2 1.0 shard_map.185
  15.1 0.0 copy-start.2
  15.1 0.7 copy-done.2
  15.8 8.2 %all-to-all-done.lr = bf16[32,32,256]{2,1,0:T(8,128)(2,1)S(1)} async-done(((bf16[32,32,256]{2,1,0:T(8,128)(2,1)}), bf16[32,32,256]{2,1,0:T(8,128)(2,1)S(1)}, u32[]{:S(2)}, u32[]{:S(2)}) %all-to-all-start) | async-done | bytes 524320 | tf_op jit(solution)/shard_map/all_to_all | solution.py:391
  24.0 0.3 shard_map.186
  24.3 13.2 %all_to_all.25.tri = bf16[32,16,256]{2,1,0:T(8,128)(2,1)S(1)} all-to-all(bf16[32,16,256]{2,1,0:T(8,128)(2,1)S(1)} %get-tuple-element.49), channel_id=1, replica_groups=mesh['tmpl'=4,'row'=32] {'row'}, dimensions={0} | all-to-all | bytes 524288 | tf_op jit(solution)/shard_map/all_to_all | solution.py:397
  37.5 1.3 %shard_map.187 = (f32[8,8,256]{2,1,0:T(8,128)S(1)}, f32[8,64,256]{2,1,0:T(8,128)S(1)}, f32[8,64,256]{2,1,0:T(8,128)S(1)}, f32[8,64,256]{2,1,0:T(8,128)S(1)}, bf1...) custom-call(bf16[32,16,256]{2,1,0:T(8,128)(2,1)S(1)} %all_to_all.25.tri, f32[8,64,256]{2,1,0:T(8,128)S(1)} %get-tuple-element.41.z, ...), custom_call_target="tpu_custom_call" | custom-call | tf_op jit(solution)/shard_map/pallas_call | solution.py:398
  38.8 7.8 %all-gather = f32[32,8,256]{2,1,0:T(8,128)S(1)} all-gather(f32[8,8,256]{2,1,0:T(8,128)S(1)} %get-tuple-element.54), channel_id=2, replica_groups=mesh['tmpl'=4,'row'=32] {'tmpl'}, dimensions={0}, use_global_device_ids=true | all-gather | bytes 327680 | tf_op jit(solution)/shard_map/all_gather | solution.py:404
  46.7 1.0 shard_map.188
  47.6 0.4 collective-permute-start
  48.1 12.8 %all_to_all.26.dtri = bf16[32,16,256]{2,1,0:T(8,128)(2,1)S(1)} all-to-all(bf16[32,16,256]{2,1,0:T(8,128)(2,1)S(1)} %get-tuple-element.60), channel_id=1, replica_groups=mesh['tmpl'=4,'row'=32] {'row'}, dimensions={0} | all-to-all | bytes 524288 | tf_op jit(solution)/shard_map/all_to_all | solution.py:412
  60.9 0.0 collective-permute-done.near
  60.9 0.3 shard_map.189
  61.2 0.0 copy-start.3
  61.2 14.6 %all_to_all.27.dlr = bf16[32,32,256]{2,1,0:T(8,128)(2,1)S(1)} all-to-all(bf16[32,32,256]{2,1,0:T(8,128)(2,1)S(1)} %get-tuple-element.63), channel_id=1, replica_groups=mesh['tmpl'=4,'row'=32] {'row'}, dimensions={0} | all-to-all | bytes 1048576 | tf_op jit(solution)/shard_map/all_to_all | solution.py:414
  75.8 3.3 %collective-permute-start.3 = (bf16[4,64,256]{2,1,0:T(8,128)(2,1)S(1)}, bf16[4,64,256]{2,1,0:T(8,128)(2,1)S(1)}, u32[]{:S(2)}, u32[]{:S(2)}) collective-permute-start(bf16[4,64,256]{2,1,0:T(8,128)(2,1)S(1)} %get-tuple-element.71), channel_id=1, source_target_pairs={{0,64},{32,96},{64,0},{96,32},{1,65},{33,97},{65,1},{97,33},{2,66}... | collective-permute-start | bytes 393224 | tf_op jit(solution)/shard_map/ppermute | solution.py:362
  79.1 0.0 copy-done.3
  79.1 0.8 shard_map.190
  79.9 0.1 collective-permute-start.1
  80.0 1.2 %collective-permute-done.1 = f32[64,128]{1,0:T(8,128)S(1)} collective-permute-done((f32[64,128]{1,0:T(8,128)S(1)}, f32[64,128]{1,0:T(8,128)S(1)}, u32[]{:S(2)}, u32[]{:S(2)}) %collective-permute-start.1) | collective-permute-done | bytes 32800 | tf_op jit(solution)/shard_map/ppermute | solution.py:362
  81.2 0.2 collective-permute-start.2
  81.5 1.2 %shard_map.192 = f32[8,64,256]{2,1,0:T(8,128)} custom-call(bf16[8,128,256]{2,1,0:T(8,128)(2,1)S(1)} %get-tuple-element.68.d, f32[8,64,256]{2,1,0:T(8,128)S(1)} %get-tuple-element.41.z, f32[8,64,256]{2,1,0:T(8,128)S(1)} %get-tuple-element.69.d_y, bf16[8,64,256]{2,1,0:T(8,128)(2,1)S(1)} %get-tuple-element.70.d_gate, ...), custom_call_target="tpu_custom_call" | custom-call | tf_op jit(solution)/shard_map/pallas_call | solution.py:419
  82.7 3.9 %collective-permute-done.2.far = f32[64,128]{1,0:T(8,128)S(1)} collective-permute-done((f32[64,128]{1,0:T(8,128)S(1)}, f32[64,128]{1,0:T(8,128)S(1)}, u32[]{:S(2)}, u32[]{:S(2)}) %collective-permute-start.2) | collective-permute-done | bytes 32800 | tf_op jit(solution)/shard_map/ppermute | solution.py:362
  86.7 0.9 shard_map.191
  87.5 0.0 collective-permute-done.3
  87.6 4.1 %all-to-all-start.4 = ((bf16[32,64,128]{2,1,0:T(8,128)(2,1)}), bf16[32,64,128]{2,1,0:T(8,128)(2,1)S(1)}, u32[]{:S(2)}, u32[]{:S(2)}) async-start(bf16[32,64,128]{2,1,0:T(8,128)(2,1)} %shard_map.191), calls=%async_computation.4 | async-start | bytes 1048576 | tf_op jit(solution)/shard_map/all_to_all | solution.py:423
  91.7 0.1 collective-permute-start.4
  91.8 1.3 %collective-permute-done.4.other = bf16[4,64,256]{2,1,0:T(8,128)(2,1)S(1)} collective-permute-done((bf16[4,64,256]{2,1,0:T(8,128)(2,1)S(1)}, bf16[4,64,256]{2,1,0:T(8,128)(2,1)S(1)}, u32[]{:S(2)}, u32[]{:S(2)}) %collective-permute-start.4) | collective-permute-done | bytes 131104 | tf_op jit(solution)/shard_map/ppermute | solution.py:362
  93.1 2.9 %shard_map.193 = f32[8,256,128]{2,1,0:T(8,128)} custom-call(bf16[4,64,256]{2,1,0:T(8,128)(2,1)S(1)} %add.7.own, bf16[4,64,256]{2,1,0:T(8,128)(2,1)S(1)} %collective-permute-done.4.other, bf16[8,256,128]{2,1,0:T(8,128)(2,1)S(1)} %copy-done, f32[1,128]{1,0:T(1,128)S(1)} %bitcast.18, bf16[64,128]{1,0:T(8,128)(2,1)S(1)} %bitcast.16), custom_call_target="tpu_custom_call" | custom-call | tf_op jit(solution)/shard_map/pallas_call | solution.py:425
  96.0 6.5 %all-to-all-done.4.parts = bf16[32,64,128]{2,1,0:T(8,128)(2,1)S(1)} async-done(((bf16[32,64,128]{2,1,0:T(8,128)(2,1)}), bf16[32,64,128]{2,1,0:T(8,128)(2,1)S(1)}, u32[]{:S(2)}, u32[]{:S(2)}) %all-to-all-start.4) | async-done | bytes 524320 | tf_op jit(solution)/shard_map/all_to_all | solution.py:423
  102.5 0.8 shard_map.194
  (2 shorter events, 0.0 us)
Async XLA Ops:
  3.5 9.0 %copy-start = (bf16[8,256,128]{2,1,0:T(8,128)(2,1)S(1)}, bf16[8,256,128]{2,1,0:T(8,128)(2,1)}, u32[]{:S(2)}) copy-start(bf16[8,256,128]{2,1,0:T(8,128)(2,1)} %query_h.1) | copy-start | bytes 1572868
  3.5 9.0 %copy-start.4 = (bf16[128,64]{0,1:T(8,128)(2,1)S(1)}, bf16[128,64]{0,1:T(8,128)(2,1)}, u32[]{:S(2)}) copy-start(bf16[128,64]{0,1:T(8,128)(2,1)} %param.31) | copy-start | bytes 49156
  3.5 9.0 %copy-start.5 = (bf16[64,128]{1,0:T(8,128)(2,1)S(1)}, bf16[64,128]{1,0:T(8,128)(2,1)}, u32[]{:S(2)}) copy-start(bf16[64,128]{1,0:T(8,128)(2,1)} %wao.1) | copy-start | bytes 49156
  3.5 20.5 %all-to-all-start = ((bf16[32,32,256]{2,1,0:T(8,128)(2,1)}), bf16[32,32,256]{2,1,0:T(8,128)(2,1)S(1)}, u32[]{:S(2)}, u32[]{:S(2)}) async-start(bf16[32,32,256]{2,1,0:T(8,128)(2,1)} %get-tuple-element.40), calls=%async_computation | async-start | bytes 1048576 | tf_op jit(solution)/shard_map/all_to_all | solution.py:391
  12.5 0.7 copy-start.6
  13.1 1.0 %copy-start.1 = (bf16[8,256,128]{2,1,0:T(8,128)(2,1)S(1)}, bf16[8,256,128]{2,1,0:T(8,128)(2,1)}, u32[]{:S(2)}) copy-start(bf16[8,256,128]{2,1,0:T(8,128)(2,1)} %cot.1) | copy-start | bytes 1572868
  15.1 0.7 copy-start.2
  47.6 13.2 %collective-permute-start = (bf16[8,64,256]{2,1,0:T(8,128)(2,1)S(1)}, bf16[8,64,256]{2,1,0:T(8,128)(2,1)S(1)}, u32[]{:S(2)}, u32[]{:S(2)}) collective-permute-start(bf16[8,64,256]{2,1,0:T(8,128)(2,1)S(1)} %get-tuple-element.62.dqh), channel_id=1, source_target_pairs={{0,32},{32,0},{64,96},{96,64},{1,33},{33,1},{65,97},{97,65},{2,34}... | collective-permute-start | bytes 786440 | tf_op jit(solution)/shard_map/ppermute | solution.py:362
  61.2 17.9 %copy-start.3 = (bf16[8,64,256]{2,1,0:T(8,128)(2,1)S(1)}, bf16[8,64,256]{2,1,0:T(8,128)(2,1)}, u32[]{:S(2)}) copy-start(bf16[8,64,256]{2,1,0:T(8,128)(2,1)} %copy-done.2) | copy-start | bytes 786436
  75.8 11.7 %collective-permute-start.3 = (bf16[4,64,256]{2,1,0:T(8,128)(2,1)S(1)}, bf16[4,64,256]{2,1,0:T(8,128)(2,1)S(1)}, u32[]{:S(2)}, u32[]{:S(2)}) collective-permute-start(bf16[4,64,256]{2,1,0:T(8,128)(2,1)S(1)} %get-tuple-element.71), channel_id=1, source_target_pairs={{0,64},{32,96},{64,0},{96,32},{1,65},{33,97},{65,1},{97,33},{2,66}... | collective-permute-start | bytes 393224 | tf_op jit(solution)/shard_map/ppermute | solution.py:362
  79.9 1.3 %collective-permute-start.1 = (f32[64,128]{1,0:T(8,128)S(1)}, f32[64,128]{1,0:T(8,128)S(1)}, u32[]{:S(2)}, u32[]{:S(2)}) collective-permute-start(f32[64,128]{1,0:T(8,128)S(1)} %get-tuple-element.67), channel_id=1, source_target_pairs={{0,32},{32,0},{64,96},{96,64},{1,33},{33,1},{65,97},{97,65},{2,34}... | collective-permute-start | bytes 98312 | tf_op jit(solution)/shard_map/ppermute | solution.py:362
  81.2 5.4 %collective-permute-start.2 = (f32[64,128]{1,0:T(8,128)S(1)}, f32[64,128]{1,0:T(8,128)S(1)}, u32[]{:S(2)}, u32[]{:S(2)}) collective-permute-start(f32[64,128]{1,0:T(8,128)S(1)} %add.6.own), channel_id=1, source_target_pairs={{0,64},{32,96},{64,0},{96,32},{1,65},{33,97},{65,1},{97,33},{2,66}... | collective-permute-start | bytes 98312 | tf_op jit(solution)/shard_map/ppermute | solution.py:362
  87.6 15.0 %all-to-all-start.4 = ((bf16[32,64,128]{2,1,0:T(8,128)(2,1)}), bf16[32,64,128]{2,1,0:T(8,128)(2,1)S(1)}, u32[]{:S(2)}, u32[]{:S(2)}) async-start(bf16[32,64,128]{2,1,0:T(8,128)(2,1)} %shard_map.191), calls=%async_computation.4 | async-start | bytes 1048576 | tf_op jit(solution)/shard_map/all_to_all | solution.py:423
  91.7 1.4 %collective-permute-start.4 = (bf16[4,64,256]{2,1,0:T(8,128)(2,1)S(1)}, bf16[4,64,256]{2,1,0:T(8,128)(2,1)S(1)}, u32[]{:S(2)}, u32[]{:S(2)}) collective-permute-start(bf16[4,64,256]{2,1,0:T(8,128)(2,1)S(1)} %add.7.own), channel_id=1, source_target_pairs={{0,32},{32,0},{64,96},{96,64},{1,33},{33,1},{65,97},{97,65},{2,34}... | collective-permute-start | bytes 393224 | tf_op jit(solution)/shard_map/ppermute | solution.py:362

commit v6 on v5

--- a/solution.py
+++ b/solution.py
@@ -26,6 +26,12 @@
     return lax.dot_general(a, b, (contract, ((), ())), preferred_element_type=F32)
 
 
+def fine_dot(a, x, contract=((1,), (0,))):
+    high = x.astype(BF16)
+    low = (x - high.astype(F32)).astype(BF16)
+    return dot(a, high, contract) + dot(a, low, contract)
+
+
 def flip(x):
     return x.astype(F32).T
 
@@ -125,11 +131,12 @@
 
 
 def project_kernel(*refs):
-    sources, outs, places = refs[:14], refs[14:19], refs[22:]
-    lhs, normed, sems = refs[19:22]
-    lr, z, pm, weights, gains = outs
+    sources, outs, places = refs[:19], refs[19:28], refs[30:]
+    lhs, sems = refs[28:30]
+    lr, z, pm, weights, gains, normed, qh_out, do_out, gate_out = outs
     arriving = copies(sources, places, sems)
-    wl, wr, norm_gain, table_t, res, res_s, mask, mask_s, pair, wg, wo, wkv, tri_gain, pair_gain = places
+    wl, wr, norm_gain, table_t, res, res_s, mask, mask_s, pair, wg, wo, wkv, tri_gain, pair_gain = places[:14]
+    query, cot, q_gain, wq_t, wao = places[14:]
     arrive(arriving[:2])
     for pair_of, tile in enumerate(owner_rows(flip(wl[...]), flip(wr[...]))):
         for side in range(2):
@@ -145,7 +152,7 @@
         z[i] = z_i
         pm_i = mask_row * mask_s[t, start + i].astype(F32)
         pm[i] = pm_i
-        normed[i * C : i * C + C, :] = (hat(z_i)[0] * g).astype(BF16)
+        normed[i] = (hat(z_i)[0] * g).astype(BF16)
         return carry
 
     each_row(body)
@@ -161,27 +168,23 @@
     some = SHARDS // PIECES
     for p in range(PIECES):
         owners = slice(p * some, (p + 1) * some)
-        both = dot(lhs[owners].reshape(some * 32, ROWS * C), normed[...]).reshape(some * 4, ROWS, N)
+        both = dot(lhs[owners].reshape(some * 32, ROWS * C), normed[...].reshape(ROWS * C, N)).reshape(some * 4, ROWS, N)
         lr[owners] = (both * pm[...].reshape(1, ROWS, N)).reshape(some, 32, N).astype(BF16)
 
-
-def prepare_kernel(z, weights, gains, query, cot, q_gain, wq_t, wao, ln_out, qh_out, do_out, gate_out):
-    wg_t, g = slab(weights, 7), twice(gains[0])
+    wg_t = flip(wg[...]).astype(BF16)
     wq_v, wao_v, g_query = wq_t[...], wao[...], q_gain[...]
 
-    def body(i, carry):
-        ln_b = (hat(z[i])[0] * g).astype(BF16)
-        ln_out[i] = ln_b
+    def heads(i, carry):
         x = query[i].astype(F32)
         cent = x - jnp.mean(x, -1, keepdims=True)
         var = jnp.mean(cent * cent, -1, keepdims=True)
-        qn = (cent * lax.rsqrt(var + 1e-05) * g_query).astype(BF16)
-        qh_out[i] = dot(wq_v, qn, ((1,), (1,))) * HEAD_DIM ** (-0.5)
+        qn = cent * lax.rsqrt(var + 1e-05) * g_query
+        qh_out[i] = fine_dot(wq_v, qn, ((1,), (1,))) * HEAD_DIM ** (-0.5)
         do_out[i] = dot(wao_v, cot[i], ((1,), (1,)))
-        gate_out[i] = jax.nn.sigmoid(dot(wg_t, ln_b))
-        return carry
-
-    each_row(body)
+        gate_out[i] = jax.nn.sigmoid(fine_dot(wg_t, hat(z[i])[0] * g))
+        return carry
+
+    each_row(heads)
 
 
 def tri_kernel(lr, tri_out, mats_out):
@@ -212,9 +215,9 @@
     def body(i, carry):
         tri_i = jnp.concatenate([take_rows(wide, i, 16), take_rows(wide, 8 + i, 16)], axis=0)
         that, rstd_t = hat(tri_i)
-        upd = dot(wo_t, (that * g_tri).astype(BF16))
+        upd = fine_dot(wo_t, that * g_tri)
         yhat, rstd_y = hat(z[i] + gate[i] * upd)
-        kv = dot(wkv_t, (yhat * g_pair).astype(BF16)).astype(BF16)
+        kv = fine_dot(wkv_t, yhat * g_pair).astype(BF16)
         kv_f = kv.astype(F32)
         score = heads_sum(qh[i] * kv_f[:C]) * pm[i] + (pm[i] - 1.0) * 1000000000.0
         dot_v = heads_sum(do[i] * kv_f[C:])
@@ -247,7 +250,7 @@
         delta = sum(ex * e[4:] for ex, e in zip(expo, every)) * inv
         prob = jnp.exp(own[:4] - top) * inv
         ds = heads_spread(pm[i] * prob * (own[4:] - delta))
-        dqh_out[n] = (ds * kv[i].astype(F32)[:C]).astype(BF16)
+        dqh_out[n] = ds * kv[i].astype(F32)[:C]
         d_kv = jnp.concatenate([ds * qh[i], heads_spread(prob) * do[i]], axis=0).astype(BF16)
         rs = rstd[i]
         d_y = hat_back(dot(wkv_v, d_kv) * g_pair, yhat[i], rs[4:5])
@@ -270,7 +273,7 @@
 
 
 def tri_back_kernel(dtri, mats, dqh, near, out, keep_out):
-    keep_out[...] = (dqh[:HALF].astype(F32) + near[HALF:].astype(F32)).astype(BF16)
+    keep_out[...] = dqh[:HALF] + near[HALF:]
     wide = dtri[...].astype(F32)
     d = [wide[:, 8 * cc : 8 * cc + 8, :].reshape(N, N).astype(BF16) for cc in range(2)]
     parts = [dot(d[cc], mats[2 + cc]) for cc in range(2)]
@@ -377,23 +380,17 @@
     sources = (
         left_weight, right_weight, row(norm_gain), relpos_table.T, row(residue_index), residue_index, template_mask,
         template_mask, pair, gate_weight, out_weight, kv_weight, row(tri_gain), row(pair_gain),
+        query_pair, cotangent, row(query_gain), query_weight.T, attn_out_weight,
     )
     scratch = fetched(*sources)
     for n in (5, 7):
         scratch[1 + n] = pltpu.SMEM(sources[n].shape, sources[n].dtype)
     outs = [((SHARDS, 32, N), BF16), (plane, F32), ((ROWS, 1, N), F32), ((C, 8 * 128), BF16), ((3, C, 128), F32)]
-    lr, z, pm, weights, gains = call(
-        project_kernel,
-        outs,
-        [HBM] * 14,
-        [pltpu.VMEM((SHARDS, 32, ROWS * C), BF16), pltpu.VMEM((ROWS * C, N), BF16)] + scratch,
+    outs += [(plane, BF16)] + [(plane, F32)] * 3
+    lr, z, pm, weights, gains, ln_b, qh, do, gate = call(
+        project_kernel, outs, [HBM] * 19, [pltpu.VMEM((SHARDS, 32, ROWS * C), BF16)] + scratch
     )(*stay(*sources))
-    lr_all = every(lr)
-    prepared = call(prepare_kernel, [(plane, BF16)] + [(plane, F32)] * 3, [VMEM] * 8)(
-        z, weights, gains, query_pair, cotangent, row(query_gain), query_weight.T, attn_out_weight
-    )
-    lr_all, ln_b, qh, do, gate = after(lr_all, *prepared)
-    tri, mats = call(tri_kernel, [((SHARDS, 16, N), BF16), ((4, N, N), BF16)], [VMEM])(lr_all)
+    tri, mats = call(tri_kernel, [((SHARDS, 16, N), BF16), ((4, N, N), BF16)], [VMEM])(every(lr))
     tri = every(tri)
     sg, that, yhat, upd, kv, rstd = call(
         attend_kernel,
@@ -404,11 +401,11 @@
     sg = lax.all_gather(sg, "tmpl")
     dtri, dqh, d_y, d_gate = call(
         back_kernel,
-        [((SHARDS, 16, N), BF16), (plane, BF16), (plane, F32), (plane, BF16)],
+        [((SHARDS, 16, N), BF16), (plane, F32), (plane, F32), (plane, BF16)],
         [VMEM] * 12,
         [wide_scratch(SHARDS * 16)],
     )(sg, that, yhat, gate, upd, qh, do, kv, rstd, pm, weights, gains)
-    dlr, keep = call(tri_back_kernel, [((SHARDS, 32, N), BF16), ((HALF, C, N), BF16)], [VMEM] * 4)(
+    dlr, keep = call(tri_back_kernel, [((SHARDS, 32, N), BF16), ((HALF, C, N), F32)], [VMEM] * 4)(
         every(dtri), mats, dqh, swap(dqh, 1)
     )
     dlr, keep = after(every(dlr), keep)
@@ -419,7 +416,7 @@
     (grad,) = call(pair_grad_kernel, [(plane, F32)], [VMEM] * 6)(d, z, d_y, d_gate, weights, gains)
     proj = proj + near
     (fan,) = call(fan_kernel, [((SHARDS, C, 2 * C), BF16)], [VMEM] * 2)(proj, swap(proj, 2))
-    fan, grad, own = after(fan, grad, keep + swap(keep, 2))
+    fan, grad, own = after(fan, grad, (keep + swap(keep, 2)).astype(BF16))
     parts = every(fan)
     sources = (query_pair, row(query_gain), query_weight.T)
     (query_grad,) = call(

time: 104 us -> 104 us (level)
  blocking collectives: 48.4 us -> 68.5 us
  starting transfers between devices: 17.1 us -> 8.38 us
  waiting for transfers between devices: 21.2 us -> 12.9 us
  local copies, waits for them, and re-layouts: 2.38 us -> 0.02 us
    all_to_all x0 -> x1, blocking collectives: none -> 20.1 us  [local(): every(lr)]
    all_to_all x1 -> x0, starting transfers between devices: 8.9 us -> none  [local(): lr_all = every(lr)]
    all_to_all x1 -> x0, waiting for transfers between devices: 8.21 us -> none  [local(): lr_all = every(lr)]
    unnamed x14 -> x6, local copies, waits for them, and re-layouts: 2.38 us -> 0.02 us
    pallas_call x4 -> x3, Pallas kernels: 5.13 us -> 4.34 us  [the longest x1 3.03 us: local(): call(project_kernel, outs, [HBM] * 19, [pltpu.VMEM((SHARDS, 32, ROWS * C)...]
  transfers between devices with their start and end apart: 7 -> 6, of which waited for: 5 -> 4; matrix products, arithmetic and copies ran while one was open for 0% -> 0% of each run, Pallas kernels for 7% -> 6%
where the time goes in v6:
time: 104 us; the launch traced here: 103 us
  blocking collectives  68.5 us (66%)
  waiting for transfers between devices  12.9 us (12%)
  Pallas kernels  12.6 us (12%)
  starting transfers between devices  8.38 us (8%)
    all_to_all x1, blocking collectives, local(): every(lr)  20.1 us
    all_to_all x1, blocking collectives, local(): dlr, keep = after(every(dlr), keep)  14.5 us
    all_to_all x1, blocking collectives, local(): tri = every(tri)  13.2 us
    all_to_all x1, blocking collectives, local(): every(dtri)  12.8 us
    all_gather x1, blocking collectives, local(): sg = lax.all_gather(sg, 'tmpl')  7.84 us
    all_to_all x1, waiting for transfers between devices, local(): parts = every(fan)  6.49 us
    ppermute x5, waiting for transfers between devices, swap(): return lax.ppermute(x, 'tmpl', [(i, i ^ bit) for i in range(4)])  6.43 us
    all_to_all x1, starting transfers between devices, local(): parts = every(fan)  4.25 us
  transfers between devices with their start and end apart: 6, of which 4 were waited for; matrix products, arithmetic and copies ran while one was open for 0% of the time, Pallas kernels for 6%

profile of v6, /device:TPU:0, one launch (start us, length us, event | category | flops | bytes accessed | tf_op | source)
XLA Modules:
  0.0 103.2 jit_solution(8092385424328768014)
XLA Ops:
  0.6 3.0 %shard_map.184 = (bf16[32,32,256]{2,1,0:T(8,128)(2,1)S(1)}, f32[8,64,256]{2,1,0:T(8,128)S(1)}, f32[8,1,256]{2,1,0:T(1,128)S(1)}, bf16[64,1024]{1,0:T(8,128)(2,1)...) custom-call(bf16[64,64]{1,0:T(8,128)(2,1)} %refs_0_.1, ...), custom_call_target="tpu_custom_call" | custom-call | tf_op jit(solution)/shard_map/pallas_call | solution.py:390
  3.7 20.1 %all_to_all.25.lr = bf16[32,32,256]{2,1,0:T(8,128)(2,1)S(1)} all-to-all(bf16[32,32,256]{2,1,0:T(8,128)(2,1)S(1)} %get-tuple-element.35), channel_id=1, replica_groups=mesh['tmpl'=4,'row'=32] {'row'}, dimensions={0} | all-to-all | bytes 1048576 | tf_op jit(solution)/shard_map/all_to_all | solution.py:393
  23.8 0.3 shard_map.185
  24.1 13.2 %all_to_all.26.tri = bf16[32,16,256]{2,1,0:T(8,128)(2,1)S(1)} all-to-all(bf16[32,16,256]{2,1,0:T(8,128)(2,1)S(1)} %get-tuple-element.36), channel_id=1, replica_groups=mesh['tmpl'=4,'row'=32] {'row'}, dimensions={0} | all-to-all | bytes 524288 | tf_op jit(solution)/shard_map/all_to_all | solution.py:394
  37.3 1.4 %shard_map.186 = (f32[8,8,256]{2,1,0:T(8,128)S(1)}, f32[8,64,256]{2,1,0:T(8,128)S(1)}, f32[8,64,256]{2,1,0:T(8,128)S(1)}, f32[8,64,256]{2,1,0:T(8,128)S(1)}, bf1...) custom-call(bf16[32,16,256]{2,1,0:T(8,128)(2,1)S(1)} %all_to_all.26.tri, f32[8,64,256]{2,1,0:T(8,128)S(1)} %get-tuple-element.37.z, ...), custom_call_target="tpu_custom_call" | custom-call | tf_op jit(solution)/shard_map/pallas_call | solution.py:395
  38.7 7.8 %all-gather = f32[32,8,256]{2,1,0:T(8,128)S(1)} all-gather(f32[8,8,256]{2,1,0:T(8,128)S(1)} %get-tuple-element.44), channel_id=2, replica_groups=mesh['tmpl'=4,'row'=32] {'tmpl'}, dimensions={0}, use_global_device_ids=true | all-gather | bytes 327680 | tf_op jit(solution)/shard_map/all_gather | solution.py:401
  46.5 1.0 shard_map.187
  47.5 0.4 collective-permute-start
  47.9 12.8 %all_to_all.27.dtri = bf16[32,16,256]{2,1,0:T(8,128)(2,1)S(1)} all-to-all(bf16[32,16,256]{2,1,0:T(8,128)(2,1)S(1)} %get-tuple-element.50), channel_id=1, replica_groups=mesh['tmpl'=4,'row'=32] {'row'}, dimensions={0} | all-to-all | bytes 524288 | tf_op jit(solution)/shard_map/all_to_all | solution.py:409
  60.7 0.0 collective-permute-done.near
  60.7 0.3 shard_map.188
  61.1 14.5 %all_to_all.28.dlr = bf16[32,32,256]{2,1,0:T(8,128)(2,1)S(1)} all-to-all(bf16[32,32,256]{2,1,0:T(8,128)(2,1)S(1)} %get-tuple-element.53), channel_id=1, replica_groups=mesh['tmpl'=4,'row'=32] {'row'}, dimensions={0} | all-to-all | bytes 1048576 | tf_op jit(solution)/shard_map/all_to_all | solution.py:411
  75.6 3.3 %collective-permute-start.3 = (f32[4,64,256]{2,1,0:T(8,128)S(1)}, f32[4,64,256]{2,1,0:T(8,128)S(1)}, u32[]{:S(2)}, u32[]{:S(2)}) collective-permute-start(f32[4,64,256]{2,1,0:T(8,128)S(1)} %get-tuple-element.61), channel_id=1, source_target_pairs={{0,64},{32,96},{64,0},{96,32},{1,65},{33,97},{65,1},{97,33},{2,66}... | collective-permute-start | bytes 786440 | tf_op jit(solution)/shard_map/ppermute | solution.py:365
  78.8 0.8 shard_map.189
  79.7 0.1 collective-permute-start.1
  79.8 1.2 %collective-permute-done.1 = f32[64,128]{1,0:T(8,128)S(1)} collective-permute-done((f32[64,128]{1,0:T(8,128)S(1)}, f32[64,128]{1,0:T(8,128)S(1)}, u32[]{:S(2)}, u32[]{:S(2)}) %collective-permute-start.1) | collective-permute-done | bytes 32800 | tf_op jit(solution)/shard_map/ppermute | solution.py:365
  81.0 0.3 collective-permute-start.2
  81.2 1.3 %shard_map.191 = f32[8,64,256]{2,1,0:T(8,128)} custom-call(bf16[8,128,256]{2,1,0:T(8,128)(2,1)S(1)} %get-tuple-element.58.d, f32[8,64,256]{2,1,0:T(8,128)S(1)} %get-tuple-element.37.z, f32[8,64,256]{2,1,0:T(8,128)S(1)} %get-tuple-element.59.d_y, bf16[8,64,256]{2,1,0:T(8,128)(2,1)S(1)} %get-tuple-element.60.d_gate, ...), custom_call_target="tpu_custom_call" | custom-call | tf_op jit(solution)/shard_map/pallas_call | solution.py:416
  82.5 3.9 %collective-permute-done.2.far = f32[64,128]{1,0:T(8,128)S(1)} collective-permute-done((f32[64,128]{1,0:T(8,128)S(1)}, f32[64,128]{1,0:T(8,128)S(1)}, u32[]{:S(2)}, u32[]{:S(2)}) %collective-permute-start.2) | collective-permute-done | bytes 32800 | tf_op jit(solution)/shard_map/ppermute | solution.py:365
  86.4 0.9 shard_map.190
  87.2 0.0 collective-permute-done.3
  87.3 0.0 copy-start
  87.3 0.0 copy-start.1
  87.3 0.0 copy-start.2
  87.3 4.2 %all-to-all-start.4 = ((bf16[32,64,128]{2,1,0:T(8,128)(2,1)}), bf16[32,64,128]{2,1,0:T(8,128)(2,1)S(1)}, u32[]{:S(2)}, u32[]{:S(2)}) async-start(bf16[32,64,128]{2,1,0:T(8,128)(2,1)} %shard_map.190), calls=%async_computation.4 | async-start | bytes 1048576 | tf_op jit(solution)/shard_map/all_to_all | solution.py:420
  91.6 0.1 collective-permute-start.4
  91.7 1.3 %collective-permute-done.4.other = bf16[4,64,256]{2,1,0:T(8,128)(2,1)S(1)} collective-permute-done((bf16[4,64,256]{2,1,0:T(8,128)(2,1)S(1)}, bf16[4,64,256]{2,1,0:T(8,128)(2,1)S(1)}, u32[]{:S(2)}, u32[]{:S(2)}) %collective-permute-start.4) | collective-permute-done | bytes 131104 | tf_op jit(solution)/shard_map/ppermute | solution.py:365
  93.0 0.0 copy-done
  93.0 0.0 copy-done.1
  93.0 0.0 copy-done.2
  93.0 2.9 %shard_map.192 = f32[8,256,128]{2,1,0:T(8,128)} custom-call(bf16[4,64,256]{2,1,0:T(8,128)(2,1)S(1)} %add_convert_fusion.own, bf16[4,64,256]{2,1,0:T(8,128)(2,1)S(1)} %collective-permute-done.4.other, bf16[8,256,128]{2,1,0:T(8,128)(2,1)S(1)} %copy-done, f32[1,128]{1,0:T(1,128)S(1)} %bitcast.18, bf16[64,128]{1,0:T(8,128)(2,1)S(1)} %bitcast.16), custom_call_target="tpu_custom_call" | custom-call | tf_op jit(solution)/shard_map/pallas_call | solution.py:422
  95.9 6.5 %all-to-all-done.4.parts = bf16[32,64,128]{2,1,0:T(8,128)(2,1)S(1)} async-done(((bf16[32,64,128]{2,1,0:T(8,128)(2,1)}), bf16[32,64,128]{2,1,0:T(8,128)(2,1)S(1)}, u32[]{:S(2)}, u32[]{:S(2)}) %all-to-all-start.4) | async-done | bytes 524320 | tf_op jit(solution)/shard_map/all_to_all | solution.py:420
  102.4 0.8 shard_map.193
  (2 shorter events, 0.0 us)
Async XLA Ops:
  47.5 13.2 %collective-permute-start = (f32[8,64,256]{2,1,0:T(8,128)S(1)}, f32[8,64,256]{2,1,0:T(8,128)S(1)}, u32[]{:S(2)}, u32[]{:S(2)}) collective-permute-start(f32[8,64,256]{2,1,0:T(8,128)S(1)} %get-tuple-element.52.dqh), channel_id=1, source_target_pairs={{0,32},{32,0},{64,96},{96,64},{1,33},{33,1},{65,97},{97,65},{2,34}... | collective-permute-start | bytes 1572872 | tf_op jit(solution)/shard_map/ppermute | solution.py:365
  75.6 11.7 %collective-permute-start.3 = (f32[4,64,256]{2,1,0:T(8,128)S(1)}, f32[4,64,256]{2,1,0:T(8,128)S(1)}, u32[]{:S(2)}, u32[]{:S(2)}) collective-permute-start(f32[4,64,256]{2,1,0:T(8,128)S(1)} %get-tuple-element.61), channel_id=1, source_target_pairs={{0,64},{32,96},{64,0},{96,32},{1,65},{33,97},{65,1},{97,33},{2,66}... | collective-permute-start | bytes 786440 | tf_op jit(solution)/shard_map/ppermute | solution.py:365
  79.7 1.3 %collective-permute-start.1 = (f32[64,128]{1,0:T(8,128)S(1)}, f32[64,128]{1,0:T(8,128)S(1)}, u32[]{:S(2)}, u32[]{:S(2)}) collective-permute-start(f32[64,128]{1,0:T(8,128)S(1)} %get-tuple-element.57), channel_id=1, source_target_pairs={{0,32},{32,0},{64,96},{96,64},{1,33},{33,1},{65,97},{97,65},{2,34}... | collective-permute-start | bytes 98312 | tf_op jit(solution)/shard_map/ppermute | solution.py:365
  81.0 5.4 %collective-permute-start.2 = (f32[64,128]{1,0:T(8,128)S(1)}, f32[64,128]{1,0:T(8,128)S(1)}, u32[]{:S(2)}, u32[]{:S(2)}) collective-permute-start(f32[64,128]{1,0:T(8,128)S(1)} %add.6.own), channel_id=1, source_target_pairs={{0,64},{32,96},{64,0},{96,32},{1,65},{33,97},{65,1},{97,33},{2,66}... | collective-permute-start | bytes 98312 | tf_op jit(solution)/shard_map/ppermute | solution.py:365
  87.3 5.7 %copy-start = (bf16[8,256,128]{2,1,0:T(8,128)(2,1)S(1)}, bf16[8,256,128]{2,1,0:T(8,128)(2,1)}, u32[]{:S(2)}) copy-start(bf16[8,256,128]{2,1,0:T(8,128)(2,1)} %query_h.1) | copy-start | bytes 1572868
  87.3 5.7 %copy-start.1 = (bf16[128,64]{0,1:T(8,128)(2,1)S(1)}, bf16[128,64]{0,1:T(8,128)(2,1)}, u32[]{:S(2)}) copy-start(bf16[128,64]{0,1:T(8,128)(2,1)} %param.31) | copy-start | bytes 49156
  87.3 5.7 %copy-start.2 = (f32[128]{0:T(128)S(1)}, f32[128]{0:T(128)}, u32[]{:S(2)}) copy-start(f32[128]{0:T(128)} %param.30) | copy-start | bytes 1540
  87.3 15.1 %all-to-all-start.4 = ((bf16[32,64,128]{2,1,0:T(8,128)(2,1)}), bf16[32,64,128]{2,1,0:T(8,128)(2,1)S(1)}, u32[]{:S(2)}, u32[]{:S(2)}) async-start(bf16[32,64,128]{2,1,0:T(8,128)(2,1)} %shard_map.190), calls=%async_computation.4 | async-start | bytes 1048576 | tf_op jit(solution)/shard_map/all_to_all | solution.py:420
  91.6 1.4 %collective-permute-start.4 = (bf16[4,64,256]{2,1,0:T(8,128)(2,1)S(1)}, bf16[4,64,256]{2,1,0:T(8,128)(2,1)S(1)}, u32[]{:S(2)}, u32[]{:S(2)}) collective-permute-start(bf16[4,64,256]{2,1,0:T(8,128)(2,1)S(1)} %add_convert_fusion.own), channel_id=1, source_target_pairs={{0,32},{32,0},{64,96},{96,64},{1,33},{33,1},{65,97},{97,65},{2,34}... | collective-permute-start | bytes 393224 | tf_op jit(solution)/shard_map/ppermute | solution.py:365

commit v7 on v6

--- a/solution.py
+++ b/solution.py
@@ -273,7 +273,7 @@
 
 
 def tri_back_kernel(dtri, mats, dqh, near, out, keep_out):
-    keep_out[...] = dqh[:HALF] + near[HALF:]
+    keep_out[...] = (dqh[:HALF] + near[HALF:]).astype(BF16)
     wide = dtri[...].astype(F32)
     d = [wide[:, 8 * cc : 8 * cc + 8, :].reshape(N, N).astype(BF16) for cc in range(2)]
     parts = [dot(d[cc], mats[2 + cc]) for cc in range(2)]
@@ -405,7 +405,7 @@
         [VMEM] * 12,
         [wide_scratch(SHARDS * 16)],
     )(sg, that, yhat, gate, upd, qh, do, kv, rstd, pm, weights, gains)
-    dlr, keep = call(tri_back_kernel, [((SHARDS, 32, N), BF16), ((HALF, C, N), F32)], [VMEM] * 4)(
+    dlr, keep = call(tri_back_kernel, [((SHARDS, 32, N), BF16), ((HALF, C, N), BF16)], [VMEM] * 4)(
         every(dtri), mats, dqh, swap(dqh, 1)
     )
     dlr, keep = after(every(dlr), keep)
@@ -416,7 +416,7 @@
     (grad,) = call(pair_grad_kernel, [(plane, F32)], [VMEM] * 6)(d, z, d_y, d_gate, weights, gains)
     proj = proj + near
     (fan,) = call(fan_kernel, [((SHARDS, C, 2 * C), BF16)], [VMEM] * 2)(proj, swap(proj, 2))
-    fan, grad, own = after(fan, grad, (keep + swap(keep, 2)).astype(BF16))
+    fan, grad, own = after(fan, grad, keep + swap(keep, 2))
     parts = every(fan)
     sources = (query_pair, row(query_gain), query_weight.T)
     (query_grad,) = call(

time: 104 us -> 104 us (level)
  no operation moved by 1% of the time
where the time goes in v7:
time: 104 us; the launch traced here: 103 us
  blocking collectives  68.5 us (66%)
  waiting for transfers between devices  12.9 us (12%)
  Pallas kernels  12.6 us (12%)
  starting transfers between devices  8.38 us (8%)
    all_to_all x1, blocking collectives, local(): every(lr)  20.1 us
    all_to_all x1, blocking collectives, local(): dlr, keep = after(every(dlr), keep)  14.5 us
    all_to_all x1, blocking collectives, local(): tri = every(tri)  13.2 us
    all_to_all x1, blocking collectives, local(): every(dtri)  12.8 us
    all_gather x1, blocking collectives, local(): sg = lax.all_gather(sg, 'tmpl')  7.84 us
    all_to_all x1, waiting for transfers between devices, local(): parts = every(fan)  6.49 us
    ppermute x5, waiting for transfers between devices, swap(): return lax.ppermute(x, 'tmpl', [(i, i ^ bit) for i in range(4)])  6.43 us
    all_to_all x1, starting transfers between devices, local(): parts = every(fan)  4.25 us
  transfers between devices with their start and end apart: 6, of which 4 were waited for; matrix products, arithmetic and copies ran while one was open for 0% of the time, Pallas kernels for 6%

profile of v7, /device:TPU:0, one launch (start us, length us, event | category | flops | bytes accessed | tf_op | source)
XLA Modules:
  0.0 103.2 jit_solution(5377517377636703517)
XLA Ops:
  0.6 3.0 %shard_map.184 = (bf16[32,32,256]{2,1,0:T(8,128)(2,1)S(1)}, f32[8,64,256]{2,1,0:T(8,128)S(1)}, f32[8,1,256]{2,1,0:T(1,128)S(1)}, bf16[64,1024]{1,0:T(8,128)(2,1)...) custom-call(bf16[64,64]{1,0:T(8,128)(2,1)} %refs_0_.1, ...), custom_call_target="tpu_custom_call" | custom-call | tf_op jit(solution)/shard_map/pallas_call | solution.py:390
  3.7 20.1 %all_to_all.25.lr = bf16[32,32,256]{2,1,0:T(8,128)(2,1)S(1)} all-to-all(bf16[32,32,256]{2,1,0:T(8,128)(2,1)S(1)} %get-tuple-element.35), channel_id=1, replica_groups=mesh['tmpl'=4,'row'=32] {'row'}, dimensions={0} | all-to-all | bytes 1048576 | tf_op jit(solution)/shard_map/all_to_all | solution.py:393
  23.8 0.3 shard_map.185
  24.1 13.2 %all_to_all.26.tri = bf16[32,16,256]{2,1,0:T(8,128)(2,1)S(1)} all-to-all(bf16[32,16,256]{2,1,0:T(8,128)(2,1)S(1)} %get-tuple-element.36), channel_id=1, replica_groups=mesh['tmpl'=4,'row'=32] {'row'}, dimensions={0} | all-to-all | bytes 524288 | tf_op jit(solution)/shard_map/all_to_all | solution.py:394
  37.3 1.4 %shard_map.186 = (f32[8,8,256]{2,1,0:T(8,128)S(1)}, f32[8,64,256]{2,1,0:T(8,128)S(1)}, f32[8,64,256]{2,1,0:T(8,128)S(1)}, f32[8,64,256]{2,1,0:T(8,128)S(1)}, bf1...) custom-call(bf16[32,16,256]{2,1,0:T(8,128)(2,1)S(1)} %all_to_all.26.tri, f32[8,64,256]{2,1,0:T(8,128)S(1)} %get-tuple-element.37.z, ...), custom_call_target="tpu_custom_call" | custom-call | tf_op jit(solution)/shard_map/pallas_call | solution.py:395
  38.7 7.8 %all-gather = f32[32,8,256]{2,1,0:T(8,128)S(1)} all-gather(f32[8,8,256]{2,1,0:T(8,128)S(1)} %get-tuple-element.44), channel_id=2, replica_groups=mesh['tmpl'=4,'row'=32] {'tmpl'}, dimensions={0}, use_global_device_ids=true | all-gather | bytes 327680 | tf_op jit(solution)/shard_map/all_gather | solution.py:401
  46.5 1.0 shard_map.187
  47.5 0.4 collective-permute-start
  47.9 12.8 %all_to_all.27.dtri = bf16[32,16,256]{2,1,0:T(8,128)(2,1)S(1)} all-to-all(bf16[32,16,256]{2,1,0:T(8,128)(2,1)S(1)} %get-tuple-element.50), channel_id=1, replica_groups=mesh['tmpl'=4,'row'=32] {'row'}, dimensions={0} | all-to-all | bytes 524288 | tf_op jit(solution)/shard_map/all_to_all | solution.py:409
  60.7 0.0 collective-permute-done.near
  60.7 0.3 shard_map.188
  61.1 14.5 %all_to_all.28.dlr = bf16[32,32,256]{2,1,0:T(8,128)(2,1)S(1)} all-to-all(bf16[32,32,256]{2,1,0:T(8,128)(2,1)S(1)} %get-tuple-element.53), channel_id=1, replica_groups=mesh['tmpl'=4,'row'=32] {'row'}, dimensions={0} | all-to-all | bytes 1048576 | tf_op jit(solution)/shard_map/all_to_all | solution.py:411
  75.6 3.3 %collective-permute-start.3 = (bf16[4,64,256]{2,1,0:T(8,128)(2,1)S(1)}, bf16[4,64,256]{2,1,0:T(8,128)(2,1)S(1)}, u32[]{:S(2)}, u32[]{:S(2)}) collective-permute-start(bf16[4,64,256]{2,1,0:T(8,128)(2,1)S(1)} %get-tuple-element.61), channel_id=1, source_target_pairs={{0,64},{32,96},{64,0},{96,32},{1,65},{33,97},{65,1},{97,33},{2,66}... | collective-permute-start | bytes 393224 | tf_op jit(solution)/shard_map/ppermute | solution.py:365
  78.8 0.8 shard_map.189
  79.7 0.1 collective-permute-start.1
  79.8 1.2 %collective-permute-done.1 = f32[64,128]{1,0:T(8,128)S(1)} collective-permute-done((f32[64,128]{1,0:T(8,128)S(1)}, f32[64,128]{1,0:T(8,128)S(1)}, u32[]{:S(2)}, u32[]{:S(2)}) %collective-permute-start.1) | collective-permute-done | bytes 32800 | tf_op jit(solution)/shard_map/ppermute | solution.py:365
  81.0 0.3 collective-permute-start.2
  81.2 1.3 %shard_map.191 = f32[8,64,256]{2,1,0:T(8,128)} custom-call(bf16[8,128,256]{2,1,0:T(8,128)(2,1)S(1)} %get-tuple-element.58.d, f32[8,64,256]{2,1,0:T(8,128)S(1)} %get-tuple-element.37.z, f32[8,64,256]{2,1,0:T(8,128)S(1)} %get-tuple-element.59.d_y, bf16[8,64,256]{2,1,0:T(8,128)(2,1)S(1)} %get-tuple-element.60.d_gate, ...), custom_call_target="tpu_custom_call" | custom-call | tf_op jit(solution)/shard_map/pallas_call | solution.py:416
  82.5 3.9 %collective-permute-done.2.far = f32[64,128]{1,0:T(8,128)S(1)} collective-permute-done((f32[64,128]{1,0:T(8,128)S(1)}, f32[64,128]{1,0:T(8,128)S(1)}, u32[]{:S(2)}, u32[]{:S(2)}) %collective-permute-start.2) | collective-permute-done | bytes 32800 | tf_op jit(solution)/shard_map/ppermute | solution.py:365
  86.4 0.9 shard_map.190
  87.2 0.0 collective-permute-done.3
  87.3 0.0 copy-start
  87.3 0.0 copy-start.1
  87.3 0.0 copy-start.2
  87.3 4.2 %all-to-all-start.4 = ((bf16[32,64,128]{2,1,0:T(8,128)(2,1)}), bf16[32,64,128]{2,1,0:T(8,128)(2,1)S(1)}, u32[]{:S(2)}, u32[]{:S(2)}) async-start(bf16[32,64,128]{2,1,0:T(8,128)(2,1)} %shard_map.190), calls=%async_computation.4 | async-start | bytes 1048576 | tf_op jit(solution)/shard_map/all_to_all | solution.py:420
  91.6 0.1 collective-permute-start.4
  91.7 1.3 %collective-permute-done.4.other = bf16[4,64,256]{2,1,0:T(8,128)(2,1)S(1)} collective-permute-done((bf16[4,64,256]{2,1,0:T(8,128)(2,1)S(1)}, bf16[4,64,256]{2,1,0:T(8,128)(2,1)S(1)}, u32[]{:S(2)}, u32[]{:S(2)}) %collective-permute-start.4) | collective-permute-done | bytes 131104 | tf_op jit(solution)/shard_map/ppermute | solution.py:365
  93.0 0.0 copy-done
  93.0 0.0 copy-done.1
  93.0 0.0 copy-done.2
  93.0 2.9 %shard_map.192 = f32[8,256,128]{2,1,0:T(8,128)} custom-call(bf16[4,64,256]{2,1,0:T(8,128)(2,1)S(1)} %add.7.own, bf16[4,64,256]{2,1,0:T(8,128)(2,1)S(1)} %collective-permute-done.4.other, bf16[8,256,128]{2,1,0:T(8,128)(2,1)S(1)} %copy-done, f32[1,128]{1,0:T(1,128)S(1)} %bitcast.18, bf16[64,128]{1,0:T(8,128)(2,1)S(1)} %bitcast.16), custom_call_target="tpu_custom_call" | custom-call | tf_op jit(solution)/shard_map/pallas_call | solution.py:422
  95.9 6.5 %all-to-all-done.4.parts = bf16[32,64,128]{2,1,0:T(8,128)(2,1)S(1)} async-done(((bf16[32,64,128]{2,1,0:T(8,128)(2,1)}), bf16[32,64,128]{2,1,0:T(8,128)(2,1)S(1)}, u32[]{:S(2)}, u32[]{:S(2)}) %all-to-all-start.4) | async-done | bytes 524320 | tf_op jit(solution)/shard_map/all_to_all | solution.py:420
  102.4 0.8 shard_map.193
  (2 shorter events, 0.0 us)
Async XLA Ops:
  47.5 13.2 %collective-permute-start = (f32[8,64,256]{2,1,0:T(8,128)S(1)}, f32[8,64,256]{2,1,0:T(8,128)S(1)}, u32[]{:S(2)}, u32[]{:S(2)}) collective-permute-start(f32[8,64,256]{2,1,0:T(8,128)S(1)} %get-tuple-element.52.dqh), channel_id=1, source_target_pairs={{0,32},{32,0},{64,96},{96,64},{1,33},{33,1},{65,97},{97,65},{2,34}... | collective-permute-start | bytes 1572872 | tf_op jit(solution)/shard_map/ppermute | solution.py:365
  75.6 11.7 %collective-permute-start.3 = (bf16[4,64,256]{2,1,0:T(8,128)(2,1)S(1)}, bf16[4,64,256]{2,1,0:T(8,128)(2,1)S(1)}, u32[]{:S(2)}, u32[]{:S(2)}) collective-permute-start(bf16[4,64,256]{2,1,0:T(8,128)(2,1)S(1)} %get-tuple-element.61), channel_id=1, source_target_pairs={{0,64},{32,96},{64,0},{96,32},{1,65},{33,97},{65,1},{97,33},{2,66}... | collective-permute-start | bytes 393224 | tf_op jit(solution)/shard_map/ppermute | solution.py:365
  79.7 1.3 %collective-permute-start.1 = (f32[64,128]{1,0:T(8,128)S(1)}, f32[64,128]{1,0:T(8,128)S(1)}, u32[]{:S(2)}, u32[]{:S(2)}) collective-permute-start(f32[64,128]{1,0:T(8,128)S(1)} %get-tuple-element.57), channel_id=1, source_target_pairs={{0,32},{32,0},{64,96},{96,64},{1,33},{33,1},{65,97},{97,65},{2,34}... | collective-permute-start | bytes 98312 | tf_op jit(solution)/shard_map/ppermute | solution.py:365
  81.0 5.4 %collective-permute-start.2 = (f32[64,128]{1,0:T(8,128)S(1)}, f32[64,128]{1,0:T(8,128)S(1)}, u32[]{:S(2)}, u32[]{:S(2)}) collective-permute-start(f32[64,128]{1,0:T(8,128)S(1)} %add.6.own), channel_id=1, source_target_pairs={{0,64},{32,96},{64,0},{96,32},{1,65},{33,97},{65,1},{97,33},{2,66}... | collective-permute-start | bytes 98312 | tf_op jit(solution)/shard_map/ppermute | solution.py:365
  87.3 5.7 %copy-start = (bf16[8,256,128]{2,1,0:T(8,128)(2,1)S(1)}, bf16[8,256,128]{2,1,0:T(8,128)(2,1)}, u32[]{:S(2)}) copy-start(bf16[8,256,128]{2,1,0:T(8,128)(2,1)} %query_h.1) | copy-start | bytes 1572868
  87.3 5.7 %copy-start.1 = (bf16[128,64]{0,1:T(8,128)(2,1)S(1)}, bf16[128,64]{0,1:T(8,128)(2,1)}, u32[]{:S(2)}) copy-start(bf16[128,64]{0,1:T(8,128)(2,1)} %param.31) | copy-start | bytes 49156
  87.3 5.7 %copy-start.2 = (f32[128]{0:T(128)S(1)}, f32[128]{0:T(128)}, u32[]{:S(2)}) copy-start(f32[128]{0:T(128)} %param.30) | copy-start | bytes 1540
  87.3 15.1 %all-to-all-start.4 = ((bf16[32,64,128]{2,1,0:T(8,128)(2,1)}), bf16[32,64,128]{2,1,0:T(8,128)(2,1)S(1)}, u32[]{:S(2)}, u32[]{:S(2)}) async-start(bf16[32,64,128]{2,1,0:T(8,128)(2,1)} %shard_map.190), calls=%async_computation.4 | async-start | bytes 1048576 | tf_op jit(solution)/shard_map/all_to_all | solution.py:420
  91.6 1.4 %collective-permute-start.4 = (bf16[4,64,256]{2,1,0:T(8,128)(2,1)S(1)}, bf16[4,64,256]{2,1,0:T(8,128)(2,1)S(1)}, u32[]{:S(2)}, u32[]{:S(2)}) collective-permute-start(bf16[4,64,256]{2,1,0:T(8,128)(2,1)S(1)} %add.7.own), channel_id=1, source_target_pairs={{0,32},{32,0},{64,96},{96,64},{1,33},{33,1},{65,97},{97,65},{2,34}... | collective-permute-start | bytes 393224 | tf_op jit(solution)/shard_map/ppermute | solution.py:365

commit v8 on v7

--- a/solution.py
+++ b/solution.py
@@ -326,10 +326,12 @@
         body((1 - core) * HALF + i, other[i])
 
 
-def fan_kernel(own, far, out):
+def fan_kernel(own, far, out, some, sems):
     total = (own[...] + far[...]).astype(BF16)
-    for s in range(SHARDS):
-        out[s] = total
+    for s in range(some.shape[0]):
+        some[s] = total
+    spots = [out.at[pl.ds(at, some.shape[0])] for at in range(0, SHARDS, some.shape[0])]
+    arrive(copies([some] * len(spots), spots, sems))
 
 
 def sum_kernel(parts, out):
@@ -415,7 +417,13 @@
     near = swap(proj, 1)
     (grad,) = call(pair_grad_kernel, [(plane, F32)], [VMEM] * 6)(d, z, d_y, d_gate, weights, gains)
     proj = proj + near
-    (fan,) = call(fan_kernel, [((SHARDS, C, 2 * C), BF16)], [VMEM] * 2)(proj, swap(proj, 2))
+    (fan,) = call(
+        fan_kernel,
+        [((SHARDS, C, 2 * C), BF16)],
+        [VMEM] * 2,
+        [pltpu.VMEM((8, C, 2 * C), BF16), pltpu.SemaphoreType.DMA((SHARDS // 8,))],
+        home=HBM,
+    )(proj, swap(proj, 2))
     fan, grad, own = after(fan, grad, keep + swap(keep, 2))
     parts = every(fan)
     sources = (query_pair, row(query_gain), query_weight.T)

time: 104 us -> 104 us (level)
  no operation moved by 1% of the time
where the time goes in v8:
time: 104 us; the launch traced here: 103 us
  blocking collectives  68.5 us (66%)
  waiting for transfers between devices  12.9 us (12%)
  Pallas kernels  12.6 us (12%)
  starting transfers between devices  8.38 us (8%)
    all_to_all x1, blocking collectives, local(): every(lr)  20.1 us
    all_to_all x1, blocking collectives, local(): dlr, keep = after(every(dlr), keep)  14.5 us
    all_to_all x1, blocking collectives, local(): tri = every(tri)  13.2 us
    all_to_all x1, blocking collectives, local(): every(dtri)  12.8 us
    all_gather x1, blocking collectives, local(): sg = lax.all_gather(sg, 'tmpl')  7.84 us
    all_to_all x1, waiting for transfers between devices, local(): parts = every(fan)  6.49 us
    ppermute x5, waiting for transfers between devices, swap(): return lax.ppermute(x, 'tmpl', [(i, i ^ bit) for i in range(4)])  6.43 us
    all_to_all x1, starting transfers between devices, local(): parts = every(fan)  4.25 us
  transfers between devices with their start and end apart: 6, of which 4 were waited for; matrix products, arithmetic and copies ran while one was open for 0% of the time, Pallas kernels for 6%

profile of v8, /device:TPU:0, one launch (start us, length us, event | category | flops | bytes accessed | tf_op | source)
XLA Modules:
  0.0 103.2 jit_solution(9505664509745306248)
XLA Ops:
  0.6 3.0 %shard_map.184 = (bf16[32,32,256]{2,1,0:T(8,128)(2,1)S(1)}, f32[8,64,256]{2,1,0:T(8,128)S(1)}, f32[8,1,256]{2,1,0:T(1,128)S(1)}, bf16[64,1024]{1,0:T(8,128)(2,1)...) custom-call(bf16[64,64]{1,0:T(8,128)(2,1)} %refs_0_.1, ...), custom_call_target="tpu_custom_call" | custom-call | tf_op jit(solution)/shard_map/pallas_call | solution.py:392
  3.7 20.1 %all_to_all.25.lr = bf16[32,32,256]{2,1,0:T(8,128)(2,1)S(1)} all-to-all(bf16[32,32,256]{2,1,0:T(8,128)(2,1)S(1)} %get-tuple-element.35), channel_id=1, replica_groups=mesh['tmpl'=4,'row'=32] {'row'}, dimensions={0} | all-to-all | bytes 1048576 | tf_op jit(solution)/shard_map/all_to_all | solution.py:395
  23.8 0.3 shard_map.185
  24.1 13.2 %all_to_all.26.tri = bf16[32,16,256]{2,1,0:T(8,128)(2,1)S(1)} all-to-all(bf16[32,16,256]{2,1,0:T(8,128)(2,1)S(1)} %get-tuple-element.36), channel_id=1, replica_groups=mesh['tmpl'=4,'row'=32] {'row'}, dimensions={0} | all-to-all | bytes 524288 | tf_op jit(solution)/shard_map/all_to_all | solution.py:396
  37.3 1.4 %shard_map.186 = (f32[8,8,256]{2,1,0:T(8,128)S(1)}, f32[8,64,256]{2,1,0:T(8,128)S(1)}, f32[8,64,256]{2,1,0:T(8,128)S(1)}, f32[8,64,256]{2,1,0:T(8,128)S(1)}, bf1...) custom-call(bf16[32,16,256]{2,1,0:T(8,128)(2,1)S(1)} %all_to_all.26.tri, f32[8,64,256]{2,1,0:T(8,128)S(1)} %get-tuple-element.37.z, ...), custom_call_target="tpu_custom_call" | custom-call | tf_op jit(solution)/shard_map/pallas_call | solution.py:397
  38.7 7.8 %all-gather = f32[32,8,256]{2,1,0:T(8,128)S(1)} all-gather(f32[8,8,256]{2,1,0:T(8,128)S(1)} %get-tuple-element.44), channel_id=2, replica_groups=mesh['tmpl'=4,'row'=32] {'tmpl'}, dimensions={0}, use_global_device_ids=true | all-gather | bytes 327680 | tf_op jit(solution)/shard_map/all_gather | solution.py:403
  46.5 1.0 shard_map.187
  47.5 0.4 collective-permute-start
  47.9 12.8 %all_to_all.27.dtri = bf16[32,16,256]{2,1,0:T(8,128)(2,1)S(1)} all-to-all(bf16[32,16,256]{2,1,0:T(8,128)(2,1)S(1)} %get-tuple-element.50), channel_id=1, replica_groups=mesh['tmpl'=4,'row'=32] {'row'}, dimensions={0} | all-to-all | bytes 524288 | tf_op jit(solution)/shard_map/all_to_all | solution.py:411
  60.7 0.0 collective-permute-done.near
  60.7 0.3 shard_map.188
  61.1 14.5 %all_to_all.28.dlr = bf16[32,32,256]{2,1,0:T(8,128)(2,1)S(1)} all-to-all(bf16[32,32,256]{2,1,0:T(8,128)(2,1)S(1)} %get-tuple-element.53), channel_id=1, replica_groups=mesh['tmpl'=4,'row'=32] {'row'}, dimensions={0} | all-to-all | bytes 1048576 | tf_op jit(solution)/shard_map/all_to_all | solution.py:413
  75.6 3.3 %collective-permute-start.3 = (bf16[4,64,256]{2,1,0:T(8,128)(2,1)S(1)}, bf16[4,64,256]{2,1,0:T(8,128)(2,1)S(1)}, u32[]{:S(2)}, u32[]{:S(2)}) collective-permute-start(bf16[4,64,256]{2,1,0:T(8,128)(2,1)S(1)} %get-tuple-element.61), channel_id=1, source_target_pairs={{0,64},{32,96},{64,0},{96,32},{1,65},{33,97},{65,1},{97,33},{2,66}... | collective-permute-start | bytes 393224 | tf_op jit(solution)/shard_map/ppermute | solution.py:367
  78.8 0.8 shard_map.189
  79.7 0.1 collective-permute-start.1
  79.8 1.2 %collective-permute-done.1 = f32[64,128]{1,0:T(8,128)S(1)} collective-permute-done((f32[64,128]{1,0:T(8,128)S(1)}, f32[64,128]{1,0:T(8,128)S(1)}, u32[]{:S(2)}, u32[]{:S(2)}) %collective-permute-start.1) | collective-permute-done | bytes 32800 | tf_op jit(solution)/shard_map/ppermute | solution.py:367
  81.0 0.3 collective-permute-start.2
  81.2 1.3 %shard_map.191 = f32[8,64,256]{2,1,0:T(8,128)} custom-call(bf16[8,128,256]{2,1,0:T(8,128)(2,1)S(1)} %get-tuple-element.58.d, f32[8,64,256]{2,1,0:T(8,128)S(1)} %get-tuple-element.37.z, f32[8,64,256]{2,1,0:T(8,128)S(1)} %get-tuple-element.59.d_y, bf16[8,64,256]{2,1,0:T(8,128)(2,1)S(1)} %get-tuple-element.60.d_gate, ...), custom_call_target="tpu_custom_call" | custom-call | tf_op jit(solution)/shard_map/pallas_call | solution.py:418
  82.5 3.9 %collective-permute-done.2.far = f32[64,128]{1,0:T(8,128)S(1)} collective-permute-done((f32[64,128]{1,0:T(8,128)S(1)}, f32[64,128]{1,0:T(8,128)S(1)}, u32[]{:S(2)}, u32[]{:S(2)}) %collective-permute-start.2) | collective-permute-done | bytes 32800 | tf_op jit(solution)/shard_map/ppermute | solution.py:367
  86.4 0.8 shard_map.190
  87.2 0.0 collective-permute-done.3
  87.3 0.0 copy-start
  87.3 0.0 copy-start.1
  87.3 0.0 copy-start.2
  87.3 4.2 %all-to-all-start.4 = ((bf16[32,64,128]{2,1,0:T(8,128)(2,1)}), bf16[32,64,128]{2,1,0:T(8,128)(2,1)S(1)}, u32[]{:S(2)}, u32[]{:S(2)}) async-start(bf16[32,64,128]{2,1,0:T(8,128)(2,1)} %shard_map.190), calls=%async_computation.4 | async-start | bytes 1048576 | tf_op jit(solution)/shard_map/all_to_all | solution.py:428
  91.6 0.1 collective-permute-start.4
  91.7 1.3 %collective-permute-done.4.other = bf16[4,64,256]{2,1,0:T(8,128)(2,1)S(1)} collective-permute-done((bf16[4,64,256]{2,1,0:T(8,128)(2,1)S(1)}, bf16[4,64,256]{2,1,0:T(8,128)(2,1)S(1)}, u32[]{:S(2)}, u32[]{:S(2)}) %collective-permute-start.4) | collective-permute-done | bytes 131104 | tf_op jit(solution)/shard_map/ppermute | solution.py:367
  93.0 0.0 copy-done
  93.0 0.0 copy-done.1
  93.0 0.0 copy-done.2
  93.0 2.9 %shard_map.192 = f32[8,256,128]{2,1,0:T(8,128)} custom-call(bf16[4,64,256]{2,1,0:T(8,128)(2,1)S(1)} %add.7.own, bf16[4,64,256]{2,1,0:T(8,128)(2,1)S(1)} %collective-permute-done.4.other, bf16[8,256,128]{2,1,0:T(8,128)(2,1)S(1)} %copy-done, f32[1,128]{1,0:T(1,128)S(1)} %bitcast.18, bf16[64,128]{1,0:T(8,128)(2,1)S(1)} %bitcast.16), custom_call_target="tpu_custom_call" | custom-call | tf_op jit(solution)/shard_map/pallas_call | solution.py:430
  95.9 6.5 %all-to-all-done.4.parts = bf16[32,64,128]{2,1,0:T(8,128)(2,1)S(1)} async-done(((bf16[32,64,128]{2,1,0:T(8,128)(2,1)}), bf16[32,64,128]{2,1,0:T(8,128)(2,1)S(1)}, u32[]{:S(2)}, u32[]{:S(2)}) %all-to-all-start.4) | async-done | bytes 524320 | tf_op jit(solution)/shard_map/all_to_all | solution.py:428
  102.4 0.8 shard_map.193
  (2 shorter events, 0.0 us)
Async XLA Ops:
  47.5 13.2 %collective-permute-start = (f32[8,64,256]{2,1,0:T(8,128)S(1)}, f32[8,64,256]{2,1,0:T(8,128)S(1)}, u32[]{:S(2)}, u32[]{:S(2)}) collective-permute-start(f32[8,64,256]{2,1,0:T(8,128)S(1)} %get-tuple-element.52.dqh), channel_id=1, source_target_pairs={{0,32},{32,0},{64,96},{96,64},{1,33},{33,1},{65,97},{97,65},{2,34}... | collective-permute-start | bytes 1572872 | tf_op jit(solution)/shard_map/ppermute | solution.py:367
  75.6 11.7 %collective-permute-start.3 = (bf16[4,64,256]{2,1,0:T(8,128)(2,1)S(1)}, bf16[4,64,256]{2,1,0:T(8,128)(2,1)S(1)}, u32[]{:S(2)}, u32[]{:S(2)}) collective-permute-start(bf16[4,64,256]{2,1,0:T(8,128)(2,1)S(1)} %get-tuple-element.61), channel_id=1, source_target_pairs={{0,64},{32,96},{64,0},{96,32},{1,65},{33,97},{65,1},{97,33},{2,66}... | collective-permute-start | bytes 393224 | tf_op jit(solution)/shard_map/ppermute | solution.py:367
  79.7 1.3 %collective-permute-start.1 = (f32[64,128]{1,0:T(8,128)S(1)}, f32[64,128]{1,0:T(8,128)S(1)}, u32[]{:S(2)}, u32[]{:S(2)}) collective-permute-start(f32[64,128]{1,0:T(8,128)S(1)} %get-tuple-element.57), channel_id=1, source_target_pairs={{0,32},{32,0},{64,96},{96,64},{1,33},{33,1},{65,97},{97,65},{2,34}... | collective-permute-start | bytes 98312 | tf_op jit(solution)/shard_map/ppermute | solution.py:367
  81.0 5.4 %collective-permute-start.2 = (f32[64,128]{1,0:T(8,128)S(1)}, f32[64,128]{1,0:T(8,128)S(1)}, u32[]{:S(2)}, u32[]{:S(2)}) collective-permute-start(f32[64,128]{1,0:T(8,128)S(1)} %add.6.own), channel_id=1, source_target_pairs={{0,64},{32,96},{64,0},{96,32},{1,65},{33,97},{65,1},{97,33},{2,66}... | collective-permute-start | bytes 98312 | tf_op jit(solution)/shard_map/ppermute | solution.py:367
  87.3 5.7 %copy-start = (bf16[8,256,128]{2,1,0:T(8,128)(2,1)S(1)}, bf16[8,256,128]{2,1,0:T(8,128)(2,1)}, u32[]{:S(2)}) copy-start(bf16[8,256,128]{2,1,0:T(8,128)(2,1)} %query_h.1) | copy-start | bytes 1572868
  87.3 5.7 %copy-start.1 = (bf16[128,64]{0,1:T(8,128)(2,1)S(1)}, bf16[128,64]{0,1:T(8,128)(2,1)}, u32[]{:S(2)}) copy-start(bf16[128,64]{0,1:T(8,128)(2,1)} %param.31) | copy-start | bytes 49156
  87.3 5.7 %copy-start.2 = (f32[128]{0:T(128)S(1)}, f32[128]{0:T(128)}, u32[]{:S(2)}) copy-start(f32[128]{0:T(128)} %param.30) | copy-start | bytes 1540
  87.3 15.1 %all-to-all-start.4 = ((bf16[32,64,128]{2,1,0:T(8,128)(2,1)}), bf16[32,64,128]{2,1,0:T(8,128)(2,1)S(1)}, u32[]{:S(2)}, u32[]{:S(2)}) async-start(bf16[32,64,128]{2,1,0:T(8,128)(2,1)} %shard_map.190), calls=%async_computation.4 | async-start | bytes 1048576 | tf_op jit(solution)/shard_map/all_to_all | solution.py:428
  91.6 1.4 %collective-permute-start.4 = (bf16[4,64,256]{2,1,0:T(8,128)(2,1)S(1)}, bf16[4,64,256]{2,1,0:T(8,128)(2,1)S(1)}, u32[]{:S(2)}, u32[]{:S(2)}) collective-permute-start(bf16[4,64,256]{2,1,0:T(8,128)(2,1)S(1)} %add.7.own), channel_id=1, source_target_pairs={{0,32},{32,0},{64,96},{96,64},{1,33},{33,1},{65,97},{97,65},{2,34}... | collective-permute-start | bytes 393224 | tf_op jit(solution)/shard_map/ppermute | solution.py:367
